TPU v7x, 32 devices: a whole 2x2x4 slice. The times are simulated.
32 devices in a mesh: dp: 8 (over y, x, core), fsdp: 4 (over z).
Axes of the slice: x: 2, y: 2, z: 4, core: 2. Of those that a mesh axis runs over, the one named last changes fastest.
Arguments:
- tokens: bfloat16 [135168, 384], P(('dp', 'fsdp')), may hold values from -6 to 6
- centers: float32 [3, 135168], P(None, ('dp', 'fsdp')), may hold values from -1 to 1
- mask_count: int32 [2048], P(('dp', 'fsdp')), may hold values from 16 to 28, as said below
- mask_index: int32 [2048, 28], P(('dp', 'fsdp')), may hold values from 0 to 63, as said below
- mask_embed: float32 [384], replicated, may hold values from -6 to 6
- place_weight: float32 [3, 128], replicated, may hold values from -3.5 to 3.5
- place_bias: float32 [128], replicated, may hold values from -3 to 3
- place_proj: bfloat16 [128, 384], P('fsdp'), may hold values from -0.5 to 0.5
- place_shift: float32 [384], replicated, may hold values from -2 to 2
- norm_gain: float32 [384], replicated, may hold values from 0.5 to 1.5
- norm_shift: float32 [384], replicated, may hold values from -2 to 2
- joint_weight: bfloat16 [384, 1152], P('fsdp'), may hold values from -0.3125 to 0.3125
- out_weight: bfloat16 [384, 384], P('fsdp'), may hold values from -0.875 to 0.875
- out_bias: float32 [384], replicated, may hold values from -2 to 2
- mlp_gain: float32 [384], replicated, may hold values from 0.5 to 1.5
- mlp_shift: float32 [384], replicated, may hold values from -2 to 2
- up_weight: bfloat16 [384, 1536], P('fsdp'), may hold values from -0.3125 to 0.3125
- up_bias: float32 [1536], replicated, may hold values from -3 to 3
- down_weight: bfloat16 [1536, 384], P('fsdp'), may hold values from -0.15625 to 0.15625
- down_bias: float32 [384], replicated, may hold values from -2 to 2
- cotangent: bfloat16 [135168, 384], P(('dp', 'fsdp')), may hold values from -6 to 6
Outputs:
- output: bfloat16 [135168, 384], P(('dp', 'fsdp'))
- tokens_grad: bfloat16 [135168, 384], P(('dp', 'fsdp'))
- embed_grad: float32 [384], replicated
- place_weight_grad: float32 [3, 128], replicated
- place_bias_grad: float32 [128], replicated
- place_proj_grad: float32 [128, 384], replicated
- place_shift_grad: float32 [384], replicated
- norm_gain_grad: float32 [384], replicated
- norm_shift_grad: float32 [384], replicated
- joint_weight_grad: float32 [384, 1152], replicated
- out_weight_grad: float32 [384, 384], replicated
- out_bias_grad: float32 [384], replicated
- mlp_gain_grad: float32 [384], replicated
- mlp_shift_grad: float32 [384], replicated
- up_weight_grad: float32 [384, 1536], replicated
- up_bias_grad: float32 [1536], replicated
- down_weight_grad: float32 [1536, 384], replicated
- down_bias_grad: float32 [384], replicated
Inputs may be any that keep to these rules, and one draw needn't show every extreme that they name: `mask_count`: number of masked patches of each cloud; some cloud has exactly 28 and some exactly 16. `mask_index`: each row holds 28 different patch numbers.
All inputs are finite; a program needn't handle non-finite values.
Results may differ from a plain program's by a relative error of at most 0.017.
Values may be sent and summed in bfloat16 or wider, within the bound.
No kernel may reach another device: no remote copies, remote signals or barrier semaphores. Data moves between devices by JAX's collectives and lax.ppermute only.
A program may use at most 256 MiB of HBM per device.

v0:
```python
import jax
import jax.numpy as jnp
from jax import lax
from jax.sharding import PartitionSpec as P

HEADS = 6
PATCHES = 64
SEQ = 66
TILE = 8
MASK_MOST = 28


def layer_norm(values, gain_row, shift_row):
    centred = values - jnp.mean(values, axis=-1, keepdims=True)
    spread = jnp.mean(centred * centred, axis=-1, keepdims=True)
    return centred * lax.rsqrt(spread + 1e-05) * gain_row + shift_row


def smooth(values):
    return jax.nn.gelu(values, approximate=False)


def masked_rows(mask_count, mask_index):
    patch_ids = jnp.arange(PATCHES, dtype=jnp.int32)
    slot_ids = jnp.arange(MASK_MOST, dtype=jnp.int32)
    chosen = (mask_index[:, :, None] == patch_ids[None, None, :]) & (
        slot_ids[None, :, None] < mask_count[:, None, None]
    )
    hit_patch = jnp.any(chosen, axis=1)
    border = jnp.zeros((hit_patch.shape[0], 1), dtype=bool)
    return jnp.concatenate([border, hit_patch, border], axis=1).reshape(-1)


def product(left, right):
    return jnp.dot(left, right, preferred_element_type=jnp.float32)


def left_product(left, right):
    return lax.dot_general(
        left, right, (((0,), (0,)), ((), ())), preferred_element_type=jnp.float32
    )


def right_product(left, right):
    return lax.dot_general(
        left, right, (((1,), (1,)), ((), ())), preferred_element_type=jnp.float32
    )


def cloud_scores(joint_tile):
    head_size = joint_tile.shape[-1]
    cloud_rows = joint_tile.shape[1]
    scores = jnp.einsum(
        "cqhd,ckhd->chqk",
        joint_tile[:, :, 0],
        joint_tile[:, :, 1],
        preferred_element_type=jnp.float32,
    ) * head_size ** (-0.5)
    live_key = jnp.arange(cloud_rows, dtype=jnp.int32) != cloud_rows - 1
    return jnp.where(live_key[None, None, None, :], scores, -1e30)


def attend_tile(joint_tile):
    scores = cloud_scores(joint_tile)
    row_top = jnp.max(scores, axis=-1, keepdims=True)
    weights = jnp.exp(scores - row_top)
    totals = jnp.sum(weights, axis=-1, keepdims=True)
    attention = (weights / totals).astype(jnp.bfloat16)
    mixture = jnp.einsum(
        "chqk,ckhd->cqhd", attention, joint_tile[:, :, 2], preferred_element_type=jnp.float32
    ).astype(jnp.bfloat16)
    return (mixture, row_top[..., 0] + jnp.log(totals[..., 0]))


def attend_back(inputs):
    joint_tile, mixture_grad, log_totals = inputs
    head_size = joint_tile.shape[-1]
    attention_full = jnp.exp(cloud_scores(joint_tile) - log_totals[..., None])
    value_grad = jnp.einsum(
        "chqk,cqhd->ckhd",
        attention_full.astype(jnp.bfloat16),
        mixture_grad,
        preferred_element_type=jnp.float32,
    )
    prob_grad = jnp.einsum(
        "cqhd,ckhd->chqk", mixture_grad, joint_tile[:, :, 2], preferred_element_type=jnp.float32
    )
    inner_sum = jnp.sum(prob_grad * attention_full, axis=-1, keepdims=True)
    score_grad = (attention_full * (prob_grad - inner_sum)).astype(jnp.bfloat16)
    query_grad = jnp.einsum(
        "chqk,ckhd->cqhd", score_grad, joint_tile[:, :, 1], preferred_element_type=jnp.float32
    ) * head_size ** (-0.5)
    key_grad = jnp.einsum(
        "chqk,cqhd->ckhd", score_grad, joint_tile[:, :, 0], preferred_element_type=jnp.float32
    ) * head_size ** (-0.5)
    return jnp.stack([query_grad, key_grad, value_grad], axis=2).astype(jnp.bfloat16)


def per_device(
    tokens,
    centers,
    mask_count,
    mask_index,
    mask_embed,
    place_weight,
    place_bias,
    place_proj,
    place_shift,
    norm_gain,
    norm_shift,
    joint_weight,
    out_weight,
    out_bias,
    mlp_gain,
    mlp_shift,
    up_weight,
    up_bias,
    down_weight,
    down_bias,
    cotangent,
):
    whole_place, whole_joint, whole_out, whole_up, whole_down = (
        lax.all_gather(place_proj, "fsdp", axis=0, tiled=True),
        lax.all_gather(joint_weight, "fsdp", axis=0, tiled=True),
        lax.all_gather(out_weight, "fsdp", axis=0, tiled=True),
        lax.all_gather(up_weight, "fsdp", axis=0, tiled=True),
        lax.all_gather(down_weight, "fsdp", axis=0, tiled=True),
    )
    row_count = tokens.shape[0]
    model_width = tokens.shape[1]
    head_size = model_width // HEADS
    tile_rows = TILE * SEQ
    tile_count = row_count // tile_rows
    hidden_rows = masked_rows(mask_count, mask_index)
    place_pre = (
        jnp.einsum("cr,ch->rh", centers, place_weight, precision=lax.Precision.HIGHEST) + place_bias
    )
    place_low = smooth(place_pre).astype(jnp.bfloat16)
    placed = product(place_low, whole_place) + place_shift
    entry_rows = (
        jnp.where(hidden_rows[:, None], mask_embed[None, :], tokens.astype(jnp.float32)) + placed
    )
    normed = layer_norm(entry_rows, norm_gain, norm_shift).astype(jnp.bfloat16)
    joint_rows = product(normed, whole_joint).astype(jnp.bfloat16)
    joint_tiles = joint_rows.reshape(tile_count, TILE, SEQ, 3, HEADS, head_size)
    mixture_tiles, log_totals = lax.map(attend_tile, joint_tiles)
    mixture = mixture_tiles.reshape(row_count, model_width)
    middle = entry_rows + (product(mixture, whole_out) + out_bias)
    normed_two = layer_norm(middle, mlp_gain, mlp_shift).astype(jnp.bfloat16)
    raised = product(normed_two, whole_up) + up_bias
    gated_rows = smooth(raised).astype(jnp.bfloat16)
    output = (middle + (product(gated_rows, whole_down) + down_bias)).astype(jnp.bfloat16)
    back_place, back_joint, back_out, back_up, back_down = (
        lax.all_gather(place_proj, "fsdp", axis=0, tiled=True),
        lax.all_gather(joint_weight, "fsdp", axis=0, tiled=True),
        lax.all_gather(out_weight, "fsdp", axis=0, tiled=True),
        lax.all_gather(up_weight, "fsdp", axis=0, tiled=True),
        lax.all_gather(down_weight, "fsdp", axis=0, tiled=True),
    )
    upstream = cotangent.astype(jnp.float32)
    down_grad = left_product(gated_rows, cotangent)
    down_bias_grad = jnp.sum(upstream, axis=0)
    gated_grad = right_product(cotangent, back_down)
    smooth_back = jax.vjp(smooth, raised)[1]
    raised_grad = smooth_back(gated_grad)[0]
    up_bias_grad = jnp.sum(raised_grad, axis=0)
    raised_low = raised_grad.astype(jnp.bfloat16)
    up_grad = left_product(normed_two, raised_low)
    norm_two_back = jax.vjp(layer_norm, middle, mlp_gain, mlp_shift)[1]
    middle_part, mlp_gain_grad, mlp_shift_grad = norm_two_back(right_product(raised_low, back_up))
    middle_grad = upstream + middle_part
    out_bias_grad = jnp.sum(middle_grad, axis=0)
    middle_low = middle_grad.astype(jnp.bfloat16)
    out_grad = left_product(mixture, middle_low)
    mixture_grad = right_product(middle_low, back_out).astype(jnp.bfloat16)
    joint_grad = lax.map(
        attend_back,
        (joint_tiles, mixture_grad.reshape(tile_count, TILE, SEQ, HEADS, head_size), log_totals),
    ).reshape(row_count, 3 * model_width)
    joint_grad_weight = left_product(normed, joint_grad)
    norm_back = jax.vjp(layer_norm, entry_rows, norm_gain, norm_shift)[1]
    entry_part, norm_gain_grad, norm_shift_grad = norm_back(right_product(joint_grad, back_joint))
    entry_grad = middle_grad + entry_part
    place_shift_grad = jnp.sum(entry_grad, axis=0)
    embed_grad = jnp.sum(jnp.where(hidden_rows[:, None], entry_grad, 0.0), axis=0)
    tokens_grad = jnp.where(hidden_rows[:, None], 0.0, entry_grad).astype(jnp.bfloat16)
    entry_low = entry_grad.astype(jnp.bfloat16)
    place_proj_grad = left_product(place_low, entry_low)
    place_back = jax.vjp(smooth, place_pre)[1]
    place_pre_grad = place_back(right_product(entry_low, back_place))[0]
    place_weight_grad = jnp.einsum(
        "cr,rh->ch", centers, place_pre_grad, precision=lax.Precision.HIGHEST
    )
    place_bias_grad = jnp.sum(place_pre_grad, axis=0)
    owned = (
        lax.psum_scatter(
            place_proj_grad.astype(jnp.bfloat16), "fsdp", scatter_dimension=0, tiled=True
        ).astype(jnp.float32),
        lax.psum_scatter(
            joint_grad_weight.astype(jnp.bfloat16), "fsdp", scatter_dimension=0, tiled=True
        ).astype(jnp.float32),
        lax.psum_scatter(
            out_grad.astype(jnp.bfloat16), "fsdp", scatter_dimension=0, tiled=True
        ).astype(jnp.float32),
        lax.psum_scatter(
            up_grad.astype(jnp.bfloat16), "fsdp", scatter_dimension=0, tiled=True
        ).astype(jnp.float32),
        lax.psum_scatter(
            down_grad.astype(jnp.bfloat16), "fsdp", scatter_dimension=0, tiled=True
        ).astype(jnp.float32),
    )
    owned = lax.psum((owned[0], owned[1], owned[2], owned[3], owned[4]), "dp")
    place_proj_grad, joint_grad_weight, out_grad, up_grad, down_grad = (
        lax.all_gather(owned[0].astype(jnp.bfloat16), "fsdp", axis=0, tiled=True).astype(
            jnp.float32
        ),
        lax.all_gather(owned[1].astype(jnp.bfloat16), "fsdp", axis=0, tiled=True).astype(
            jnp.float32
        ),
        lax.all_gather(owned[2].astype(jnp.bfloat16), "fsdp", axis=0, tiled=True).astype(
            jnp.float32
        ),
        lax.all_gather(owned[3].astype(jnp.bfloat16), "fsdp", axis=0, tiled=True).astype(
            jnp.float32
        ),
        lax.all_gather(owned[4].astype(jnp.bfloat16), "fsdp", axis=0, tiled=True).astype(
            jnp.float32
        ),
    )
    (
        embed_grad,
        place_weight_grad,
        place_bias_grad,
        place_shift_grad,
        norm_gain_grad,
        norm_shift_grad,
        out_bias_grad,
        mlp_gain_grad,
        mlp_shift_grad,
        up_bias_grad,
        down_bias_grad,
    ) = lax.psum(
        (
            embed_grad,
            place_weight_grad,
            place_bias_grad,
            place_shift_grad,
            norm_gain_grad,
            norm_shift_grad,
            out_bias_grad,
            mlp_gain_grad,
            mlp_shift_grad,
            up_bias_grad,
            down_bias_grad,
        ),
        ("dp", "fsdp"),
    )
    return (
        output,
        tokens_grad,
        embed_grad,
        place_weight_grad,
        place_bias_grad,
        place_proj_grad,
        place_shift_grad,
        norm_gain_grad,
        norm_shift_grad,
        joint_grad_weight,
        out_grad,
        out_bias_grad,
        mlp_gain_grad,
        mlp_shift_grad,
        up_grad,
        up_bias_grad,
        down_grad,
        down_bias_grad,
    )


def solution(mesh):
    in_specs = (
        P(("dp", "fsdp"), None),
        P(None, ("dp", "fsdp")),
        P(("dp", "fsdp")),
        P(("dp", "fsdp"), None),
        P(),
        P(),
        P(),
        P("fsdp", None),
        P(),
        P(),
        P(),
        P("fsdp", None),
        P("fsdp", None),
        P(),
        P(),
        P(),
        P("fsdp", None),
        P(),
        P("fsdp", None),
        P(),
        P(("dp", "fsdp"), None),
    )
    out_specs = (
        P(("dp", "fsdp"), None),
        P(("dp", "fsdp"), None),
        P(),
        P(),
        P(),
        P(),
        P(),
        P(),
        P(),
        P(),
        P(),
        P(),
        P(),
        P(),
        P(),
        P(),
        P(),
        P(),
    )
    return jax.shard_map(
        per_device, mesh=mesh, in_specs=in_specs, out_specs=out_specs, check_vma=False
    )
```

profile of v0, /device:TPU:0, one launch (start us, length us, event | category | flops | bytes accessed | tf_op | source)
XLA Modules:
  0.0 830.5 jit_solution(9180563821050712737)
XLA Ops:
  11.1 15.4 %all_gather.35 = bf16[128,384]{1,0:T(8,128)(2,1)S(1)} all-gather(bf16[32,384]{1,0:T(8,128)(2,1)} %param.32), channel_id=1, replica_groups=mesh['dp'=8,'fsdp'=4] {'fsdp'}, dimensions={0}, use_global_device_ids=true | all-gather | bytes 122880 | tf_op jit(solution)/shard_map/all_gather | solution.py:123
  26.5 4.4 copy.83
  31.0 8.8 %multiply_convert_fusion.4 = (bf16[4224,128]{1,0:T(8,128)(2,1)S(1)}, f32[4224,128]{1,0:T(8,128)}) fusion(f32[128]{0:T(128)S(1)} %copy-done.48, f32[3,4224]{1,0:T(4,128)S(1)} %copy-done, f32[3,128]{1,0:T(4,128)S(1)} %copy-done.42), kind=kOutput, calls=%fused_computation.95 | convolution fusion | flops 55148544 | bytes 3296768 | tf_op jit(solution)/shard_map/cr,ch->rh/dot_general | solution.py:136
  43.2 26.8 %all_gather.36 = bf16[384,1152]{1,0:T(8,128)(2,1)S(1)} all-gather(bf16[96,1152]{1,0:T(8,128)(2,1)S(1)} %copy-done.21), channel_id=1, replica_groups=mesh['dp'=8,'fsdp'=4] {'fsdp'}, dimensions={0}, use_global_device_ids=true | all-gather | bytes 1105920 | tf_op jit(solution)/shard_map/all_gather | solution.py:124
  70.9 8.2 convolution_convert_fusion.2
  79.1 29.2 %reshape.227 = bf16[8,8,66,3,6,64]{5,4,3,2,1,0:T(8,128)(2,1)} reshape(bf16[4224,1152]{1,0:T(8,128)(2,1)} %convolution_convert_fusion.2) | data formatting | bytes 19464192 | tf_op jit(solution)/shard_map/reshape | solution.py:145
  108.3 30.2 %copy.85 = bf16[8,8,66,3,6,64]{2,5,4,1,3,0:T(8,128)(2,1)} copy(bf16[8,8,66,3,6,64]{5,4,3,2,1,0:T(8,128)(2,1)} %reshape.227) | data formatting | bytes 19464192 | tf_op jit(solution)/shard_map/while | solution.py:146
  138.5 50.9 %while.22 = (s32[]{:T(128)}, bf16[8,8,66,6,64]{2,1,0,4,3:T(8,128)(2,1)}, f32[8,8,6,66]{3,2,1,0:T(8,128)}, bf16[8,8,66,3,6,64]{2,5,4,1,3,0:T(8,128)(2,1)}, s32[]{:T(128)}) while((s32[]{:T(128)}, bf16[8,8,66,6,64]{2,1,0,4,3:T(8,128)(2,1)}, f32[8,8,6,66]{3,2,1,0:T(8,128)}, bf16[8,8,66,3,6,64]{2,5,4,1,3,0:T(8,128)(2,1)}, s32[]{:T(128)}) %tuple.71), condition=%wide.region_6.7_spmd, body=%wide.region_3.6_spmd.sunk | while | flops 56235236 | bytes 9995845 | solution.py:146
  138.5 2.1 dynamic-slice_bitcast_fusion.6
  144.9 2.1 dynamic-slice_bitcast_fusion.6
  151.2 2.1 dynamic-slice_bitcast_fusion.6
  157.6 2.1 dynamic-slice_bitcast_fusion.6
  164.0 2.1 dynamic-slice_bitcast_fusion.6
  170.3 2.1 dynamic-slice_bitcast_fusion.6
  176.7 2.1 dynamic-slice_bitcast_fusion.6
  189.4 9.8 %reshape.223 = bf16[4224,384]{0,1:T(8,128)(2,1)S(1)} reshape(bf16[8,8,66,6,64]{2,1,0,4,3:T(8,128)(2,1)} %get-tuple-element.68) | data formatting | bytes 6488064 | tf_op jit(solution)/shard_map/reshape | solution.py:147
  199.2 14.0 %all_gather.37 = bf16[384,384]{1,0:T(8,128)(2,1)S(1)} all-gather(bf16[96,384]{1,0:T(8,128)(2,1)S(1)} %copy-done.30), channel_id=1, replica_groups=mesh['dp'=8,'fsdp'=4] {'fsdp'}, dimensions={0}, use_global_device_ids=true | all-gather | bytes 368640 | tf_op jit(solution)/shard_map/all_gather | solution.py:125
  213.2 5.1 fusion.62
  219.0 2.6 copy-done.2
  222.6 5.5 copy.89
  228.1 67.8 %multiply_convert_fusion.3 = (bf16[4224,1536]{1,0:T(8,128)(2,1)}, f32[4224,1536]{1,0:T(8,128)}, f32[4224,1536]{1,0:T(8,128)}) fusion(f32[1536]{0:T(1024)S(1)} %copy-done.41, bf16[384,1536]{1,0:T(8,128)(2,1)} %all-gather.5.cloned.1.call-done, f32[4224,384]{0,1:T(8,128)} %copy-done.2, f32[384]{0:T(512)S(1)} %copy-done.45, f32[384]{0:T(512)S(1)} %copy-done.35, ...), kind=kOutput, calls=%fused_computation.46 | convolution fusion | flops 5419155456 | bytes 72591360 | tf_op jit(solution)/shard_map/dot_general | solution.py:35
  296.0 25.8 %fusion.66 = (f32[1536]{0:T(1024)}, bf16[4224,1536]{1,0:T(8,128)(2,1)}) fusion(f32[4224,1536]{1,0:T(8,128)} %get-tuple-element.197, bf16[4224,384]{1,0:T(8,128)(2,1)S(1)} %copy-done.13, bf16[1536,384]{1,0:T(8,128)(2,1)} %all-gather.7.cloned.1.call-done, f32[4224,1536]{1,0:T(8,128)} %get-tuple-element.211, f32[1536]{0:T(1024)S(1)} %copy-done.41), kind=kOutput, calls=%fused_computation.142 | convolution fusion | flops 5086640640 | bytes 69316608 | tf_op jit(solution)/shard_map/dot_general | solution.py:45
  321.7 12.5 %fusion.65 = (f32[384]{0:T(512)}, f32[4224,384]{1,0:T(8,128)}) fusion(bf16[384,1536]{1,0:T(8,128)(2,1)} %all-gather.5.cloned.1.call-done, bf16[4224,1536]{1,0:T(8,128)(2,1)} %get-tuple-element.219), kind=kOutput, calls=%fused_computation.141 | convolution fusion | flops 4984454656 | bytes 20645376 | tf_op jit(solution)/shard_map/dot_general | solution.py:45
  334.3 8.1 copy.90
  342.3 7.8 multiply_reduce_fusion.1
  353.0 2.5 copy-done.4
  357.2 2.6 convolution_convert_fusion.6
  359.8 4.1 convolution_convert_fusion.3
  364.0 8.5 %reshape.226 = bf16[8,8,66,6,64]{4,3,2,1,0:T(8,128)(2,1)} reshape(bf16[4224,384]{1,0:T(8,128)(2,1)S(1)} %convolution_convert_fusion.3) | data formatting | bytes 6488064 | tf_op jit(solution)/shard_map/reshape | solution.py:178
  372.5 11.7 %copy.93 = bf16[8,8,66,6,64]{2,4,3,1,0:T(8,128)(2,1)} copy(bf16[8,8,66,6,64]{4,3,2,1,0:T(8,128)(2,1)} %reshape.226) | data formatting | bytes 6488064 | tf_op jit(solution)/shard_map/while | solution.py:176
  384.2 103.4 %while.23 = (s32[]{:T(128)}, bf16[8,8,66,3,6,64]{2,1,0,5,4,3:T(8,128)(2,1)}, bf16[8,8,66,3,6,64]{2,5,4,1,3,0:T(8,128)(2,1)}, f32[8,8,6,66]{3,2,1,0:T(8,128)}, bf16[8,8,66,6,64]{2,4,3,1,0:T(8,128)(2,1)}, /*index=5*/s32[]{:T(128)}) while((s32[]{:T(128)}, bf16[8,8,66,3,6,64]{2,1,0,5,4,3:T(8,128)(2,1)}, ...), condition=%wide.region_13.14_spmd, body=%wide.region_11.13_spmd.sunk | while | flops 137925280 | bytes 23387920 | solution.py:176
  384.2 2.2 dynamic-slice_bitcast_fusion.8
  393.4 3.6 copy_dynamic-update-slice_fusion.5
  406.2 3.7 copy_dynamic-update-slice_fusion.5
  419.2 3.8 copy_dynamic-update-slice_fusion.5
  432.2 3.7 copy_dynamic-update-slice_fusion.5
  445.1 3.8 copy_dynamic-update-slice_fusion.5
  458.1 3.7 copy_dynamic-update-slice_fusion.5
  471.0 3.6 copy_dynamic-update-slice_fusion.5
  483.9 3.7 copy_dynamic-update-slice_fusion.5
  487.6 29.9 %reshape.225 = bf16[4224,1152]{0,1:T(8,128)(2,1)} reshape(bf16[8,8,66,3,6,64]{2,1,0,5,4,3:T(8,128)(2,1)} %get-tuple-element.70) | data formatting | bytes 19464192 | tf_op jit(solution)/shard_map/reshape | solution.py:179
  517.6 11.2 %convolution_convert_fusion.5 = bf16[384,1152]{1,0:T(8,128)(2,1)} fusion(bf16[4224,1152]{0,1:T(8,128)(2,1)} %reshape.225, f32[4224,384]{0,1:T(8,128)} %copy-done.1, f32[384]{0:T(512)S(1)} %copy-done.44, f32[384]{0:T(512)S(1)} %copy-done.33, f32[4224]{0:T(1024)S(1)} %copy-done.23, f32[4224]{0:T(1024)S(1)} %copy-done.18), kind=kOutput, calls=%fused_computation.92 | convolution fusion | flops 3745677312 | bytes 17141760 | tf_op jit(solution)/shard_map/dot_general | solution.py:39
  528.9 12.5 %fusion.32 = bf16[384,1536]{1,0:T(8,128)(2,1)} fusion(bf16[4224,1536]{1,0:T(8,128)(2,1)} %get-tuple-element.219, f32[4224,384]{0,1:T(8,128)} %copy-done.2, f32[384]{0:T(512)S(1)} %copy-done.46, f32[384]{0:T(512)S(1)} %copy-done.35, f32[4224]{0:T(1024)S(1)} %fusion.55, f32[4224]{0:T(1024)S(1)} %broadcast_multiply_fusion), kind=kOutput, calls=%fused_computation.90 | convolution fusion | flops 4991533056 | bytes 20680704 | tf_op jit(solution)/shard_map/dot_general | solution.py:39
  541.5 11.0 %convolution_convert_fusion.4 = bf16[1536,384]{1,0:T(8,128)(2,1)} fusion(bf16[4224,1536]{1,0:T(8,128)(2,1)} %get-tuple-element.196, bf16[4224,384]{1,0:T(8,128)(2,1)S(1)} %copy-done.14), kind=kOutput, calls=%fused_computation.91 | convolution fusion | flops 4983422976 | bytes 17399808 | tf_op jit(solution)/shard_map/dot_general | solution.py:39
  552.5 10.5 %fusion.64 = (f32[384]{0:T(512)S(1)}, f32[4224,384]{1,0:T(8,128)}) fusion(bf16[4224,1152]{0,1:T(8,128)(2,1)} %reshape.225, bf16[384,1152]{1,0:T(8,128)(2,1)} %copy-done.16), kind=kOutput, calls=%fused_computation.140 | convolution fusion | flops 3738746368 | bytes 17106432 | tf_op jit(solution)/shard_map/dot_general | solution.py:45
  563.1 8.0 copy.95
  571.1 6.0 multiply_reduce_fusion.3
  579.1 3.1 multiply_reduce_fusion.2
  582.2 3.2 reduce-scatter.12.cloned.1.call-done
  585.4 30.7 %reduce-scatter.14.cloned.1.call-done = bf16[384,384]{1,0:T(8,128)(2,1)} async-done(((bf16[1536,384]{1,0:T(8,128)(2,1)}), bf16[384,384]{1,0:T(8,128)(2,1)}) %reduce-scatter.14.cloned.1.call-update) | async-done | bytes 294928 | tf_op jit(solution)/shard_map/reduce_scatter | solution.py:208
  616.1 10.6 %convert_reduce_fusion = (f32[384]{0:T(512)S(1)}, f32[384]{0:T(512)S(1)}, f32[384]{0:T(512)S(1)}, f32[384]{0:T(512)S(1)}, bf16[4224,384]{0,1:T(8,128)(2,1)S(1)}) fusion(bf16[4224,384]{0,1:T(8,128)(2,1)} %copy.89, f32[4224,384]{0,1:T(8,128)} %copy-done.4, f32[4224]{0:T(1024)S(1)} %negate_multiply_fusion.3, pred[4224]{0:T(1024)(128)(4,1)S(1)} %copy-done.29, ...), kind=kLoop, calls=%fused_computation.63 | loop fusion | flops 27572736 | bytes 26048640 | tf_op jit(solution)/shard_map/reduce_sum | solution.py:162
  628.6 2.2 select_convert_fusion
  630.9 5.6 copy.99
  636.5 38.1 %all-reduce.4.cloned.1.call-done = (bf16[96,1152]{1,0:T(8,128)(2,1)}, bf16[96,384]{1,0:T(8,128)(2,1)}, bf16[96,1536]{1,0:T(8,128)(2,1)}, bf16[384,384]{1,0:T(8,128)(2,1)}) async-done(((bf16[96,1152]{1,0:T(8,128)(2,1)}, bf16[96,384]{1,0:T(8,128)(2,1)}, bf16[96,1536]{1,0:T(8,128)(2,1)}, bf16[384,384]{1,0:T(8,128)(2,1)}), (bf16[96,1152]{1,0:T(8,128)(2,1)}, bf16[96,384]{1,0:T(8,128)(2,1)}, ...) | async-done | bytes 884752 | tf_op jit(solution)/shard_map/psum | solution.py:212
  674.7 14.1 %fusion.27 = bf16[4224,384]{0,1:T(8,128)(2,1)} fusion(f32[4224,384]{0,1:T(8,128)} %copy-done.2, bf16[4224,1536]{1,0:T(8,128)(2,1)} %get-tuple-element.196, bf16[1536,384]{1,0:T(8,128)(2,1)} %all-gather.7.cloned.1.call-done, f32[384]{0:T(512)S(1)} %copy-done.47), kind=kOutput, calls=%fused_computation.72 | convolution fusion | flops 4987699200 | bytes 23889408 | tf_op jit(solution)/shard_map/dot_general | solution.py:35
  688.8 5.9 copy.98
  694.7 7.0 fusion.63
  703.1 41.2 %all-reduce = (f32[384]{0:T(512)}, f32[3,128]{1,0:T(4,128)}, f32[128]{0:T(128)}, f32[384]{0:T(512)}, f32[384]{0:T(512)}, /*index=5*/f32[384]{0:T(512)}, f32[384]...) all-reduce(f32[384]{0:T(512)S(1)} %get-tuple-element.202, ...), channel_id=1, replica_groups=mesh['dp'=8,'fsdp'=4] {'dp','fsdp'}, use_global_device_ids=true, to_apply=%region_17.18 | all-reduce | flops 5120 | bytes 40960 | tf_op jit(solution)/shard_map/psum | solution.py:242
  744.2 25.1 %psum.115 = bf16[32,384]{1,0:T(8,128)(2,1)S(1)} all-reduce(bf16[32,384]{1,0:T(8,128)(2,1)} %reduce-scatter.6.cloned.1.call-done), channel_id=1, replica_groups=mesh['dp'=8,'fsdp'=4] {'dp'}, use_global_device_ids=true, to_apply=%region_22.23 | all-reduce | flops 12288 | bytes 49152 | tf_op jit(solution)/shard_map/psum | solution.py:212
  769.3 13.3 %all_gather.40 = bf16[128,384]{1,0:T(8,128)(2,1)S(1)} all-gather(bf16[32,384]{1,0:T(8,128)(2,1)S(1)} %psum.115), channel_id=1, replica_groups=mesh['dp'=8,'fsdp'=4] {'fsdp'}, dimensions={0}, use_global_device_ids=true | all-gather | bytes 122880 | tf_op jit(solution)/shard_map/all_gather | solution.py:214
  783.3 18.2 %all_gather.41 = bf16[384,1152]{1,0:T(8,128)(2,1)S(1)} all-gather(bf16[96,1152]{1,0:T(8,128)(2,1)} %get-tuple-element.189), channel_id=1, replica_groups=mesh['dp'=8,'fsdp'=4] {'fsdp'}, dimensions={0}, use_global_device_ids=true | all-gather | bytes 1105920 | tf_op jit(solution)/shard_map/all_gather | solution.py:217
  802.8 13.9 %all_gather.42 = bf16[384,384]{1,0:T(8,128)(2,1)S(1)} all-gather(bf16[96,384]{1,0:T(8,128)(2,1)S(1)} %copy-done.31), channel_id=1, replica_groups=mesh['dp'=8,'fsdp'=4] {'fsdp'}, dimensions={0}, use_global_device_ids=true | all-gather | bytes 368640 | tf_op jit(solution)/shard_map/all_gather | solution.py:220
  817.6 3.0 convert_element_type.150
  820.5 2.8 convert_element_type.154
  (287 shorter events, 129.7 us)
Async XLA Ops:
  7.2 23.7 %copy-start = (f32[3,4224]{1,0:T(4,128)S(1)}, f32[3,4224]{1,0:T(4,128)}, u32[]{:S(2)}) copy-start(f32[3,4224]{1,0:T(4,128)} %param.26) | copy-start | bytes 152068
  7.2 220.9 %all-gather.5.cloned.1.call-start = ((), (), s32[]{:S(2)}) async-start(), calls=%async_computation.5 | async-start | bytes 1474560 | tf_op jit(solution)/shard_map/all_gather | solution.py:126
  7.9 288.0 %all-gather.7.cloned.1.call-start = ((), (), s32[]{:S(2)}) async-start(), calls=%async_computation.6 | async-start | bytes 1474560 | tf_op jit(solution)/shard_map/all_gather | solution.py:127
  8.7 573.5 %reduce-scatter.10.cloned.1.call-start = ((), (), s32[]{:S(2)}) async-start(), calls=%async_computation.9 | async-start | bytes 368640 | tf_op jit(solution)/shard_map/reduce_scatter | solution.py:202
  11.1 28.7 %copy-start.28 = (pred[4224]{0:T(1024)(128)(4,1)}, pred[4224]{0:T(1024)(128)(4,1)S(1)}, u32[]{:S(2)}) copy-start(pred[4224]{0:T(1024)(128)(4,1)S(1)} %broadcast_in_dim.119) | copy-start | bytes 12676
  26.5 13.3 %copy-start.19 = (bf16[128,384]{1,0:T(8,128)(2,1)}, bf16[128,384]{1,0:T(8,128)(2,1)S(1)}, u32[]{:S(2)}) copy-start(bf16[128,384]{1,0:T(8,128)(2,1)S(1)} %all_gather.35) | copy-start | bytes 294916
  26.5 4.4 copy-start.42
  26.5 4.4 copy-start.48
  31.0 8.9 %copy-start.38 = (f32[384]{0:T(512)S(1)}, f32[384]{0:T(512)}, u32[]{:S(2)}) copy-start(f32[384]{0:T(512)} %param.33) | copy-start | bytes 4612
  31.0 8.9 %copy-start.39 = (f32[384]{0:T(512)S(1)}, f32[384]{0:T(512)}, u32[]{:S(2)}) copy-start(f32[384]{0:T(512)} %param.29) | copy-start | bytes 4612
  39.8 1.5 copy-start.10
  41.4 28.6 %copy-start.1 = (f32[4224,384]{0,1:T(8,128)}, f32[4224,384]{0,1:T(8,128)S(1)}, u32[]{:S(2)}) copy-start(f32[4224,384]{0,1:T(8,128)S(1)} %get-tuple-element.208) | copy-start | bytes 19464196
  41.4 28.6 %copy-start.17 = (f32[4224]{0:T(1024)}, f32[4224]{0:T(1024)S(1)}, u32[]{:S(2)}) copy-start(f32[4224]{0:T(1024)S(1)} %broadcast_multiply_fusion.1) | copy-start | bytes 50692
  41.4 1.8 copy-start.21
  41.4 29.5 %copy-start.32 = (f32[384]{0:T(512)S(1)}, f32[384]{0:T(512)}, u32[]{:S(2)}) copy-start(f32[384]{0:T(512)} %param.34) | copy-start | bytes 4612
  41.4 29.5 %copy-start.43 = (f32[384]{0:T(512)S(1)}, f32[384]{0:T(512)}, u32[]{:S(2)}) copy-start(f32[384]{0:T(512)} %param.35) | copy-start | bytes 4612
  42.1 1.1 copy-start.24
  43.2 26.8 %copy-start.22 = (f32[4224]{0:T(1024)}, f32[4224]{0:T(1024)S(1)}, u32[]{:S(2)}) copy-start(f32[4224]{0:T(1024)S(1)} %fusion.54) | copy-start | bytes 50692
  70.0 1.0 copy-start.16
  189.4 9.8 %copy-start.30 = (bf16[96,384]{1,0:T(8,128)(2,1)S(1)}, bf16[96,384]{1,0:T(8,128)(2,1)}, u32[]{:S(2)}) copy-start(bf16[96,384]{1,0:T(8,128)(2,1)} %param.37) | copy-start | bytes 221188
  189.4 23.8 %copy-start.34 = (f32[384]{0:T(512)S(1)}, f32[384]{0:T(512)}, u32[]{:S(2)}) copy-start(f32[384]{0:T(512)} %param.38) | copy-start | bytes 4612
  199.2 19.1 %copy-start.7 = (bf16[4224,384]{0,1:T(8,128)(2,1)}, bf16[4224,384]{0,1:T(8,128)(2,1)S(1)}, u32[]{:S(2)}) copy-start(bf16[4224,384]{0,1:T(8,128)(2,1)S(1)} %reshape.223) | copy-start | bytes 9732100
  213.2 5.1 copy-start.15
  218.3 3.3 copy-start.2
  218.3 4.3 copy-start.12
  221.6 6.5 copy-start.26
  222.6 5.5 copy-start.35
  222.6 5.5 copy-start.41
  222.6 5.5 copy-start.45
  228.1 67.8 %copy-start.13 = (bf16[4224,384]{1,0:T(8,128)(2,1)S(1)}, bf16[4224,384]{1,0:T(8,128)(2,1)}, u32[]{:S(2)}) copy-start(bf16[4224,384]{1,0:T(8,128)(2,1)} %param.45) | copy-start | bytes 9732100
  334.3 15.9 %slice-start.2 = ((s8[6488064]{0:T(1024)(128)(4,1)}), s8[2293760]{0:T(1024)(128)(4,1)S(1)}, s32[]{:S(2)}) async-start(s8[6488064]{0:T(1024)(128)(4,1)} %bitcast.142), calls=%async_computation.17 | async-start | bytes 4587520
  342.3 7.9 copy-start.27
  342.3 7.9 slice-start.3
  342.3 7.9 copy-start.5
  350.2 2.0 copy-start.6
  352.2 3.3 copy-start.4
  352.3 5.0 copy-start.8
  355.5 1.7 copy-start.9
  364.0 218.2 %reduce-scatter.8.cloned.1.call-start = ((), (), s32[]{:S(2)}) async-start(), calls=%async_computation.8 | async-start | bytes 1105920 | tf_op jit(solution)/shard_map/reduce_scatter | solution.py:199
  487.6 30.0 %copy-start.18 = (f32[4224]{0:T(1024)S(1)}, f32[4224]{0:T(1024)}, u32[]{:S(2)}) copy-start(f32[4224]{0:T(1024)} %copy-done.17) | copy-start | bytes 50692
  487.6 30.0 %copy-start.23 = (f32[4224]{0:T(1024)S(1)}, f32[4224]{0:T(1024)}, u32[]{:S(2)}) copy-start(f32[4224]{0:T(1024)} %copy-done.22) | copy-start | bytes 50692
  487.6 30.0 %copy-start.33 = (f32[384]{0:T(512)S(1)}, f32[384]{0:T(512)}, u32[]{:S(2)}) copy-start(f32[384]{0:T(512)} %param.34) | copy-start | bytes 4612
  487.6 30.0 %copy-start.44 = (f32[384]{0:T(512)S(1)}, f32[384]{0:T(512)}, u32[]{:S(2)}) copy-start(f32[384]{0:T(512)} %param.35) | copy-start | bytes 4612
  517.6 11.3 %copy-start.46 = (f32[384]{0:T(512)S(1)}, f32[384]{0:T(512)}, u32[]{:S(2)}) copy-start(f32[384]{0:T(512)} %param.40) | copy-start | bytes 4612
  528.8 12.7 %copy-start.14 = (bf16[4224,384]{1,0:T(8,128)(2,1)S(1)}, bf16[4224,384]{1,0:T(8,128)(2,1)}, u32[]{:S(2)}) copy-start(bf16[4224,384]{1,0:T(8,128)(2,1)} %param.45) | copy-start | bytes 9732100
  528.8 56.5 %reduce-scatter.12.cloned.1.call-start = ((), (), s32[]{:S(2)}) async-start(), calls=%async_computation.10 | async-start | bytes 1474560 | tf_op jit(solution)/shard_map/reduce_scatter | solution.py:205
  541.4 74.6 %reduce-scatter.14.cloned.1.call-start = ((), (), s32[]{:S(2)}) async-start(), calls=%async_computation.12 | async-start | bytes 1474560 | tf_op jit(solution)/shard_map/reduce_scatter | solution.py:208
  552.5 122.2 %all-reduce.4.cloned.1.call-start = ((), (), s32[]{:S(2)}) async-start(), calls=%async_computation.14 | async-start | bytes 1769472 | tf_op jit(solution)/shard_map/psum | solution.py:212
  563.1 14.1 %slice-start = ((s8[6488064]{0:T(1024)(128)(4,1)}), s8[2293760]{0:T(1024)(128)(4,1)S(1)}, s32[]{:S(2)}) async-start(s8[6488064]{0:T(1024)(128)(4,1)} %bitcast.140), calls=%async_computation.15 | async-start | bytes 4587520
  571.1 6.0 copy-start.25
  571.1 6.1 slice-start.1
  571.1 7.9 copy-start.3
  579.1 37.1 %copy-start.29 = (pred[4224]{0:T(1024)(128)(4,1)S(1)}, pred[4224]{0:T(1024)(128)(4,1)}, u32[]{:S(2)}) copy-start(pred[4224]{0:T(1024)(128)(4,1)} %copy-done.28) | copy-start | bytes 12676
  616.1 128.2 %reduce-scatter.6.cloned.1.call-start = ((), (), s32[]{:S(2)}) async-start(), calls=%async_computation.7 | async-start | bytes 122880 | tf_op jit(solution)/shard_map/reduce_scatter | solution.py:196
  616.1 10.7 %copy-start.11 = (bf16[4224,128]{1,0:T(8,128)(2,1)S(1)}, bf16[4224,128]{1,0:T(8,128)(2,1)}, u32[]{:S(2)}) copy-start(bf16[4224,128]{1,0:T(8,128)(2,1)} %copy-done.10) | copy-start | bytes 3244036
  628.6 189.0 %all-gather.9.cloned.1.call-start = ((), (), s32[]{:S(2)}) async-start(), calls=%async_computation.11 | async-start | bytes 1474560 | tf_op jit(solution)/shard_map/all_gather | solution.py:223
  630.9 43.8 %copy-start.47 = (f32[384]{0:T(512)S(1)}, f32[384]{0:T(512)}, u32[]{:S(2)}) copy-start(f32[384]{0:T(512)} %param.44) | copy-start | bytes 4612
  674.7 145.9 %all-gather.11.cloned.1.call-start = ((), (), s32[]{:S(2)}) async-start(), calls=%async_computation.13 | async-start | bytes 1474560 | tf_op jit(solution)/shard_map/all_gather | solution.py:226
  688.8 5.9 copy-start.20
  694.7 8.3 %copy-start.36 = (f32[384]{0:T(512)S(1)}, f32[384]{0:T(512)}, u32[]{:S(2)}) copy-start(f32[384]{0:T(512)} %get-tuple-element.154) | copy-start | bytes 4612
  694.7 8.3 %copy-start.37 = (f32[1536]{0:T(1024)S(1)}, f32[1536]{0:T(1024)}, u32[]{:S(2)}) copy-start(f32[1536]{0:T(1024)} %get-tuple-element.218) | copy-start | bytes 18436
  694.7 8.3 %copy-start.40 = (f32[384]{0:T(512)S(1)}, f32[384]{0:T(512)}, u32[]{:S(2)}) copy-start(f32[384]{0:T(512)} %get-tuple-element.216) | copy-start | bytes 4612
  701.8 101.0 %copy-start.31 = (bf16[96,384]{1,0:T(8,128)(2,1)S(1)}, bf16[96,384]{1,0:T(8,128)(2,1)}, u32[]{:S(2)}) copy-start(bf16[96,384]{1,0:T(8,128)(2,1)} %get-tuple-element.190) | copy-start | bytes 221188
Sparse Core Ops, SparseCore 0:
  9.6 33.8 all-gather.4
  45.1 34.0 all-gather.6
  364.1 20.7 reduce-scatter.9
  529.0 25.3 reduce-scatter.7
  557.1 28.2 reduce-scatter.11
  588.1 27.8 reduce-scatter.13
  619.6 54.9 all-reduce.3
  677.5 18.4 reduce-scatter.5
  697.6 29.0 all-gather.8
  728.2 29.8 all-gather.10
where the time goes:
time: 840 us; the launch traced here: 830 us
  matrix products  261 us (31%)
  local copies, waits for them, and re-layouts  251 us (30%)
  blocking collectives  168 us (20%)
  waiting for transfers between devices  73.5 us (9%)
  other arithmetic  61.3 us (7%)
  between operations  15.1 us (2%)
    dot_general x5, matrix products, product(): return jnp.dot(left, right, preferred_element_type=jnp.float32)  96.7 us
    dot_general x5, matrix products, right_product(): lax.dot_general(left, right, (((1,), (1,)), ((), ())), preferred_element_...  60 us
    psum x1, blocking collectives, per_device(): lax.psum((embed_grad, place_weight_grad, place_bias_grad, place_shift_gra...  41.2 us
    dot_general x5, matrix products, left_product(): lax.dot_general(left, right, (((0,), (0,)), ((), ())), preferred_element_...  39 us
    psum x1, waiting for transfers between devices, per_device(): owned = lax.psum((owned[0], owned[1], owned[2], owned[3], owned[4]), 'dp')  38.1 us
    squeeze x16, local copies, waits for them, and re-layouts, per_device(): mixture_tiles, log_totals = lax.map(attend_tile, joint_tiles)  34.4 us
    unnamed x110, local copies, waits for them, and re-layouts  33.3 us
    reduce_scatter x1, waiting for transfers between devices, per_device(): lax.psum_scatter(down_grad.astype(jnp.bfloat16), 'fsdp', scatter_dimensio...  30.7 us
  transfers between devices with their start and end apart: 10, of which 3 were waited for; matrix products, arithmetic and copies ran while one was open for 60% of the time, Pallas kernels for 0%

commit v1 on v0

v1 whole, which is shorter than its diff:
```python
import functools

import jax
import jax.numpy as jnp
from jax import lax
from jax.experimental import pallas as pl
from jax.experimental.pallas import tpu as pltpu
from jax.sharding import PartitionSpec as P

D = 384
HEADS = 6
FF = 1536
POSH = 128
SEQ = 66
TILE = 8
ROWS = TILE * SEQ
STEP = 64
WIN = 80
KEYS = 128
PAIRS = HEADS // 2
GROUP = 12
VMEM = 60 * 2**20
LOG2E = 1.4426950408889634
ROOT_HALF = 0.7071067811865476
PDF = 0.3989422804014327
bf16 = jnp.bfloat16
f32 = jnp.float32

NN = (((1,), (0,)), ((), ()))
NT = (((1,), (1,)), ((), ()))
TN = (((0,), (0,)), ((), ()))


def dot(left, right, dims=NN):
    return lax.dot_general(left, right, dims, preferred_element_type=f32)


def cdf(u):
    return 0.5 + 0.5 * lax.erf(u * ROOT_HALF)


def smooth_slope(u, mass):
    return mass + u * (PDF * jnp.exp2(u * u * (-0.5 * LOG2E)))


def row_mean(values):
    return jnp.sum(values, axis=-1, keepdims=True) * (1.0 / values.shape[-1])


def normalised(values):
    centred = values - row_mean(values)
    scale = lax.rsqrt(row_mean(centred * centred) + 1e-05)
    return centred * scale, scale


def hidden_column(targets, rows):
    row_ids = lax.broadcasted_iota(jnp.int32, (rows, targets.shape[1]), 0)
    hits = jnp.where(row_ids == targets, 1.0, 0.0)
    return jnp.max(hits, axis=1, keepdims=True)


def lane_mask(rows, odd, kind=bf16):
    lanes = lax.broadcasted_iota(jnp.int32, (rows, 128), 1)
    return (lanes >= 64) if odd else (lanes < 64)


def stacked_heads(tile):
    zero = jnp.zeros_like(tile)
    even = lane_mask(tile.shape[0], False)
    return jnp.concatenate([jnp.where(even, tile, zero), jnp.where(even, zero, tile)], axis=0)


def merged_heads(pair):
    half = pair.shape[0] // 2
    even = lane_mask(half, False)
    return jnp.where(even, pair[:half], pair[half:])


def row_range(rows, low, high, width=128):
    ids = lax.broadcasted_iota(jnp.int32, (rows, width), 0)
    return (ids >= low) & (ids < high)


def spread_heads(flipped):
    none = jnp.zeros((64, flipped.shape[1]), flipped.dtype)
    left = jnp.concatenate([flipped[:64], none], axis=0)
    right = jnp.concatenate([none, flipped[64:]], axis=0)
    return jnp.concatenate([left, right], axis=1)


def head_ones(value):
    rows = lax.broadcasted_iota(jnp.int32, (2 * KEYS, 128), 0) < KEYS
    lanes = lax.broadcasted_iota(jnp.int32, (2 * KEYS, 128), 1) < 64
    return jnp.where(rows == lanes, value, 0.0).astype(bf16)


def lane_ones(value):
    rows = lax.broadcasted_iota(jnp.int32, (128, 2 * KEYS), 0) < 64
    lanes = lax.broadcasted_iota(jnp.int32, (128, 2 * KEYS), 1) < KEYS
    return jnp.where(rows == lanes, value, 0.0).astype(bf16)


def pack_kernel(spot, proj, joint, out, up, down, half_early, half_late, early, late):
    rows = joint.shape[0]
    for part in range(3):
        early[part * rows : part * rows + rows, :] = joint[:, part * D : part * D + D]
    early[3 * rows :, :] = proj[...]
    late[:rows, :] = out[...]
    for part in range(4):
        late[(part + 1) * rows : (part + 2) * rows, :] = up[:, part * D : part * D + D]
    late[5 * rows : 5 * rows + down.shape[0], :] = down[...]
    for source, target in ((early, half_early), (late, half_late)):
        half = target.shape[0]
        target[...] = source[pl.ds(pl.multiple_of(spot[0] * half, 16), half), :]


def pack(core, proj, joint, out, up, down):
    rows, low, deep = joint.shape[0], proj.shape[0], down.shape[0]
    sizes = (3 * rows + low, 5 * rows + deep)
    vmem = pl.BlockSpec(memory_space=pltpu.VMEM)
    return pl.pallas_call(
        pack_kernel,
        in_specs=[pl.BlockSpec(memory_space=pltpu.SMEM)] + [vmem] * 5,
        out_specs=[vmem, vmem],
        out_shape=[shape_of((size // 2, D), bf16) for size in sizes],
        scratch_shapes=[pltpu.VMEM((size, D), bf16) for size in sizes],
        compiler_params=settings(),
        name="pack",
    )(core, proj, joint, out, up, down)


def unpack_early(core, mine, other, joint_w, proj):
    groups, half, _ = mine.shape
    rows, low = D // groups, POSH // groups

    def place(side, source):
        for group in range(groups):
            at = 0
            while at < half:
                row = side * half + at
                if row < 3 * rows:
                    part, inner = divmod(row, rows)
                    size = min(half - at, rows - inner)
                    first = group * rows + inner
                    joint_w[first : first + size, part * D : part * D + D] = source[group, at : at + size]
                else:
                    size = half - at
                    first = group * low + row - 3 * rows
                    proj[first : first + size, :] = source[group, at : at + size]
                at += size

    @pl.when(core == 0)
    def _():
        place(0, mine)
        place(1, other)

    @pl.when(core == 1)
    def _():
        place(0, other)
        place(1, mine)


def unpack_late(core, mine, other, out_w, up_w, down_w):
    groups, half, _ = mine.shape
    rows, deep = D // groups, FF // groups

    def place(side, source):
        for group in range(groups):
            at = 0
            while at < half:
                row = side * half + at
                if row < rows:
                    size = min(half - at, rows - row)
                    first = group * rows + row
                    out_w[first : first + size, :] = source[group, at : at + size]
                elif row < 5 * rows:
                    block, inner = divmod(row - rows, rows)
                    size = min(half - at, rows - inner)
                    first = group * rows + inner
                    up_w[first : first + size, block * D : block * D + D] = source[group, at : at + size]
                else:
                    size = half - at
                    first = group * deep + row - 5 * rows
                    down_w[first : first + size, :] = source[group, at : at + size]
                at += size

    @pl.when(core == 0)
    def _():
        place(0, mine)
        place(1, other)

    @pl.when(core == 1)
    def _():
        place(0, other)
        place(1, mine)


def picked(rows, first, source):
    ids = lax.broadcasted_iota(jnp.int32, (16, rows), 0) - lax.broadcasted_iota(jnp.int32, (16, rows), 1)
    return dot(jnp.where(ids == first, 1.0, 0.0).astype(bf16), source)


def split16(values):
    high = values.astype(bf16)
    return high, (values - high.astype(f32)).astype(bf16)


def place_inputs(centers, place_weight, place_bias, cen, place_w):
    for tile in range(cen.shape[0]):
        high, rest = split16(centers[:, tile * ROWS : tile * ROWS + ROWS])
        ids = lax.broadcasted_iota(jnp.int32, (16, ROWS), 0)
        ones = jnp.where((ids == 9) | (ids == 10), 1.0, 0.0)
        cen[tile] = (picked(3, 0, high) + picked(3, 3, rest) + picked(3, 6, high) + ones).astype(bf16)
    high, rest = split16(place_weight[...])
    bias_high, bias_rest = split16(place_bias[...])
    value = picked(3, 0, high) + picked(3, 3, high) + picked(3, 6, rest) + picked(1, 9, bias_high) + picked(1, 10, bias_rest)
    place_w[...] = value.astype(bf16)


def front_kernel(core, tokens, centers, targets, vec, place_weight, place_bias, mine, other,
                 entry, joint, mixture, shares, weights, joint_w, proj, cen, place_w, qkv):
    step = pl.program_id(0)

    @pl.when(step == 0)
    def _():
        qkv[ROWS:, :] = jnp.zeros((qkv.shape[0] - ROWS, 3 * D), bf16)
        unpack_early(core[0], mine, other, joint_w, proj)
        place_inputs(centers, place_weight, place_bias, cen, place_w)

    pre = dot(cen[step], place_w[...], TN)
    low = (pre * cdf(pre)).astype(bf16)
    placed = dot(low, proj[...]) + vec[1:2, :]
    hidden = hidden_column(targets[0], ROWS)
    rows = jnp.where(hidden > 0.5, vec[0:1, :], tokens[...].astype(f32)) + placed
    entry[...] = rows
    unit, _ = normalised(rows)
    normed = (unit * vec[2:3, :] + vec[3:4, :]).astype(bf16)
    for part in range(9):
        cols = slice(part * 128, part * 128 + 128)
        value = dot(normed, joint_w[:, cols])
        if part < 3:
            value = value * (0.125 * LOG2E)
        value = value.astype(bf16)
        qkv[:ROWS, cols] = value
        joint[:, cols] = value
    jobs = [(pair, cloud) for pair in range(PAIRS) for cloud in range(TILE)]
    tails = {}
    lanes = lax.broadcasted_iota(jnp.int32, (1, 2 * KEYS), 1) % KEYS
    sums_of = head_ones(1.0)
    for at in range(0, len(jobs), GROUP):
        group = jobs[at : at + GROUP]
        scores = []
        for pair, cloud in group:
            base = cloud * STEP
            query = qkv[base : base + WIN, pair * 128 : pair * 128 + 128]
            key = qkv[base : base + KEYS, D + pair * 128 : D + pair * 128 + 128]
            scores.append(dot(query, spread_heads(key.T)))
        exps = []
        for (pair, cloud), score in zip(group, scores):
            live = (lanes >= 2 * cloud) & (lanes < 2 * cloud + SEQ - 1)
            score = jnp.where(live, score, -1e30)
            parts = []
            for half in (score[:, :KEYS], score[:, KEYS:]):
                parts.append(jnp.exp2(half - jnp.max(half, axis=-1, keepdims=True)).astype(bf16))
            exps.append(jnp.concatenate(parts, axis=1))
        boths = []
        for (pair, cloud), e in zip(group, exps):
            base = cloud * STEP
            value = qkv[base : base + KEYS, 2 * D + pair * 128 : 2 * D + pair * 128 + 128]
            boths.append(dot(e, jnp.concatenate([stacked_heads(value), sums_of], axis=1)))
        for (pair, cloud), e, both in zip(group, exps, boths):
            base = cloud * STEP
            cols = slice(pair * 128, pair * 128 + 128)
            share = 1.0 / both[:, 128:]
            mix = both[:, :128] * share
            spot = slice(pair * 256, pair * 256 + 256)
            none = jnp.zeros((16, 2 * KEYS), bf16)
            weights[cloud, :16, spot] = jnp.where(row_range(16, 2 * cloud, 16, 256), e[:16], none)
            weights[cloud, 16:64, spot] = e[16:64]
            weights[cloud, 64:80, spot] = jnp.where(row_range(16, 0, 2 * cloud + 2, 256), e[64:80], none)
            head_mix, head_share = mix[:16], share[:16]
            if cloud:
                head = row_range(16, 0, 2 * cloud)
                tail_mix, tail_share = tails[pair]
                head_mix = jnp.where(head, tail_mix, head_mix)
                head_share = jnp.where(head, tail_share, head_share)
            mixture[base : base + 16, cols] = head_mix.astype(bf16)
            shares[base : base + 16, cols] = head_share.astype(bf16)
            mixture[base + 16 : base + 64, cols] = mix[16:64].astype(bf16)
            shares[base + 16 : base + 64, cols] = share[16:64].astype(bf16)
            tails[pair] = (mix[64:], share[64:])
            if cloud == TILE - 1:
                mixture[ROWS - 16 :, cols] = mix[64:].astype(bf16)
                shares[ROWS - 16 :, cols] = share[64:].astype(bf16)


def whole(shape):
    return pl.BlockSpec(shape, lambda i: (0,) * len(shape))


def rows_of(width, rows=ROWS):
    return pl.BlockSpec((rows, width), lambda i: (i, 0))


def slab(shape):
    return pl.BlockSpec((1, *shape), lambda i: (i,) + (0,) * len(shape))


def shape_of(dims, kind):
    return jax.ShapeDtypeStruct(dims, kind)


def cost(microseconds):
    return pl.CostEstimate(flops=int(microseconds * 9e8), bytes_accessed=int(microseconds * 2e6), transcendentals=0)


def settings():
    return pltpu.CompilerParams(vmem_limit_bytes=VMEM)


def front(core, tokens, centers, targets, vec, place_weight, place_bias, mine, other):
    count = tokens.shape[0]
    steps = count // ROWS
    return pl.pallas_call(
        front_kernel,
        grid=(steps,),
        in_specs=[
            pl.BlockSpec(memory_space=pltpu.SMEM), rows_of(D), whole(centers.shape), slab((1, 256)), whole((8, D)),
            whole((3, POSH)), whole((1, POSH)), whole(mine.shape), whole(other.shape),
        ],
        out_specs=[
            rows_of(D), rows_of(3 * D), rows_of(D), rows_of(D),
            pl.BlockSpec((TILE, WIN, HEADS * KEYS), lambda i: (i, 0, 0)), whole((D, 3 * D)), whole((POSH, D)),
            whole((steps, 16, ROWS)), whole((16, POSH)),
        ],
        out_shape=[
            shape_of((count, D), f32), shape_of((count, 3 * D), bf16),
            shape_of((count, D), bf16), shape_of((count, D), bf16),
            shape_of((steps * TILE, WIN, HEADS * KEYS), bf16), shape_of((D, 3 * D), bf16), shape_of((POSH, D), bf16),
            shape_of((steps, 16, ROWS), bf16), shape_of((16, POSH), bf16),
        ],
        scratch_shapes=[pltpu.VMEM((ROWS + 48, 3 * D), bf16)],
        compiler_params=settings(),
        cost_estimate=cost(28),
        name="front",
    )(core, tokens, centers, targets, vec, place_weight, place_bias, mine, other)


def write_sums(sums, order, first, values):
    size = sums.shape[0] // len(order)
    at = 0
    while at < values.shape[0]:
        row = first + at
        segment, inner = divmod(row, size)
        step = min(size - inner, values.shape[0] - at)
        spot = order[segment] * size + inner
        sums[spot : spot + step, :] = values[at : at + step].astype(bf16)
        at += step


def share_halves(core, sums, kept, sent):
    half = sent.shape[0]
    kept[...] = sums[pl.ds(pl.multiple_of(core * half, 16), half), :]
    sent[...] = sums[pl.ds(pl.multiple_of((1 - core) * half, 16), half), :]


def padded(rows, size):
    return -(-rows // (16 * size)) * 16 * size


def middle_kernel(chunk, order, core, entry, mixture, shares, cot, vec, up_b, mine, other,
                  middle, gated, mid_grad, mix_grad, kept, sent, up_bg, vec_g, down_w,
                  down_acc, up_acc, out_acc, out_w, up_w, sums):
    step = pl.program_id(0)

    @pl.when(step == 0)
    def _():
        unpack_late(core[0], mine, other, out_w, up_w, down_w)
        for ref in (down_acc, up_acc, out_acc, up_bg, vec_g):
            ref[...] = jnp.zeros(ref.shape, ref.dtype)

    parts = FF // chunk
    spans = [slice(part * chunk, part * chunk + chunk) for part in range(parts)]
    mix = mixture[...]
    cotangent = cot[...]
    mid = entry[...] + (dot(mix, out_w[...]) + vec[4:5, :])
    gates = [dot(cotangent, down_w[spans[0], :], NT)]
    middle[...] = mid
    unit, scale = normalised(mid)
    normed = (unit * vec[5:6, :] + vec[6:7, :]).astype(bf16)
    lows = []

    def down_part(part):
        down_acc[:, spans[part]] += dot(cotangent, gated[:, spans[part]], TN)

    def up_part(part):
        up_acc[:, spans[part]] += dot(normed, lows[part], TN)

    for part in range(parts):
        cols = spans[part]
        raised = dot(normed, up_w[:, cols]) + up_b[:, cols]
        if part + 1 < parts:
            gates.append(dot(cotangent, down_w[spans[part + 1], :], NT))
        mass = cdf(raised)
        gated[:, cols] = (raised * mass).astype(bf16)
        grad = gates[part] * smooth_slope(raised, mass)
        up_bg[:, cols] += jnp.sum(grad, axis=0, keepdims=True)
        lows.append(grad.astype(bf16))
        if part:
            down_part(part - 1)
            if part > 1:
                up_part(part - 2)
    back = dot(jnp.concatenate(lows, axis=1), up_w[...], NT)
    up_part(parts - 2)
    down_part(parts - 1)
    up_part(parts - 1)
    upstream = cotangent.astype(f32)
    tilted = back * vec[5:6, :]
    grad = upstream + scale * (tilted - row_mean(tilted) - unit * row_mean(tilted * unit))
    mid_grad[...] = grad
    low = grad.astype(bf16)
    mix_grad[...] = (dot(low, out_w[...], NT) * shares[...].astype(f32)).astype(bf16)
    out_acc[...] += dot(mix, low, TN)
    vec_g[0:1, :] += jnp.sum(back * unit, axis=0, keepdims=True)
    vec_g[1:2, :] += jnp.sum(back, axis=0, keepdims=True)
    vec_g[2:3, :] += jnp.sum(grad, axis=0, keepdims=True)
    vec_g[3:4, :] += jnp.sum(upstream, axis=0, keepdims=True)

    @pl.when(step == pl.num_programs(0) - 1)
    def _():
        for part in range(4):
            write_sums(sums, order, part * D, up_acc[:, part * D : part * D + D])
        write_sums(sums, order, 4 * D, down_acc[...].T)
        write_sums(sums, order, 8 * D, out_acc[...])
        if sums.shape[0] > 9 * D:
            write_sums(sums, order, 9 * D, jnp.zeros((sums.shape[0] - 9 * D, D), f32))
        share_halves(core[0], sums, kept, sent)


def middle_part(core, entry, mixture, shares, cot, vec, up_b, mine, other, order, rows=1056, chunk=512):
    count = entry.shape[0]
    size = padded(9 * D, len(order))
    return pl.pallas_call(
        functools.partial(middle_kernel, chunk, order),
        grid=(count // rows,),
        in_specs=[
            pl.BlockSpec(memory_space=pltpu.SMEM), rows_of(D, rows), rows_of(D, rows), rows_of(D, rows), rows_of(D, rows),
            whole((8, D)), whole((1, FF)), whole(mine.shape), whole(other.shape),
        ],
        out_specs=[
            rows_of(D, rows), rows_of(FF, rows), rows_of(D, rows), rows_of(D, rows),
            whole((size // 2, D)), whole((size // 2, D)), whole((1, FF)), whole((8, D)), whole((FF, D)),
        ],
        out_shape=[
            shape_of((count, D), f32), shape_of((count, FF), bf16), shape_of((count, D), f32), shape_of((count, D), bf16),
            shape_of((size // 2, D), bf16), shape_of((size // 2, D), bf16),
            shape_of((1, FF), f32), shape_of((8, D), f32), shape_of((FF, D), bf16),
        ],
        scratch_shapes=[
            pltpu.VMEM((D, FF), f32), pltpu.VMEM((D, FF), f32), pltpu.VMEM((D, D), f32),
            pltpu.VMEM((D, D), bf16), pltpu.VMEM((D, FF), bf16), pltpu.VMEM((size, D), bf16),
        ],
        compiler_params=settings(),
        cost_estimate=cost(55),
        name="middle",
    )(core, entry, mixture, shares, cot, vec, up_b, mine, other)


def back_kernel(is_first, is_last, order, *refs):
    entry, joint, mixture, weights, mix_grad, mid_grad, cen, targets, vec, place_w, proj, joint_w = refs[:12]
    refs = refs[12:]
    if not is_first:
        before, refs = refs[1:5], refs[5:]
    if is_last:
        core, up_bg, mid_vec_g, tokens_g, kept, sent, joint_g, proj_g, place_g, vec_g, qkv, dqkv, sums = refs
    else:
        tokens_g, joint_g, proj_g, place_g, vec_g, qkv, dqkv = refs
    step = pl.program_id(0)

    @pl.when(step == 0)
    def _():
        for at, ref in enumerate((joint_g, proj_g, place_g, vec_g)):
            ref[...] = jnp.zeros(ref.shape, ref.dtype) if is_first else before[at][...]
        qkv[ROWS:, :] = jnp.zeros((qkv.shape[0] - ROWS, 3 * D), bf16)

    qkv[:ROWS, :] = joint[...]
    pre = dot(cen[0], place_w[...], TN)
    unit, scale = normalised(entry[...])
    normed = (unit * vec[2:3, :] + vec[3:4, :]).astype(bf16)
    minus = lane_ones(-1.0)
    jobs = [(pair, cloud) for pair in range(PAIRS) for cloud in range(TILE)]
    tails = {}
    for at in range(0, len(jobs), GROUP):
        group = jobs[at : at + GROUP]
        gaps = []
        for pair, cloud in group:
            base = cloud * STEP
            window = slice(base, base + WIN)
            cols = slice(pair * 128, pair * 128 + 128)
            value = qkv[base : base + KEYS, 2 * D + pair * 128 : 2 * D + pair * 128 + 128]
            dmw = mix_grad[window, cols]
            left = jnp.concatenate([dmw, dmw * mixture[window, cols]], axis=1)
            gaps.append(dot(left, jnp.concatenate([spread_heads(value.T), minus], axis=0)))
        es, dss = [], []
        for (pair, cloud), gap in zip(group, gaps):
            e = weights[cloud, :, pair * 256 : pair * 256 + 256]
            es.append(e)
            dss.append((e.astype(f32) * gap).astype(bf16))
        results = []
        for (pair, cloud), e, ds in zip(group, es, dss):
            base = cloud * STEP
            query = stacked_heads(qkv[base : base + WIN, pair * 128 : pair * 128 + 128])
            key = stacked_heads(qkv[base : base + KEYS, D + pair * 128 : D + pair * 128 + 128])
            sdm = stacked_heads(mix_grad[base : base + WIN, pair * 128 : pair * 128 + 128])
            e = jnp.concatenate([e[:, :KEYS], e[:, KEYS:]], axis=0)
            tall = jnp.concatenate([ds[:, :KEYS], ds[:, KEYS:]], axis=0)
            results.append((dot(ds, key), dot(tall, query, TN), dot(e, sdm, TN)))
        for (pair, cloud), (dq, dk, dv) in zip(group, results):
            base = cloud * STEP
            parts = (dq * 0.125, dk[:WIN] * (1.0 / LOG2E), dv[:WIN])
            for which, part in enumerate(parts):
                cols = slice(which * D + pair * 128, which * D + pair * 128 + 128)
                head = part[:16]
                if cloud:
                    head = jnp.where(row_range(16, 0, 2 * cloud), tails[pair, which], head)
                dqkv[base : base + 16, cols] = head.astype(bf16)
                dqkv[base + 16 : base + 64, cols] = part[16:64].astype(bf16)
                tails[pair, which] = part[64:80]
                if cloud == TILE - 1:
                    dqkv[ROWS - 16 :, cols] = part[64:80].astype(bf16)


    back = dot(dqkv[...], joint_w[...], NT)
    for part in range(3):
        cols = slice(part * D, part * D + D)
        joint_g[:, cols] += dot(normed, dqkv[:, cols], TN)
    tilted = back * vec[2:3, :]
    grad = mid_grad[...] + scale * (tilted - row_mean(tilted) - unit * row_mean(tilted * unit))
    low = grad.astype(bf16)
    mass = cdf(pre)
    place_low = (pre * mass).astype(bf16)
    pre_grad = dot(low, proj[...], NT) * smooth_slope(pre, mass)
    proj_g[...] += dot(place_low, low, TN)
    hidden = hidden_column(targets[0], ROWS)
    marked = jnp.where(hidden > 0.5, grad, 0.0)
    tokens_g[...] = (grad - marked).astype(bf16)
    high_part = pre_grad.astype(bf16)
    low_part = (pre_grad - high_part.astype(f32)).astype(bf16)
    place_g[...] += dot(cen[0], jnp.concatenate([high_part, low_part], axis=1))
    vec_g[0:1, :] += jnp.sum(marked, axis=0, keepdims=True)
    vec_g[1:2, :] += jnp.sum(grad, axis=0, keepdims=True)
    vec_g[2:3, :] += jnp.sum(back * unit, axis=0, keepdims=True)
    vec_g[3:4, :] += jnp.sum(back, axis=0, keepdims=True)
    if not is_last:
        return

    @pl.when(step == pl.num_programs(0) - 1)
    def _():
        for part in range(3):
            write_sums(sums, order, part * D, joint_g[:, part * D : part * D + D])
        write_sums(sums, order, 3 * D, proj_g[...])
        place = place_g[:, :POSH] + place_g[:, POSH:]
        place_weight = place[0:3] + place_g[3:6, :POSH]
        small = jnp.concatenate(
            [
                vec_g[0:4, :],
                mid_vec_g[0:4, :],
                jnp.concatenate([place_weight[0:1], place_weight[1:2], place_weight[2:3]], axis=1),
                jnp.concatenate([place[9:10], jnp.zeros((1, D - POSH), f32)], axis=1),
                jnp.concatenate([up_bg[:, part * D : part * D + D] for part in range(4)], axis=0),
                jnp.zeros((sums.shape[0] - 3 * D - POSH - 14, D), f32),
            ],
            axis=0,
        )
        write_sums(sums, order, 3 * D + POSH, small)
        share_halves(core[0], sums, kept, sent)


def back_part(given, first, steps, order, before=None, extra=None):
    count = given[0].shape[0]

    def shifted(width):
        return pl.BlockSpec((ROWS, width), lambda i: (i + first, 0))

    def shifted_slab(shape):
        return pl.BlockSpec((1, *shape), lambda i: (i + first, 0, 0))

    accs = [(D, 3 * D), (POSH, D), (16, 256), (8, D)]
    in_specs = [
        shifted(D), shifted(3 * D), shifted(D),
        pl.BlockSpec((TILE, WIN, HEADS * KEYS), lambda i: (i + first, 0, 0)),
        shifted(D), shifted(D), shifted_slab((16, ROWS)), shifted_slab((1, 256)),
        whole((8, D)), whole((16, POSH)), whole((POSH, D)), whole((D, 3 * D)),
    ]
    given = list(given)
    if before is not None:
        given += before
        in_specs += [pl.BlockSpec(memory_space=pl.ANY)] + [whole(acc) for acc in accs]
    out_specs, out_shape = [shifted(D)], [shape_of((count, D), bf16)]
    scratch = [pltpu.VMEM((ROWS + 48, 3 * D), bf16), pltpu.VMEM((ROWS, 3 * D), bf16)]
    if extra is not None:
        given += extra
        in_specs += [pl.BlockSpec(memory_space=pltpu.SMEM), whole((1, FF)), whole((8, D))]
        size = padded(3 * D + POSH + 16, len(order))
        out_specs += [whole((size // 2, D))] * 2
        out_shape += [shape_of((size // 2, D), bf16)] * 2
        scratch = [pltpu.VMEM(acc, f32) for acc in accs] + scratch + [pltpu.VMEM((size, D), bf16)]
    else:
        out_specs += [whole(acc) for acc in accs]
        out_shape += [shape_of(acc, f32) for acc in accs]
    return pl.pallas_call(
        functools.partial(back_kernel, before is None, extra is not None, order),
        grid=(steps,),
        in_specs=in_specs,
        out_specs=out_specs,
        out_shape=out_shape,
        scratch_shapes=scratch,
        input_output_aliases={} if before is None else {12: 0},
        compiler_params=settings(),
        cost_estimate=cost(5 * steps),
        name="back",
    )(*given)


def finish_kernel(middle, gated, vec, down_w, output):
    output[...] = (middle[...] + (dot(gated[...], down_w[...]) + vec[7:8, :])).astype(bf16)


def finish(middle, gated, vec, down_w, rows=528):
    count = middle.shape[0]
    return pl.pallas_call(
        finish_kernel,
        grid=(count // rows,),
        in_specs=[rows_of(D, rows), rows_of(FF, rows), whole((8, D)), whole((FF, D))],
        out_specs=rows_of(D, rows),
        out_shape=shape_of((count, D), bf16),
        compiler_params=settings(),
        cost_estimate=cost(12),
        name="finish",
    )(middle, gated, vec, down_w)


def marked_targets(mask_count, mask_index):
    clouds, most = mask_index.shape
    slot = jnp.arange(most, dtype=jnp.int32)[None, :]
    cloud = (jnp.arange(clouds, dtype=jnp.int32) % TILE)[:, None]
    targets = jnp.where(slot < mask_count[:, None], mask_index + (1 + SEQ * cloud), -1)
    return jnp.pad(targets, ((0, 0), (0, 32 - most)), constant_values=-1).reshape(clouds // TILE, 1, 256)


def joined_offsets(size):
    held, groups = [0], [[0]]
    bit = size // 2
    while bit:
        groups.append([offset ^ bit for offset in held])
        held = held + groups[-1]
        bit //= 2
    return groups


def close_kernel(groups, spot, *refs):
    pieces, (joint_g, proj_g, small, sums) = refs[:-4], refs[-4:]
    segment = pieces[0].shape[0]
    for piece, offsets in zip(pieces, groups):
        for at, offset in enumerate(offsets):
            row = pl.multiple_of((spot[0] ^ offset) * segment, 16)
            sums[pl.ds(row, segment), :] = piece[at * segment : at * segment + segment, :]
    for part in range(3):
        joint_g[:, part * D : part * D + D] = sums[part * D : part * D + D, :].astype(f32)
    proj_g[...] = sums[3 * D : 3 * D + POSH, :].astype(f32)
    small[...] = sums[3 * D + POSH : 3 * D + POSH + 16, :].astype(f32)


def close(spot, pieces, size):
    vmem = pl.BlockSpec(memory_space=pltpu.VMEM)
    return pl.pallas_call(
        functools.partial(close_kernel, joined_offsets(size)),
        in_specs=[pl.BlockSpec(memory_space=pltpu.SMEM)] + [vmem] * len(pieces),
        out_specs=[vmem] * 3,
        out_shape=[shape_of((D, 3 * D), f32), shape_of((POSH, D), f32), shape_of((16, D), f32)],
        scratch_shapes=[pltpu.VMEM((pieces[0].shape[0] * size, D), bf16)],
        compiler_params=settings(),
        name="close",
    )(spot, *pieces)


CALLS = 4


def bits_of(size):
    return [1 << bit for bit in range(size.bit_length() - 1)]


def spot_of(index, size):
    spot, span = 0, size
    for bit in bits_of(size):
        span //= 2
        spot += span * ((index // bit) % 2)
    return spot


def segments(size):
    return [spot_of(index, size) for index in range(size)]


def swapped(values, bit, size):
    return lax.ppermute(values, "dp", [(i, i ^ bit) for i in range(size)])


def total(terms):
    return sum(term.astype(f32) for term in terms).astype(bf16)


def halves(terms, bit):
    side = (lax.axis_index("dp") // bit) % 2
    pairs = [term.reshape(2, term.shape[0] // 2, D) for term in terms]
    sent = [lax.dynamic_index_in_dim(pair, 1 - side, 0, keepdims=False) for pair in pairs]
    kept = [lax.dynamic_index_in_dim(pair, side, 0, keepdims=False) for pair in pairs]
    return sent, kept


def halved(terms, bit, size, ready=None):
    sent, kept = halves(terms, bit)
    return kept + [swapped(total(sent) if ready is None else ready, bit, size)]


def across(terms, bit, size):
    value = total(terms)
    return [value, lax.ppermute(value, "fsdp", [(i, i ^ bit) for i in range(size)])]


def tied(first, second):
    return lax.optimization_barrier((first, second))


def wide(blocks):
    return jnp.concatenate(blocks, axis=1).astype(f32)


def per_device(
    sizes,
    tokens,
    centers,
    mask_count,
    mask_index,
    mask_embed,
    place_weight,
    place_bias,
    place_proj,
    place_shift,
    norm_gain,
    norm_shift,
    joint_weight,
    out_weight,
    out_bias,
    mlp_gain,
    mlp_shift,
    up_weight,
    up_bias,
    down_weight,
    down_bias,
    cotangent,
):
    dp, fsdp = sizes["dp"], sizes["fsdp"]
    spot = lax.axis_index("dp").astype(jnp.int32)[None]
    core = spot % 2
    early, late = pack(core, place_proj, joint_weight, out_weight, up_weight, down_weight)
    early = lax.all_gather(early, "fsdp", axis=0)
    early_other = swapped(early, 1, dp)
    late, early = tied(late, early)
    late = lax.all_gather(late, "fsdp", axis=0)
    targets = marked_targets(mask_count, mask_index)
    vec = jnp.stack([mask_embed, place_shift, norm_gain, norm_shift, out_bias, mlp_gain, mlp_shift, down_bias])
    up_b = up_bias[None, :]
    entry, joint, mixture, shares, weights, joint_w, proj, cen, place_w = front(
        core, tokens, centers, targets, vec, place_weight, place_bias[None, :], early, early_other
    )
    late_other = swapped(late, 1, dp)
    late, mixture = tied(late, mixture)
    late_other = swapped(late, 1, dp)
    order = segments(dp)
    middle, gated, mid_grad, mix_grad, kept, sent, up_bg, vec_g, down_w = middle_part(
        core, entry, mixture, shares, cotangent, vec, up_b, late, late_other, order
    )
    stages = [functools.partial(halved, bit=bit, size=dp) for bit in bits_of(dp)]
    stages += [functools.partial(across, bit=bit, size=fsdp) for bit in bits_of(fsdp)]
    steps = tokens.shape[0] // ROWS
    parts = [steps * (part + 1) // CALLS - steps * part // CALLS for part in range(CALLS)]
    before, first = None, 0
    sums = [kept, swapped(sent, 1, dp)]
    for part, count in enumerate(parts):
        if part:
            mix_grad, sums[-1] = tied(mix_grad, sums[-1])
            sums = stages[part](sums)
        given = (entry, joint, mixture, weights, mix_grad, mid_grad, cen, targets, vec, place_w, proj, joint_w)
        extra = [core, up_bg, vec_g] if part == CALLS - 1 else None
        before = back_part(given, first, count, order, before, extra)
        first += count
    tokens_grad, kept, sent = before
    sent, sums[-1] = tied(sent, sums[-1])
    for stage in stages[CALLS:]:
        sums = stage(sums)
    last = stages[1]([kept, swapped(sent, 1, dp)])
    output = finish(middle, gated, vec, down_w)
    sums[-1], output = tied(sums[-1], output)
    sums = total(sums)
    last[-1], sums = tied(last[-1], sums)
    sums = lax.all_gather(sums, "dp", axis=0, tiled=True)
    for stage in stages[2:]:
        last = stage(last)
    pieces = [total(last)]
    for bit in reversed(bits_of(dp)):
        held = pieces[0] if len(pieces) == 1 else jnp.concatenate(pieces, axis=0)
        pieces.append(swapped(held, bit, dp))
    joint_grad, proj_grad, small = close(spot, pieces, dp)
    up_grad = wide([sums[part * D : part * D + D] for part in range(4)])
    down_grad = sums[4 * D : 8 * D].astype(f32)
    out_grad = sums[8 * D : 9 * D].astype(f32)
    return (
        output,
        tokens_grad,
        small[0],
        small[8].reshape(3, POSH),
        small[9, :POSH],
        proj_grad,
        small[1],
        small[2],
        small[3],
        joint_grad,
        out_grad,
        small[6],
        small[4],
        small[5],
        up_grad,
        small[10:14].reshape(FF),
        down_grad,
        small[7],
    )


def solution(mesh):
    rows = P(("dp", "fsdp"), None)
    in_specs = (
        rows,
        P(None, ("dp", "fsdp")),
        P(("dp", "fsdp")),
        rows,
        P(),
        P(),
        P(),
        P("fsdp", None),
        P(),
        P(),
        P(),
        P("fsdp", None),
        P("fsdp", None),
        P(),
        P(),
        P(),
        P("fsdp", None),
        P(),
        P("fsdp", None),
        P(),
        rows,
    )
    out_specs = (rows, rows) + (P(),) * 16
    return jax.shard_map(
        functools.partial(per_device, dict(mesh.shape)), mesh=mesh, in_specs=in_specs, out_specs=out_specs, check_vma=False
    )
```

time: 840 us -> 259 us (0.31); the launches traced: 830 us -> 258 us
  matrix products: 261 us -> 0 us
  local copies, waits for them, and re-layouts: 251 us -> 14.5 us
  Pallas kernels: 0 us -> 151 us
  blocking collectives: 168 us -> 17.2 us
  other arithmetic: 61.3 us -> 11.1 us
  waiting for transfers between devices: 73.5 us -> 36 us
  starting transfers between devices: 0.4 us -> 13.9 us
    dot_general x73 -> x0, matrix products: 261 us -> none  [the longest x5 96.7 us: product(): return jnp.dot(left, right, preferred_element_type=jnp.float32)]
    pallas_call x0 -> x9, Pallas kernels: none -> 151 us  [the longest x4 53.2 us: back_part(): pl.pallas_call(functools.partial(back_kernel, before is None, extra is no...]
    all_gather x6 -> x1, blocking collectives: 101 us -> 17.2 us  [per_device(): early = lax.all_gather(early, 'fsdp', axis=0)]
    reshape x4 -> x2, local copies, waits for them, and re-layouts: 77.4 us -> 1.29 us  [the longest x1 0.68 us: marked_targets(): jnp.pad(targets, ((0, 0), (0, 32 - most)), constant_values=-1)]
    psum x2 -> x0, blocking collectives: 66.3 us -> none  [the longest x1 41.2 us: per_device(): lax.psum((embed_grad, place_weight_grad, place_bias_grad, place_shift_gra...]
    while x2 -> x0, local copies, waits for them, and re-layouts: 41.8 us -> none  [the longest x1 30.2 us: per_device(): mixture_tiles, log_totals = lax.map(attend_tile, joint_tiles)]
    dynamic_update_slice x16 -> x0, local copies, waits for them, and re-layouts: 41.4 us -> none  [the longest x8 29.5 us: per_device(): lax.map(attend_back, (joint_tiles, mixture_grad.reshape(tile_count, TILE,...]
    psum x1 -> x0, waiting for transfers between devices: 38.1 us -> none  [per_device(): owned = lax.psum((owned[0], owned[1], owned[2], owned[3], owned[4]), 'dp')]
  transfers between devices with their start and end apart: 10 -> 17, of which waited for: 3 -> 8; matrix products, arithmetic and copies ran while one was open for 60% -> 6% of each run, Pallas kernels for 0% -> 38%
where the time goes in v1:
time: 259 us; the launch traced here: 258 us
  Pallas kernels  151 us (58%)
  waiting for transfers between devices  36 us (14%)
  blocking collectives  17.2 us (7%)
  local copies, waits for them, and re-layouts  14.5 us (6%)
  between operations  14.3 us (6%)
  starting transfers between devices  13.9 us (5%)
  other arithmetic  11.1 us (4%)
    pallas_call x4, Pallas kernels, back_part(): pl.pallas_call(functools.partial(back_kernel, before is None, extra is no...  53.2 us
    pallas_call x1, Pallas kernels, middle_part(): pl.pallas_call(functools.partial(middle_kernel, chunk, order), grid=(coun...  51.6 us
    pallas_call x1, Pallas kernels, front(): pl.pallas_call(front_kernel, grid=(steps,), in_specs=[pl.BlockSpec(memory...  27.9 us
    ppermute x11, waiting for transfers between devices, swapped(): return lax.ppermute(values, 'dp', [(i, i ^ bit) for i in range(size)])  25.9 us
    all_gather x1, blocking collectives, per_device(): early = lax.all_gather(early, 'fsdp', axis=0)  17.2 us
    pallas_call x1, Pallas kernels, finish(): pl.pallas_call(finish_kernel, grid=(count // rows,), in_specs=[rows_of(D,...  13.9 us
    ppermute x4, waiting for transfers between devices, across(): lax.ppermute(value, 'fsdp', [(i, i ^ bit) for i in range(size)])  10.1 us
    ppermute x11, starting transfers between devices, swapped(): return lax.ppermute(values, 'dp', [(i, i ^ bit) for i in range(size)])  6.95 us
  transfers between devices with their start and end apart: 17, of which 8 were waited for; matrix products, arithmetic and copies ran while one was open for 6% of the time, Pallas kernels for 38%

profile of v1, /device:TPU:0, one launch (start us, length us, event | category | flops | bytes accessed | tf_op | source)
XLA Modules:
  0.0 258.4 jit_solution(10342914029807426831)
XLA Ops:
  7.2 2.1 pack.1
  9.3 17.2 %all-gather = bf16[640,384]{1,0:T(8,128)(2,1)S(1)} all-gather(bf16[160,384]{1,0:T(8,128)(2,1)} %get-tuple-element.76), channel_id=2, replica_groups=mesh['dp'=8,'fsdp'=4] {'fsdp'}, dimensions={0}, use_global_device_ids=true | all-gather | bytes 614400 | tf_op jit(solution)/shard_map/all_gather | solution.py:768
  26.6 0.7 stack.27
  27.3 0.7 stack.28
  28.0 0.7 stack.29
  28.7 0.7 stack.30
  29.4 0.7 stack.31
  30.1 0.7 stack.32
  30.7 0.7 stack.33
  31.4 0.7 stack.34
  32.1 0.7 add_select_fusion
  32.8 0.1 copy.49
  32.9 0.7 reshape.136.targets.refs_7_
  33.6 0.6 stack.35.vec.refs_8_
  34.2 0.8 copy-done.9
  35.0 27.9 %front.1 = (f32[4224,384]{1,0:T(8,128)}, bf16[4224,1152]{1,0:T(8,128)(2,1)}, bf16[4224,384]{1,0:T(8,128)(2,1)}, bf16[4224,384]{1,0:T(8,128)(2,1)}, bf16[64,80,76...) custom-call(s32[1]{0:T(128)S(6)} %select_n.76.spot.core.refs_17_, ...), custom_call_target="tpu_custom_call" | custom-call | flops 25200001024 | bytes 56000000 | tf_op jit(solution)/shard_map/front/pallas_call | solution.py:324
  63.0 0.5 collective-permute-start.1
  63.5 0.6 broadcast_in_dim.19.up_b
  64.1 2.3 collective-permute-done.1.other
  66.4 1.1 copy-done.8
  67.5 51.6 %middle.1 = (f32[4224,384]{1,0:T(8,128)}, bf16[4224,1536]{1,0:T(8,128)(2,1)}, f32[4224,384]{1,0:T(8,128)}, bf16[4224,384]{1,0:T(8,128)(2,1)}, bf16[1728,384]{1,0...) custom-call(s32[1]{0:T(128)S(6)} %select_n.76.spot.core.refs_17_, ...), custom_call_target="tpu_custom_call" | custom-call | flops 49500000256 | bytes 110000000 | tf_op jit(solution)/shard_map/middle/pallas_call | solution.py:443
  119.1 0.4 collective-permute-start.2
  119.6 12.9 %back.4 = (bf16[4224,384]{1,0:T(8,128)(2,1)}, f32[384,1152]{1,0:T(8,128)}, f32[128,384]{1,0:T(8,128)}, f32[16,256]{1,0:T(8,128)}, f32[8,384]{1,0:T(8,128)}) custom-call(f32[4224,384]{1,0:T(8,128)} %get-tuple-element.78.entry.refs_0_, bf16[4224,1152]{1,0:T(8,128)(2,1)} %get-tuple-element.92.refs_1_, bf16[4224,384]{1,0:T(8,128)(2,1)} %get-tuple-element.81.mixture.refs_2_, ...), custom_call_target="tpu_custom_call" | custom-call | flops 8999999488 | bytes 20000000 | tf_op jit(solution)/shard_map/back/pallas_call | solution.py:611
  132.5 0.1 constant_dynamic-slice_fusion.2
  132.6 1.0 fusion
  133.6 1.5 collective-permute-start.3
  135.1 13.3 %back.5 = (bf16[4224,384]{1,0:T(8,128)(2,1)}, f32[384,1152]{1,0:T(8,128)}, f32[128,384]{1,0:T(8,128)}, f32[16,256]{1,0:T(8,128)}, f32[8,384]{1,0:T(8,128)}) custom-call(f32[4224,384]{1,0:T(8,128)} %get-tuple-element.78.entry.refs_0_, bf16[4224,1152]{1,0:T(8,128)(2,1)} %get-tuple-element.92.refs_1_, ...), custom_call_target="tpu_custom_call", output_to_operand_aliasing={{0}: (12, {})} | custom-call | flops 8999999488 | bytes 20000000 | tf_op jit(solution)/shard_map/back/pallas_call | solution.py:611
  148.4 2.4 collective-permute-done.3
  150.8 0.1 fusion.2
  150.9 1.6 collective-permute-start.4
  152.5 13.6 %back.6 = (bf16[4224,384]{1,0:T(8,128)(2,1)}, f32[384,1152]{1,0:T(8,128)}, f32[128,384]{1,0:T(8,128)}, f32[16,256]{1,0:T(8,128)}, f32[8,384]{1,0:T(8,128)}) custom-call(f32[4224,384]{1,0:T(8,128)} %get-tuple-element.78.entry.refs_0_, bf16[4224,1152]{1,0:T(8,128)(2,1)} %get-tuple-element.92.refs_1_, ...), custom_call_target="tpu_custom_call", output_to_operand_aliasing={{0}: (12, {})} | custom-call | flops 8999999488 | bytes 20000000 | tf_op jit(solution)/shard_map/back/pallas_call | solution.py:611
  166.1 0.2 fusion.1
  166.3 2.2 collective-permute-start.5
  168.5 13.5 %back.7 = (bf16[4224,384]{1,0:T(8,128)(2,1)}, bf16[704,384]{1,0:T(8,128)(2,1)}, bf16[704,384]{1,0:T(8,128)(2,1)}) custom-call(f32[4224,384]{1,0:T(8,128)} %get-tuple-element.78.entry.refs_0_, bf16[4224,1152]{1,0:T(8,128)(2,1)} %get-tuple-element.92.refs_1_, bf16[4224,384]{1,0:T(8,128)(2,1)} %get-tuple-element.81.mixture.refs_2_, ...), custom_call_target="tpu_custom_call", output_to_operand_aliasing={{0}: (12, {})} | custom-call | flops 8999999488 | bytes 20000000 | tf_op jit(solution)/shard_map/back/pallas_call | solution.py:611
  181.9 0.1 collective-permute-start.7
  182.0 0.1 add_convert_fusion.2
  182.1 2.6 %collective-permute-start.6 = (bf16[432,384]{1,0:T(8,128)(2,1)S(1)}, bf16[432,384]{1,0:T(8,128)(2,1)S(1)}, u32[]{:S(2)}, u32[]{:S(2)}) collective-permute-start(bf16[432,384]{1,0:T(8,128)(2,1)S(1)} %add_convert_fusion.2), channel_id=1, source_target_pairs={{0,2},{1,3},{2,0},{3,1},{4,6},{5,7},{6,4},{7,5},{8,10},{9,11},{10,... | collective-permute-start | bytes 995336 | tf_op jit(solution)/shard_map/ppermute | solution.py:729
  184.7 1.0 fusion.3
  185.7 1.5 collective-permute-start.8
  187.3 13.9 %finish.1 = bf16[4224,384]{1,0:T(8,128)(2,1)} custom-call(f32[4224,384]{1,0:T(8,128)} %get-tuple-element.119.middle, bf16[4224,1536]{1,0:T(8,128)(2,1)} %get-tuple-element.120.gated, f32[8,384]{1,0:T(8,128)} %stack.35.vec.refs_8_, bf16[1536,384]{1,0:T(8,128)(2,1)} %get-tuple-element.121.down_w), custom_call_target="tpu_custom_call" | custom-call | flops 10800000000 | bytes 24000000 | tf_op jit(solution)/shard_map/finish/pallas_call | solution.py:631
  201.2 0.8 add_convert_fusion.1
  202.1 0.1 fusion.5
  202.2 0.6 collective-permute-start.9
  202.7 4.9 %collective-permute-done.9 = bf16[176,384]{1,0:T(8,128)(2,1)S(1)} collective-permute-done((bf16[176,384]{1,0:T(8,128)(2,1)S(1)}, bf16[176,384]{1,0:T(8,128)(2,1)S(1)}, u32[]{:S(2)}, u32[]{:S(2)}) %collective-permute-start.9) | collective-permute-done | bytes 135200 | tf_op jit(solution)/shard_map/ppermute | solution.py:707
  207.7 0.1 fusion.4
  207.7 0.1 collective-permute-start.10
  207.8 5.0 %collective-permute-done.10 = bf16[176,384]{1,0:T(8,128)(2,1)S(1)} collective-permute-done((bf16[176,384]{1,0:T(8,128)(2,1)S(1)}, bf16[176,384]{1,0:T(8,128)(2,1)S(1)}, u32[]{:S(2)}, u32[]{:S(2)}) %collective-permute-start.10) | collective-permute-done | bytes 135200 | tf_op jit(solution)/shard_map/ppermute | solution.py:729
  212.9 2.0 collective-permute-start.11
  214.9 5.1 %collective-permute-done.11 = bf16[176,384]{1,0:T(8,128)(2,1)S(1)} collective-permute-done((bf16[176,384]{1,0:T(8,128)(2,1)S(1)}, bf16[176,384]{1,0:T(8,128)(2,1)S(1)}, u32[]{:S(2)}, u32[]{:S(2)}) %collective-permute-start.11) | collective-permute-done | bytes 135200 | tf_op jit(solution)/shard_map/ppermute | solution.py:729
  220.0 0.6 collective-permute-start.12
  220.6 7.9 %collective-permute-done.12.refs_1_ = bf16[176,384]{1,0:T(8,128)(2,1)S(1)} collective-permute-done((bf16[176,384]{1,0:T(8,128)(2,1)S(1)}, bf16[176,384]{1,0:T(8,128)(2,1)S(1)}, u32[]{:S(2)}, u32[]{:S(2)}) %collective-permute-start.12) | collective-permute-done | bytes 135200 | tf_op jit(solution)/shard_map/ppermute | solution.py:707
  228.5 0.1 collective-permute-start.13
  228.6 6.4 %collective-permute-done.13.refs_2_ = bf16[352,384]{1,0:T(8,128)(2,1)S(1)} collective-permute-done((bf16[352,384]{1,0:T(8,128)(2,1)S(1)}, bf16[352,384]{1,0:T(8,128)(2,1)S(1)}, u32[]{:S(2)}, u32[]{:S(2)}) %collective-permute-start.13) | collective-permute-done | bytes 270368 | tf_op jit(solution)/shard_map/ppermute | solution.py:707
  235.1 0.1 collective-permute-start.14
  235.2 1.9 collective-permute-done.14.refs_3_
  237.1 0.8 copy-done.5
  237.9 2.7 %close.1 = (f32[384,1152]{1,0:T(8,128)}, f32[128,384]{1,0:T(8,128)}, f32[16,384]{1,0:T(8,128)}) custom-call(s32[1]{0:T(128)} %bitcast.spot, bf16[176,384]{1,0:T(8,128)(2,1)} %copy-done, bf16[176,384]{1,0:T(8,128)(2,1)} %copy-done.2, bf16[352,384]{1,0:T(8,128)(2,1)} %copy-done.3, bf16[704,384]{1,0:T(8,128)(2,1)} %copy-done.5), custom_call_target="tpu_custom_call" | custom-call | tf_op jit(solution)/shard_map/close/pallas_call | solution.py:676
  240.6 0.7 slice.65
  241.3 0.6 reshape.133
  241.9 1.6 slice_reduce_fusion
  243.6 1.2 slice_bitcast_fusion
  244.8 2.3 fusion.8
  247.0 1.7 maximum_convert_fusion
  248.7 2.8 %slice_convert_fusion = f32[1536,384]{1,0:T(8,128)} fusion(bf16[3456,384]{1,0:T(8,128)(2,1)} %all-gather.5.cloned.1.call-done), kind=kLoop, calls=%fused_computation.1 | loop fusion | flops 589824 | bytes 3538944 | tf_op jit(solution)/shard_map/convert_element_type | solution.py:817
  (39 shorter events, 0.4 us)
Async XLA Ops:
  7.2 55.8 %all-gather.7.cloned.1.call-start = ((), (), s32[]{:S(2)}) async-start(), calls=%async_computation.1 | async-start | bytes 1658880 | tf_op jit(solution)/shard_map/all_gather | solution.py:771
  26.5 7.7 %copy-start.6 = (bf16[640,384]{1,0:T(8,128)(2,1)}, bf16[640,384]{1,0:T(8,128)(2,1)S(1)}, u32[]{:S(2)}) copy-start(bf16[640,384]{1,0:T(8,128)(2,1)S(1)} %all-gather) | copy-start | bytes 1474564
  26.5 7.7 %collective-permute-start = (bf16[4,160,384]{2,1,0:T(8,128)(2,1)S(1)}, bf16[4,160,384]{2,1,0:T(8,128)(2,1)S(1)}, u32[]{:S(2)}, u32[]{:S(2)}) collective-permute-start(bf16[4,160,384]{2,1,0:T(8,128)(2,1)S(1)} %bitcast.51), channel_id=1, source_target_pairs={{0,4},{4,0},{8,12},{12,8},{16,20},{20,16},{24,28},{28,24},{1,5},{5... | collective-permute-start | bytes 1474568 | tf_op jit(solution)/shard_map/ppermute | solution.py:707
  26.6 218.2 %all-gather.5.cloned.1.call-start = ((), (), s32[]{:S(2)}) async-start(), calls=%async_computation | async-start | bytes 2985984 | tf_op jit(solution)/shard_map/all_gather | solution.py:808
  34.2 0.8 copy-start.9
  35.0 28.5 %copy-start.7 = (f32[1536]{0:T(1024)S(1)}, f32[1536]{0:T(1024)}, u32[]{:S(2)}) copy-start(f32[1536]{0:T(1024)} %param.38) | copy-start | bytes 18436
  63.0 3.4 %collective-permute-start.1 = (bf16[4,432,384]{2,1,0:T(8,128)(2,1)}, bf16[4,432,384]{2,1,0:T(8,128)(2,1)S(1)}, u32[]{:S(2)}, u32[]{:S(2)}) collective-permute-start(bf16[4,432,384]{2,1,0:T(8,128)(2,1)} %bitcast.56), channel_id=1, source_target_pairs={{0,4},{4,0},{8,12},{12,8},{16,20},{20,16},{24,28},{28,24},{1,5},{5... | collective-permute-start | bytes 3981320 | tf_op jit(solution)/shard_map/ppermute | solution.py:707
  66.4 1.1 copy-start.8
  119.1 13.3 %collective-permute-start.2 = (bf16[1728,384]{1,0:T(8,128)(2,1)}, bf16[1728,384]{1,0:T(8,128)(2,1)S(1)}, u32[]{:S(2)}, u32[]{:S(2)}) collective-permute-start(bf16[1728,384]{1,0:T(8,128)(2,1)} %get-tuple-element.86), channel_id=1, source_target_pairs={{0,4},{4,0},{8,12},{12,8},{16,20},{20,16},{24,28},{28,24},{1,5},{5... | collective-permute-start | bytes 3981320 | tf_op jit(solution)/shard_map/ppermute | solution.py:707
  119.6 12.9 %copy-start.1 = (bf16[1728,384]{1,0:T(8,128)(2,1)S(1)}, bf16[1728,384]{1,0:T(8,128)(2,1)}, u32[]{:S(2)}) copy-start(bf16[1728,384]{1,0:T(8,128)(2,1)} %get-tuple-element.84) | copy-start | bytes 3981316
  133.6 17.2 %collective-permute-start.3 = (bf16[864,384]{1,0:T(8,128)(2,1)}, bf16[864,384]{1,0:T(8,128)(2,1)S(1)}, u32[]{:S(2)}, u32[]{:S(2)}) collective-permute-start(bf16[864,384]{1,0:T(8,128)(2,1)} %fusion), channel_id=1, source_target_pairs={{0,8},{4,12},{8,0},{12,4},{16,24},{20,28},{24,16},{28,20},{1,9},{5... | collective-permute-start | bytes 1990664 | tf_op jit(solution)/shard_map/ppermute | solution.py:707
  150.9 15.2 %collective-permute-start.4 = (bf16[432,384]{1,0:T(8,128)(2,1)S(1)}, bf16[432,384]{1,0:T(8,128)(2,1)S(1)}, u32[]{:S(2)}, u32[]{:S(2)}) collective-permute-start(bf16[432,384]{1,0:T(8,128)(2,1)S(1)} %fusion.2), channel_id=1, source_target_pairs={{0,16},{4,20},{8,24},{12,28},{16,0},{20,4},{24,8},{28,12},{1,17},{... | collective-permute-start | bytes 995336 | tf_op jit(solution)/shard_map/ppermute | solution.py:707
  166.3 15.6 %collective-permute-start.5 = (bf16[432,384]{1,0:T(8,128)(2,1)S(1)}, bf16[432,384]{1,0:T(8,128)(2,1)S(1)}, u32[]{:S(2)}, u32[]{:S(2)}) collective-permute-start(bf16[432,384]{1,0:T(8,128)(2,1)S(1)} %fusion.1), channel_id=1, source_target_pairs={{0,1},{1,0},{2,3},{3,2},{4,5},{5,4},{6,7},{7,6},{8,9},{9,8},{10,11... | collective-permute-start | bytes 995336 | tf_op jit(solution)/shard_map/ppermute | solution.py:729
  181.9 2.8 %collective-permute-start.7 = (bf16[704,384]{1,0:T(8,128)(2,1)}, bf16[704,384]{1,0:T(8,128)(2,1)S(1)}, u32[]{:S(2)}, u32[]{:S(2)}) collective-permute-start(bf16[704,384]{1,0:T(8,128)(2,1)} %get-tuple-element.125), channel_id=1, source_target_pairs={{0,4},{4,0},{8,12},{12,8},{16,20},{20,16},{24,28},{28,24},{1,5},{5... | collective-permute-start | bytes 1622024 | tf_op jit(solution)/shard_map/ppermute | solution.py:707
  182.1 19.1 %collective-permute-start.6 = (bf16[432,384]{1,0:T(8,128)(2,1)S(1)}, bf16[432,384]{1,0:T(8,128)(2,1)S(1)}, u32[]{:S(2)}, u32[]{:S(2)}) collective-permute-start(bf16[432,384]{1,0:T(8,128)(2,1)S(1)} %add_convert_fusion.2), channel_id=1, source_target_pairs={{0,2},{1,3},{2,0},{3,1},{4,6},{5,7},{6,4},{7,5},{8,10},{9,11},{10,... | collective-permute-start | bytes 995336 | tf_op jit(solution)/shard_map/ppermute | solution.py:729
  185.7 16.2 %collective-permute-start.8 = (bf16[352,384]{1,0:T(8,128)(2,1)S(1)}, bf16[352,384]{1,0:T(8,128)(2,1)S(1)}, u32[]{:S(2)}, u32[]{:S(2)}) collective-permute-start(bf16[352,384]{1,0:T(8,128)(2,1)S(1)} %fusion.3), channel_id=1, source_target_pairs={{0,8},{4,12},{8,0},{12,4},{16,24},{20,28},{24,16},{28,20},{1,9},{5... | collective-permute-start | bytes 811016 | tf_op jit(solution)/shard_map/ppermute | solution.py:707
  187.3 14.7 %copy-start.4 = (bf16[704,384]{1,0:T(8,128)(2,1)S(1)}, bf16[704,384]{1,0:T(8,128)(2,1)}, u32[]{:S(2)}) copy-start(bf16[704,384]{1,0:T(8,128)(2,1)} %get-tuple-element.124) | copy-start | bytes 1622020
  202.2 5.5 %collective-permute-start.9 = (bf16[176,384]{1,0:T(8,128)(2,1)S(1)}, bf16[176,384]{1,0:T(8,128)(2,1)S(1)}, u32[]{:S(2)}, u32[]{:S(2)}) collective-permute-start(bf16[176,384]{1,0:T(8,128)(2,1)S(1)} %fusion.5), channel_id=1, source_target_pairs={{0,16},{4,20},{8,24},{12,28},{16,0},{20,4},{24,8},{28,12},{1,17},{... | collective-permute-start | bytes 405512 | tf_op jit(solution)/shard_map/ppermute | solution.py:707
  207.7 5.1 %collective-permute-start.10 = (bf16[176,384]{1,0:T(8,128)(2,1)S(1)}, bf16[176,384]{1,0:T(8,128)(2,1)S(1)}, u32[]{:S(2)}, u32[]{:S(2)}) collective-permute-start(bf16[176,384]{1,0:T(8,128)(2,1)S(1)} %fusion.4), channel_id=1, source_target_pairs={{0,1},{1,0},{2,3},{3,2},{4,5},{5,4},{6,7},{7,6},{8,9},{9,8},{10,11... | collective-permute-start | bytes 405512 | tf_op jit(solution)/shard_map/ppermute | solution.py:729
  212.9 7.1 %collective-permute-start.11 = (bf16[176,384]{1,0:T(8,128)(2,1)S(1)}, bf16[176,384]{1,0:T(8,128)(2,1)S(1)}, u32[]{:S(2)}, u32[]{:S(2)}) collective-permute-start(bf16[176,384]{1,0:T(8,128)(2,1)S(1)} %add_convert_fusion.6), channel_id=1, source_target_pairs={{0,2},{1,3},{2,0},{3,1},{4,6},{5,7},{6,4},{7,5},{8,10},{9,11},{10,... | collective-permute-start | bytes 405512 | tf_op jit(solution)/shard_map/ppermute | solution.py:729
  220.0 17.1 %copy-start = (bf16[176,384]{1,0:T(8,128)(2,1)}, bf16[176,384]{1,0:T(8,128)(2,1)S(1)}, u32[]{:S(2)}) copy-start(bf16[176,384]{1,0:T(8,128)(2,1)S(1)} %add_convert_fusion.5.refs_0_) | copy-start | bytes 405508
  220.0 8.5 %collective-permute-start.12 = (bf16[176,384]{1,0:T(8,128)(2,1)S(1)}, bf16[176,384]{1,0:T(8,128)(2,1)S(1)}, u32[]{:S(2)}, u32[]{:S(2)}) collective-permute-start(bf16[176,384]{1,0:T(8,128)(2,1)S(1)} %add_convert_fusion.5.refs_0_), channel_id=1, source_target_pairs={{0,16},{4,20},{8,24},{12,28},{16,0},{20,4},{24,8},{28,12},{1,17},{... | collective-permute-start | bytes 405512 | tf_op jit(solution)/shard_map/ppermute | solution.py:707
  228.5 8.6 %copy-start.2 = (bf16[176,384]{1,0:T(8,128)(2,1)}, bf16[176,384]{1,0:T(8,128)(2,1)S(1)}, u32[]{:S(2)}) copy-start(bf16[176,384]{1,0:T(8,128)(2,1)S(1)} %collective-permute-done.12.refs_1_) | copy-start | bytes 405508
  228.5 6.5 %collective-permute-start.13 = (bf16[352,384]{1,0:T(8,128)(2,1)S(1)}, bf16[352,384]{1,0:T(8,128)(2,1)S(1)}, u32[]{:S(2)}, u32[]{:S(2)}) collective-permute-start(bf16[352,384]{1,0:T(8,128)(2,1)S(1)} %pad_maximum_fusion.1), channel_id=1, source_target_pairs={{0,8},{4,12},{8,0},{12,4},{16,24},{20,28},{24,16},{28,20},{1,9},{5... | collective-permute-start | bytes 811016 | tf_op jit(solution)/shard_map/ppermute | solution.py:707
  235.0 2.1 copy-start.3
  235.1 2.0 collective-permute-start.14
  237.1 0.8 copy-start.5
Sparse Core Ops, SparseCore 0:
  26.7 34.8 all-gather.6
  202.1 30.8 all-gather.4

commit v2 on v1

--- a/solution.py
+++ b/solution.py
@@ -18,7 +18,8 @@
 WIN = 80
 KEYS = 128
 PAIRS = HEADS // 2
-GROUP = 12
+GROUP = 8
+SUBS = 2
 VMEM = 60 * 2**20
 LOG2E = 1.4426950408889634
 ROOT_HALF = 0.7071067811865476
@@ -100,7 +101,10 @@
     return jnp.where(rows == lanes, value, 0.0).astype(bf16)
 
 
-def pack_kernel(spot, proj, joint, out, up, down, half_early, half_late, early, late):
+def pack_kernel(spot, proj, joint, out, up, down, *refs):
+    vectors, (packed, vec, early, late) = refs[:8], refs[8:]
+    for at, vector in enumerate(vectors):
+        vec[at : at + 1, :] = vector[...].reshape(1, D)
     rows = joint.shape[0]
     for part in range(3):
         early[part * rows : part * rows + rows, :] = joint[:, part * D : part * D + D]
@@ -109,29 +113,34 @@
     for part in range(4):
         late[(part + 1) * rows : (part + 2) * rows, :] = up[:, part * D : part * D + D]
     late[5 * rows : 5 * rows + down.shape[0], :] = down[...]
-    for source, target in ((early, half_early), (late, half_late)):
-        half = target.shape[0]
-        target[...] = source[pl.ds(pl.multiple_of(spot[0] * half, 16), half), :]
-
-
-def pack(core, proj, joint, out, up, down):
+    half = early.shape[0] // 2
+    piece = packed.shape[0] - half
+    packed[:half, :] = early[pl.ds(pl.multiple_of((spot[0] % 2) * half, 16), half), :]
+    chips = late.shape[0] // piece // 2
+    own = (spot[0] % 2) * chips + spot[0] // 2
+    packed[half:, :] = late[pl.ds(pl.multiple_of(own * piece, 16), piece), :]
+
+
+def pack(spot, proj, joint, out, up, down, vectors, parts):
     rows, low, deep = joint.shape[0], proj.shape[0], down.shape[0]
-    sizes = (3 * rows + low, 5 * rows + deep)
+    size = 3 * rows + low
+    late = padded(5 * rows + deep, parts)
     vmem = pl.BlockSpec(memory_space=pltpu.VMEM)
     return pl.pallas_call(
         pack_kernel,
-        in_specs=[pl.BlockSpec(memory_space=pltpu.SMEM)] + [vmem] * 5,
+        in_specs=[pl.BlockSpec(memory_space=pltpu.SMEM)] + [vmem] * 13,
         out_specs=[vmem, vmem],
-        out_shape=[shape_of((size // 2, D), bf16) for size in sizes],
-        scratch_shapes=[pltpu.VMEM((size, D), bf16) for size in sizes],
+        out_shape=[shape_of((size // 2 + late // parts, D), bf16), shape_of((8, D), f32)],
+        scratch_shapes=[pltpu.VMEM((size, D), bf16), pltpu.VMEM((late, D), bf16)],
         compiler_params=settings(),
         name="pack",
-    )(core, proj, joint, out, up, down)
+    )(spot, proj, joint, out, up, down, *vectors)
 
 
 def unpack_early(core, mine, other, joint_w, proj):
-    groups, half, _ = mine.shape
+    groups = mine.shape[0]
     rows, low = D // groups, POSH // groups
+    half = (3 * rows + low) // 2
 
     def place(side, source):
         for group in range(groups):
@@ -160,39 +169,38 @@
         place(1, mine)
 
 
-def unpack_late(core, mine, other, out_w, up_w, down_w):
-    groups, half, _ = mine.shape
+def unpack_late(spot, mine, other, near, near_other, lates, out_w, up_w, down_w):
+    _, chips, groups, piece, _ = lates.shape
     rows, deep = D // groups, FF // groups
-
-    def place(side, source):
+    half = mine.shape[1] - piece
+    core, chip = spot % 2, spot // 2
+    for side, own, rest in ((core, mine, near), (1 - core, other, near_other)):
+        lates[side, chip] = own[:, half:, :]
+        for offset, source in enumerate(rest):
+            lates[side, chip ^ (offset + 1)] = source[...]
+    for at_chip in range(2 * chips):
         for group in range(groups):
             at = 0
-            while at < half:
-                row = side * half + at
+            while at < piece:
+                row = at_chip * piece + at
+                source = lates.at[at_chip // chips, at_chip % chips, group]
                 if row < rows:
-                    size = min(half - at, rows - row)
+                    size = min(piece - at, rows - row)
                     first = group * rows + row
-                    out_w[first : first + size, :] = source[group, at : at + size]
+                    out_w[first : first + size, :] = source[at : at + size, :]
                 elif row < 5 * rows:
                     block, inner = divmod(row - rows, rows)
-                    size = min(half - at, rows - inner)
+                    size = min(piece - at, rows - inner)
                     first = group * rows + inner
-                    up_w[first : first + size, block * D : block * D + D] = source[group, at : at + size]
+                    up_w[first : first + size, block * D : block * D + D] = source[at : at + size, :]
+                elif row < 5 * rows + deep:
+                    inner = row - 5 * rows
+                    size = min(piece - at, deep - inner)
+                    first = group * deep + inner
+                    down_w[first : first + size, :] = source[at : at + size, :]
                 else:
-                    size = half - at
-                    first = group * deep + row - 5 * rows
-                    down_w[first : first + size, :] = source[group, at : at + size]
+                    size = piece - at
                 at += size
-
-    @pl.when(core == 0)
-    def _():
-        place(0, mine)
-        place(1, other)
-
-    @pl.when(core == 1)
-    def _():
-        place(0, other)
-        place(1, mine)
 
 
 def picked(rows, first, source):
@@ -223,75 +231,104 @@
 
     @pl.when(step == 0)
     def _():
-        qkv[ROWS:, :] = jnp.zeros((qkv.shape[0] - ROWS, 3 * D), bf16)
+        for sub in range(SUBS):
+            qkv[sub, ROWS:, :] = jnp.zeros((qkv.shape[1] - ROWS, 3 * D), bf16)
         unpack_early(core[0], mine, other, joint_w, proj)
         place_inputs(centers, place_weight, place_bias, cen, place_w)
 
-    pre = dot(cen[step], place_w[...], TN)
-    low = (pre * cdf(pre)).astype(bf16)
-    placed = dot(low, proj[...]) + vec[1:2, :]
-    hidden = hidden_column(targets[0], ROWS)
-    rows = jnp.where(hidden > 0.5, vec[0:1, :], tokens[...].astype(f32)) + placed
-    entry[...] = rows
-    unit, _ = normalised(rows)
-    normed = (unit * vec[2:3, :] + vec[3:4, :]).astype(bf16)
-    for part in range(9):
-        cols = slice(part * 128, part * 128 + 128)
-        value = dot(normed, joint_w[:, cols])
-        if part < 3:
-            value = value * (0.125 * LOG2E)
-        value = value.astype(bf16)
-        qkv[:ROWS, cols] = value
-        joint[:, cols] = value
-    jobs = [(pair, cloud) for pair in range(PAIRS) for cloud in range(TILE)]
-    tails = {}
     lanes = lax.broadcasted_iota(jnp.int32, (1, 2 * KEYS), 1) % KEYS
     sums_of = head_ones(1.0)
-    for at in range(0, len(jobs), GROUP):
-        group = jobs[at : at + GROUP]
-        scores = []
-        for pair, cloud in group:
-            base = cloud * STEP
-            query = qkv[base : base + WIN, pair * 128 : pair * 128 + 128]
-            key = qkv[base : base + KEYS, D + pair * 128 : D + pair * 128 + 128]
-            scores.append(dot(query, spread_heads(key.T)))
-        exps = []
-        for (pair, cloud), score in zip(group, scores):
-            live = (lanes >= 2 * cloud) & (lanes < 2 * cloud + SEQ - 1)
-            score = jnp.where(live, score, -1e30)
-            parts = []
-            for half in (score[:, :KEYS], score[:, KEYS:]):
-                parts.append(jnp.exp2(half - jnp.max(half, axis=-1, keepdims=True)).astype(bf16))
-            exps.append(jnp.concatenate(parts, axis=1))
-        boths = []
-        for (pair, cloud), e in zip(group, exps):
-            base = cloud * STEP
-            value = qkv[base : base + KEYS, 2 * D + pair * 128 : 2 * D + pair * 128 + 128]
-            boths.append(dot(e, jnp.concatenate([stacked_heads(value), sums_of], axis=1)))
-        for (pair, cloud), e, both in zip(group, exps, boths):
-            base = cloud * STEP
-            cols = slice(pair * 128, pair * 128 + 128)
-            share = 1.0 / both[:, 128:]
-            mix = both[:, :128] * share
-            spot = slice(pair * 256, pair * 256 + 256)
-            none = jnp.zeros((16, 2 * KEYS), bf16)
-            weights[cloud, :16, spot] = jnp.where(row_range(16, 2 * cloud, 16, 256), e[:16], none)
-            weights[cloud, 16:64, spot] = e[16:64]
-            weights[cloud, 64:80, spot] = jnp.where(row_range(16, 0, 2 * cloud + 2, 256), e[64:80], none)
-            head_mix, head_share = mix[:16], share[:16]
-            if cloud:
-                head = row_range(16, 0, 2 * cloud)
-                tail_mix, tail_share = tails[pair]
-                head_mix = jnp.where(head, tail_mix, head_mix)
-                head_share = jnp.where(head, tail_share, head_share)
-            mixture[base : base + 16, cols] = head_mix.astype(bf16)
-            shares[base : base + 16, cols] = head_share.astype(bf16)
-            mixture[base + 16 : base + 64, cols] = mix[16:64].astype(bf16)
-            shares[base + 16 : base + 64, cols] = share[16:64].astype(bf16)
-            tails[pair] = (mix[64:], share[64:])
-            if cloud == TILE - 1:
-                mixture[ROWS - 16 :, cols] = mix[64:].astype(bf16)
-                shares[ROWS - 16 :, cols] = share[64:].astype(bf16)
+    none = jnp.zeros((16, 2 * KEYS), bf16)
+    scale_row = jnp.where(lax.broadcasted_iota(jnp.int32, (1, 3 * D), 1) < D, 0.125 * LOG2E, 1.0)
+
+    def normal_rows(sub):
+        span = slice(sub * ROWS, sub * ROWS + ROWS)
+        pre = dot(cen[step * SUBS + sub], place_w[...], TN)
+        low = (pre * cdf(pre)).astype(bf16)
+        placed = dot(low, proj[...]) + vec[1:2, :]
+        hidden = hidden_column(targets[sub], ROWS)
+        rows = jnp.where(hidden > 0.5, vec[0:1, :], tokens[span, :].astype(f32)) + placed
+        entry[span, :] = rows
+        unit, _ = normalised(rows)
+        return (unit * vec[2:3, :] + vec[3:4, :]).astype(bf16)
+
+    def project(sub, normed, first):
+        cols = slice(first, min(first + 256, 3 * D))
+        value = (dot(normed, joint_w[:, cols]) * scale_row[:, cols]).astype(bf16)
+        qkv[sub, :ROWS, cols] = value
+        joint[sub * ROWS : sub * ROWS + ROWS, cols] = value
+
+    def score(sub, pair, cloud):
+        base = cloud * STEP
+        query = qkv[sub, base : base + WIN, pair * 128 : pair * 128 + 128]
+        key = qkv[sub, base : base + KEYS, D + pair * 128 : D + pair * 128 + 128]
+        return dot(query, spread_heads(key.T))
+
+    def exponentials(cloud, scores):
+        live = (lanes >= 2 * cloud) & (lanes < 2 * cloud + SEQ - 1)
+        scores = jnp.where(live, scores, -1e30)
+        parts = []
+        for half in (scores[:, :KEYS], scores[:, KEYS:]):
+            parts.append(jnp.exp2(half - jnp.max(half, axis=-1, keepdims=True)).astype(bf16))
+        return jnp.concatenate(parts, axis=1)
+
+    def mixed(sub, pair, cloud, e):
+        base = cloud * STEP
+        value = qkv[sub, base : base + KEYS, 2 * D + pair * 128 : 2 * D + pair * 128 + 128]
+        return dot(e, jnp.concatenate([stacked_heads(value), sums_of], axis=1))
+
+    tails = {}
+
+    def store(sub, pair, cloud, e, both):
+        base = sub * ROWS + cloud * STEP
+        cols = slice(pair * 128, pair * 128 + 128)
+        share = 1.0 / both[:, 128:]
+        mix = both[:, :128] * share
+        spot = slice(pair * 256, pair * 256 + 256)
+        at = sub * TILE + cloud
+        weights[at, :16, spot] = jnp.where(row_range(16, 2 * cloud, 16, 256), e[:16], none)
+        weights[at, 16:64, spot] = e[16:64]
+        weights[at, 64:80, spot] = jnp.where(row_range(16, 0, 2 * cloud + 2, 256), e[64:80], none)
+        head_mix, head_share = mix[:16], share[:16]
+        if cloud:
+            head = row_range(16, 0, 2 * cloud)
+            tail_mix, tail_share = tails[sub, pair]
+            head_mix = jnp.where(head, tail_mix, head_mix)
+            head_share = jnp.where(head, tail_share, head_share)
+        mixture[base : base + 16, cols] = head_mix.astype(bf16)
+        shares[base : base + 16, cols] = head_share.astype(bf16)
+        mixture[base + 16 : base + 64, cols] = mix[16:64].astype(bf16)
+        shares[base + 16 : base + 64, cols] = share[16:64].astype(bf16)
+        tails[sub, pair] = (mix[64:], share[64:])
+        if cloud == TILE - 1:
+            mixture[base + 64 : base + 80, cols] = mix[64:].astype(bf16)
+            shares[base + 64 : base + 80, cols] = share[64:].astype(bf16)
+
+    jobs = [(pair, cloud) for pair in range(PAIRS) for cloud in range(TILE)]
+    groups = [jobs[at : at + GROUP] for at in range(0, len(jobs), GROUP)]
+    normed = [normal_rows(sub) for sub in range(SUBS)]
+    chunks = range(0, 3 * D, 256)
+    for first in chunks:
+        project(0, normed[0], first)
+    waiting = None
+    for sub in range(SUBS):
+        fill = [functools.partial(project, sub + 1, normed[sub + 1], first) for first in chunks] if sub + 1 < SUBS else []
+        share_of = -(-len(fill) // len(groups))
+        for group in groups:
+            exps = [exponentials(cloud, score(sub, pair, cloud)) for pair, cloud in group]
+            for task in fill[:share_of]:
+                task()
+            fill = fill[share_of:]
+            if waiting:
+                close_group(mixed, store, *waiting)
+            waiting = (sub, group, exps)
+    close_group(mixed, store, *waiting)
+
+
+def close_group(mixed, store, sub, group, exps):
+    boths = [mixed(sub, pair, cloud, e) for (pair, cloud), e in zip(group, exps)]
+    for (pair, cloud), e, both in zip(group, exps, boths):
+        store(sub, pair, cloud, e, both)
 
 
 def whole(shape):
@@ -321,16 +358,18 @@
 def front(core, tokens, centers, targets, vec, place_weight, place_bias, mine, other):
     count = tokens.shape[0]
     steps = count // ROWS
+    rows = SUBS * ROWS
     return pl.pallas_call(
         front_kernel,
-        grid=(steps,),
+        grid=(steps // SUBS,),
         in_specs=[
-            pl.BlockSpec(memory_space=pltpu.SMEM), rows_of(D), whole(centers.shape), slab((1, 256)), whole((8, D)),
+            pl.BlockSpec(memory_space=pltpu.SMEM), rows_of(D, rows), whole(centers.shape),
+            pl.BlockSpec((SUBS, 1, 256), lambda i: (i, 0, 0)), whole((8, D)),
             whole((3, POSH)), whole((1, POSH)), whole(mine.shape), whole(other.shape),
         ],
         out_specs=[
-            rows_of(D), rows_of(3 * D), rows_of(D), rows_of(D),
-            pl.BlockSpec((TILE, WIN, HEADS * KEYS), lambda i: (i, 0, 0)), whole((D, 3 * D)), whole((POSH, D)),
+            rows_of(D, rows), rows_of(3 * D, rows), rows_of(D, rows), rows_of(D, rows),
+            pl.BlockSpec((SUBS * TILE, WIN, HEADS * KEYS), lambda i: (i, 0, 0)), whole((D, 3 * D)), whole((POSH, D)),
             whole((steps, 16, ROWS)), whole((16, POSH)),
         ],
         out_shape=[
@@ -339,7 +378,7 @@
             shape_of((steps * TILE, WIN, HEADS * KEYS), bf16), shape_of((D, 3 * D), bf16), shape_of((POSH, D), bf16),
             shape_of((steps, 16, ROWS), bf16), shape_of((16, POSH), bf16),
         ],
-        scratch_shapes=[pltpu.VMEM((ROWS + 48, 3 * D), bf16)],
+        scratch_shapes=[pltpu.VMEM((SUBS, ROWS + 48, 3 * D), bf16)],
         compiler_params=settings(),
         cost_estimate=cost(28),
         name="front",
@@ -368,14 +407,16 @@
     return -(-rows // (16 * size)) * 16 * size
 
 
-def middle_kernel(chunk, order, core, entry, mixture, shares, cot, vec, up_b, mine, other,
-                  middle, gated, mid_grad, mix_grad, kept, sent, up_bg, vec_g, down_w,
-                  down_acc, up_acc, out_acc, out_w, up_w, sums):
+def middle_kernel(chunk, order, spot, entry, mixture, shares, cot, vec, up_b, mine, other, *refs):
+    chips = len(order) // 2
+    near, near_other, refs = refs[: chips - 1], refs[chips - 1 : 2 * chips - 2], refs[2 * chips - 2 :]
+    (output, mid_grad, mix_grad, kept, sent, up_bg, vec_g,
+     down_acc, up_acc, out_acc, out_w, up_w, down_w, gated, sums, lates) = refs
     step = pl.program_id(0)
 
     @pl.when(step == 0)
     def _():
-        unpack_late(core[0], mine, other, out_w, up_w, down_w)
+        unpack_late(spot[0], mine, other, near, near_other, lates, out_w, up_w, down_w)
         for ref in (down_acc, up_acc, out_acc, up_bg, vec_g):
             ref[...] = jnp.zeros(ref.shape, ref.dtype)
 
@@ -385,7 +426,6 @@
     cotangent = cot[...]
     mid = entry[...] + (dot(mix, out_w[...]) + vec[4:5, :])
     gates = [dot(cotangent, down_w[spans[0], :], NT)]
-    middle[...] = mid
     unit, scale = normalised(mid)
     normed = (unit * vec[5:6, :] + vec[6:7, :]).astype(bf16)
     lows = []
@@ -414,6 +454,7 @@
     up_part(parts - 2)
     down_part(parts - 1)
     up_part(parts - 1)
+    output[...] = (mid + (dot(gated[...], down_w[...]) + vec[7:8, :])).astype(bf16)
     upstream = cotangent.astype(f32)
     tilted = back * vec[5:6, :]
     grad = upstream + scale * (tilted - row_mean(tilted) - unit * row_mean(tilted * unit))
@@ -434,10 +475,10 @@
         write_sums(sums, order, 8 * D, out_acc[...])
         if sums.shape[0] > 9 * D:
             write_sums(sums, order, 9 * D, jnp.zeros((sums.shape[0] - 9 * D, D), f32))
-        share_halves(core[0], sums, kept, sent)
-
-
-def middle_part(core, entry, mixture, shares, cot, vec, up_b, mine, other, order, rows=1056, chunk=512):
+        share_halves(spot[0] % 2, sums, kept, sent)
+
+
+def middle_part(spot, entry, mixture, shares, cot, vec, up_b, mine, other, near, near_other, order, rows=1056, chunk=512):
     count = entry.shape[0]
     size = padded(9 * D, len(order))
     return pl.pallas_call(
@@ -446,24 +487,26 @@
         in_specs=[
             pl.BlockSpec(memory_space=pltpu.SMEM), rows_of(D, rows), rows_of(D, rows), rows_of(D, rows), rows_of(D, rows),
             whole((8, D)), whole((1, FF)), whole(mine.shape), whole(other.shape),
-        ],
+        ]
+        + [whole(piece.shape) for piece in [*near, *near_other]],
         out_specs=[
-            rows_of(D, rows), rows_of(FF, rows), rows_of(D, rows), rows_of(D, rows),
-            whole((size // 2, D)), whole((size // 2, D)), whole((1, FF)), whole((8, D)), whole((FF, D)),
+            rows_of(D, rows), rows_of(D, rows), rows_of(D, rows),
+            whole((size // 2, D)), whole((size // 2, D)), whole((1, FF)), whole((8, D)),
         ],
         out_shape=[
-            shape_of((count, D), f32), shape_of((count, FF), bf16), shape_of((count, D), f32), shape_of((count, D), bf16),
-            shape_of((size // 2, D), bf16), shape_of((size // 2, D), bf16),
-            shape_of((1, FF), f32), shape_of((8, D), f32), shape_of((FF, D), bf16),
+            shape_of((count, D), bf16), shape_of((count, D), f32), shape_of((count, D), bf16),
+            shape_of((size // 2, D), bf16), shape_of((size // 2, D), bf16), shape_of((1, FF), f32), shape_of((8, D), f32),
         ],
         scratch_shapes=[
             pltpu.VMEM((D, FF), f32), pltpu.VMEM((D, FF), f32), pltpu.VMEM((D, D), f32),
-            pltpu.VMEM((D, D), bf16), pltpu.VMEM((D, FF), bf16), pltpu.VMEM((size, D), bf16),
+            pltpu.VMEM((D, D), bf16), pltpu.VMEM((D, FF), bf16), pltpu.VMEM((FF, D), bf16),
+            pltpu.VMEM((rows, FF), bf16), pltpu.VMEM((size, D), bf16),
+            pltpu.VMEM((2, len(order) // 2, *near[0].shape), bf16),
         ],
         compiler_params=settings(),
         cost_estimate=cost(55),
         name="middle",
-    )(core, entry, mixture, shares, cot, vec, up_b, mine, other)
+    )(spot, entry, mixture, shares, cot, vec, up_b, mine, other, *near, *near_other)
 
 
 def back_kernel(is_first, is_last, order, *refs):
@@ -531,9 +574,7 @@
 
 
     back = dot(dqkv[...], joint_w[...], NT)
-    for part in range(3):
-        cols = slice(part * D, part * D + D)
-        joint_g[:, cols] += dot(normed, dqkv[:, cols], TN)
+    joint_g[...] += dot(normed, dqkv[...], TN)
     tilted = back * vec[2:3, :]
     grad = mid_grad[...] + scale * (tilted - row_mean(tilted) - unit * row_mean(tilted * unit))
     low = grad.astype(bf16)
@@ -622,24 +663,6 @@
     )(*given)
 
 
-def finish_kernel(middle, gated, vec, down_w, output):
-    output[...] = (middle[...] + (dot(gated[...], down_w[...]) + vec[7:8, :])).astype(bf16)
-
-
-def finish(middle, gated, vec, down_w, rows=528):
-    count = middle.shape[0]
-    return pl.pallas_call(
-        finish_kernel,
-        grid=(count // rows,),
-        in_specs=[rows_of(D, rows), rows_of(FF, rows), whole((8, D)), whole((FF, D))],
-        out_specs=rows_of(D, rows),
-        out_shape=shape_of((count, D), bf16),
-        compiler_params=settings(),
-        cost_estimate=cost(12),
-        name="finish",
-    )(middle, gated, vec, down_w)
-
-
 def marked_targets(mask_count, mask_index):
     clouds, most = mask_index.shape
     slot = jnp.arange(most, dtype=jnp.int32)[None, :]
@@ -648,80 +671,99 @@
     return jnp.pad(targets, ((0, 0), (0, 32 - most)), constant_values=-1).reshape(clouds // TILE, 1, 256)
 
 
-def joined_offsets(size):
-    held, groups = [0], [[0]]
-    bit = size // 2
-    while bit:
-        groups.append([offset ^ bit for offset in held])
-        held = held + groups[-1]
-        bit //= 2
-    return groups
-
-
-def close_kernel(groups, spot, *refs):
-    pieces, (joint_g, proj_g, small, sums) = refs[:-4], refs[-4:]
+def gather_pieces(spot, offsets, pieces, sums):
     segment = pieces[0].shape[0]
-    for piece, offsets in zip(pieces, groups):
-        for at, offset in enumerate(offsets):
-            row = pl.multiple_of((spot[0] ^ offset) * segment, 16)
-            sums[pl.ds(row, segment), :] = piece[at * segment : at * segment + segment, :]
+    chips = len(pieces) // 2
+    for offset, piece in zip(offsets, pieces):
+        holder = spot ^ offset
+        row = pl.multiple_of(((holder % 2) * chips + holder // 2) * segment, 16)
+        sums[pl.ds(row, segment), :] = piece[...]
+
+
+def close_kernel(offsets, spot, *refs):
+    pieces, refs = refs[: len(offsets)], refs[len(offsets) :]
+    joint_g, proj_g, place_g, small, sums = refs[0], refs[1], refs[2], refs[3:-1], refs[-1]
+    gather_pieces(spot[0], offsets, pieces, sums)
     for part in range(3):
         joint_g[:, part * D : part * D + D] = sums[part * D : part * D + D, :].astype(f32)
     proj_g[...] = sums[3 * D : 3 * D + POSH, :].astype(f32)
-    small[...] = sums[3 * D + POSH : 3 * D + POSH + 16, :].astype(f32)
-
-
-def close(spot, pieces, size):
+    rows = sums[3 * D + POSH : 3 * D + POSH + 16, :].astype(f32)
+    for part in range(3):
+        place_g[part : part + 1, :] = rows[8:9, part * POSH : part * POSH + POSH]
+    small[0][...] = rows[9:10, :POSH].reshape(POSH)
+    small[1][...] = jnp.concatenate([rows[10 + part : 11 + part] for part in range(4)], axis=1).reshape(FF)
+    for at in range(8):
+        small[2 + at][...] = rows[at : at + 1].reshape(D)
+
+
+def widen_kernel(offsets, spot, *refs):
+    pieces, refs = refs[: len(offsets)], refs[len(offsets) :]
+    up_g, down_g, out_g, sums = refs
+    gather_pieces(spot[0], offsets, pieces, sums)
+    for part in range(4):
+        up_g[:, part * D : part * D + D] = sums[part * D : part * D + D, :].astype(f32)
+    down_g[...] = sums[4 * D : 8 * D, :].astype(f32)
+    out_g[...] = sums[8 * D : 9 * D, :].astype(f32)
+
+
+def unpacked(kernel, name, shapes, spot, offsets, pieces):
     vmem = pl.BlockSpec(memory_space=pltpu.VMEM)
     return pl.pallas_call(
-        functools.partial(close_kernel, joined_offsets(size)),
+        functools.partial(kernel, offsets),
         in_specs=[pl.BlockSpec(memory_space=pltpu.SMEM)] + [vmem] * len(pieces),
-        out_specs=[vmem] * 3,
-        out_shape=[shape_of((D, 3 * D), f32), shape_of((POSH, D), f32), shape_of((16, D), f32)],
-        scratch_shapes=[pltpu.VMEM((pieces[0].shape[0] * size, D), bf16)],
+        out_specs=[vmem] * len(shapes),
+        out_shape=[shape_of(shape, f32) for shape in shapes],
+        scratch_shapes=[pltpu.VMEM((pieces[0].shape[0] * len(pieces), D), bf16)],
         compiler_params=settings(),
-        name="close",
+        cost_estimate=cost(4),
+        name=name,
     )(spot, *pieces)
 
 
-CALLS = 4
+CALLS = 1
 
 
 def bits_of(size):
     return [1 << bit for bit in range(size.bit_length() - 1)]
 
 
-def spot_of(index, size):
-    spot, span = 0, size
-    for bit in bits_of(size):
-        span //= 2
-        spot += span * ((index // bit) % 2)
-    return spot
-
-
-def segments(size):
-    return [spot_of(index, size) for index in range(size)]
-
-
-def swapped(values, bit, size):
-    return lax.ppermute(values, "dp", [(i, i ^ bit) for i in range(size)])
+def chip_bits(size):
+    bits = bits_of(size)[:0:-1]
+    return [bits[at : at + 2] for at in range(0, len(bits), 2)]
+
+
+def offsets_of(bits):
+    found = [0]
+    for bit in reversed(bits):
+        found += [offset + bit for offset in found]
+    return found
+
+
+def swapped(values, offset, size):
+    return lax.ppermute(values, "dp", [(i, i ^ offset) for i in range(size)])
 
 
 def total(terms):
     return sum(term.astype(f32) for term in terms).astype(bf16)
 
 
-def halves(terms, bit):
-    side = (lax.axis_index("dp") // bit) % 2
-    pairs = [term.reshape(2, term.shape[0] // 2, D) for term in terms]
-    sent = [lax.dynamic_index_in_dim(pair, 1 - side, 0, keepdims=False) for pair in pairs]
-    kept = [lax.dynamic_index_in_dim(pair, side, 0, keepdims=False) for pair in pairs]
-    return sent, kept
-
-
-def halved(terms, bit, size, ready=None):
-    sent, kept = halves(terms, bit)
-    return kept + [swapped(total(sent) if ready is None else ready, bit, size)]
+def scattered(terms, bits, size):
+    offsets = offsets_of(bits)
+    mine = (lax.axis_index("dp") // bits[-1]) % len(offsets)
+    parts = [term.reshape(len(offsets), -1, D) for term in terms]
+
+    def part(offset):
+        return [lax.dynamic_index_in_dim(term, mine ^ (offset // bits[-1]), 0, keepdims=False) for term in parts]
+
+    return part(0) + [swapped(total(part(offset)), offset, size) for offset in offsets[1:]]
+
+
+def joined(pieces, bits, size):
+    found = dict(pieces)
+    for offset in offsets_of(bits)[1:]:
+        for held, piece in pieces.items():
+            found[held ^ offset] = swapped(piece, offset, size)
+    return found
 
 
 def across(terms, bit, size):
@@ -731,10 +773,6 @@
 
 def tied(first, second):
     return lax.optimization_barrier((first, second))
-
-
-def wide(blocks):
-    return jnp.concatenate(blocks, axis=1).astype(f32)
 
 
 def per_device(
@@ -764,64 +802,74 @@
     dp, fsdp = sizes["dp"], sizes["fsdp"]
     spot = lax.axis_index("dp").astype(jnp.int32)[None]
     core = spot % 2
-    early, late = pack(core, place_proj, joint_weight, out_weight, up_weight, down_weight)
-    early = lax.all_gather(early, "fsdp", axis=0)
-    early_other = swapped(early, 1, dp)
-    late, early = tied(late, early)
-    late = lax.all_gather(late, "fsdp", axis=0)
+    vectors = (mask_embed, place_shift, norm_gain, norm_shift, out_bias, mlp_gain, mlp_shift, down_bias)
+    packed, vec = pack(spot, place_proj, joint_weight, out_weight, up_weight, down_weight, vectors, dp)
+    packed = lax.all_gather(packed, "fsdp", axis=0)
+    packed_other = swapped(packed, 1, dp)
+    half = (3 * joint_weight.shape[0] + place_proj.shape[0]) // 2
+    late = packed[:, half:]
+    near = [swapped(late, 2 * offset, dp) for offset in range(1, dp // 2)]
     targets = marked_targets(mask_count, mask_index)
-    vec = jnp.stack([mask_embed, place_shift, norm_gain, norm_shift, out_bias, mlp_gain, mlp_shift, down_bias])
     up_b = up_bias[None, :]
     entry, joint, mixture, shares, weights, joint_w, proj, cen, place_w = front(
-        core, tokens, centers, targets, vec, place_weight, place_bias[None, :], early, early_other
+        core, tokens, centers, targets, vec, place_weight, place_bias[None, :], packed, packed_other
     )
-    late_other = swapped(late, 1, dp)
-    late, mixture = tied(late, mixture)
-    late_other = swapped(late, 1, dp)
-    order = segments(dp)
-    middle, gated, mid_grad, mix_grad, kept, sent, up_bg, vec_g, down_w = middle_part(
-        core, entry, mixture, shares, cotangent, vec, up_b, late, late_other, order
+    near, mixture = tied(near, mixture)
+    near_other = [swapped(piece, 1, dp) for piece in near]
+    order = list(range(dp))
+    output, mid_grad, mix_grad, kept, sent, up_bg, vec_g = middle_part(
+        spot, entry, mixture, shares, cotangent, vec, up_b, packed, packed_other, near, near_other, order
     )
-    stages = [functools.partial(halved, bit=bit, size=dp) for bit in bits_of(dp)]
+    chips = chip_bits(dp)
+    stages = [functools.partial(scattered, bits=bits, size=dp) for bits in chips]
     stages += [functools.partial(across, bit=bit, size=fsdp) for bit in bits_of(fsdp)]
     steps = tokens.shape[0] // ROWS
     parts = [steps * (part + 1) // CALLS - steps * part // CALLS for part in range(CALLS)]
     before, first = None, 0
     sums = [kept, swapped(sent, 1, dp)]
     for part, count in enumerate(parts):
-        if part:
-            mix_grad, sums[-1] = tied(mix_grad, sums[-1])
-            sums = stages[part](sums)
+        mix_grad, sums[-1] = tied(mix_grad, sums[-1])
+        sums = stages[part](sums)
         given = (entry, joint, mixture, weights, mix_grad, mid_grad, cen, targets, vec, place_w, proj, joint_w)
         extra = [core, up_bg, vec_g] if part == CALLS - 1 else None
         before = back_part(given, first, count, order, before, extra)
         first += count
     tokens_grad, kept, sent = before
+    rest = stages[CALLS:]
     sent, sums[-1] = tied(sent, sums[-1])
-    for stage in stages[CALLS:]:
+    sums = rest[0](sums)
+    last = [kept, swapped(sent, 1, dp)]
+    sums[-1], last[-1] = tied(sums[-1], last[-1])
+    for at, stage in enumerate(rest[1:]):
         sums = stage(sums)
-    last = stages[1]([kept, swapped(sent, 1, dp)])
-    output = finish(middle, gated, vec, down_w)
-    sums[-1], output = tied(sums[-1], output)
-    sums = total(sums)
-    last[-1], sums = tied(last[-1], sums)
-    sums = lax.all_gather(sums, "dp", axis=0, tiled=True)
-    for stage in stages[2:]:
+        last = stages[at](last)
+        sums[-1], last[-1] = tied(sums[-1], last[-1])
+    sums = {0: total(sums)}
+    for bits in reversed(chips):
+        sums = joined(sums, bits, dp)
+    for stage in stages[len(rest) - 1 :]:
         last = stage(last)
-    pieces = [total(last)]
-    for bit in reversed(bits_of(dp)):
-        held = pieces[0] if len(pieces) == 1 else jnp.concatenate(pieces, axis=0)
-        pieces.append(swapped(held, bit, dp))
-    joint_grad, proj_grad, small = close(spot, pieces, dp)
-    up_grad = wide([sums[part * D : part * D + D] for part in range(4)])
-    down_grad = sums[4 * D : 8 * D].astype(f32)
-    out_grad = sums[8 * D : 9 * D].astype(f32)
+    last = {0: total(last)}
+    for bits in reversed(chips):
+        last = joined(last, bits, dp)
+    sums, last = joined(sums, [1], dp), joined(last, [1], dp)
+    up_grad, down_grad, out_grad = unpacked(
+        widen_kernel, "widen", [(D, FF), (FF, D), (D, D)], spot, list(sums), list(sums.values())
+    )
+    joint_grad, proj_grad, place_weight_grad, place_bias_grad, up_bias_grad, *small = unpacked(
+        close_kernel,
+        "close",
+        [(D, 3 * D), (POSH, D), (3, POSH), (POSH,), (FF,)] + [(D,)] * 8,
+        spot,
+        list(last),
+        list(last.values()),
+    )
     return (
         output,
         tokens_grad,
         small[0],
-        small[8].reshape(3, POSH),
-        small[9, :POSH],
+        place_weight_grad,
+        place_bias_grad,
         proj_grad,
         small[1],
         small[2],
@@ -832,7 +880,7 @@
         small[4],
         small[5],
         up_grad,
-        small[10:14].reshape(FF),
+        up_bias_grad,
         down_grad,
         small[7],
     )

time: 259 us -> 228 us (0.88)
  Pallas kernels: 151 us -> 124 us
  between operations: 14.3 us -> 1.02 us
  waiting for transfers between devices: 36 us -> 47.4 us
  starting transfers between devices: 13.9 us -> 22.9 us
  local copies, waits for them, and re-layouts: 14.5 us -> 5.79 us
  other arithmetic: 11.1 us -> 3.87 us
  blocking collectives: 17.2 us -> 22.1 us
    ppermute x4, waiting for transfers between devices: 10.1 us -> 29.1 us  [across(): lax.ppermute(value, 'fsdp', [(i, i ^ bit) for i in range(size)])]
    pallas_call x3, Pallas kernels: 44.5 us -> 27.3 us  [the longest x1 20.1 us: front(): pl.pallas_call(front_kernel, grid=(steps // SUBS,), in_specs=[pl.BlockSpe...]
    pallas_call x4 -> x1, Pallas kernels: 53.2 us -> 36.8 us  [back_part(): pl.pallas_call(functools.partial(back_kernel, before is None, extra is no...]
    ppermute x11 -> x29, starting transfers between devices: 6.95 us -> 21.5 us  [swapped(): return lax.ppermute(values, 'dp', [(i, i ^ offset) for i in range(size)])]
    ppermute x11 -> x29, waiting for transfers between devices: 25.9 us -> 18.3 us  [swapped(): return lax.ppermute(values, 'dp', [(i, i ^ offset) for i in range(size)])]
    pallas_call x1, Pallas kernels: 51.6 us -> 58 us  [middle_part(): pl.pallas_call(functools.partial(middle_kernel, chunk, order), grid=(coun...]
    another operation x9 -> x0, local copies, waits for them, and re-layouts: 6.11 us -> none  [per_device(): jnp.stack([mask_embed, place_shift, norm_gain, norm_shift, out_bias, mlp_...]
    ppermute x4, starting transfers between devices: 6.88 us -> 1.38 us  [across(): lax.ppermute(value, 'fsdp', [(i, i ^ bit) for i in range(size)])]
  transfers between devices with their start and end apart: 17 -> 33, of which waited for: 8 -> 13; matrix products, arithmetic and copies ran while one was open for 6% -> 2% of each run, Pallas kernels for 38% -> 26%
where the time goes in v2:
time: 228 us; the launch traced here: 227 us
  Pallas kernels  124 us (54%)
  waiting for transfers between devices  47.4 us (21%)
  starting transfers between devices  22.9 us (10%)
  blocking collectives  22.1 us (10%)
  local copies, waits for them, and re-layouts  5.79 us (3%)
  other arithmetic  3.87 us (2%)
    pallas_call x1, Pallas kernels, middle_part(): pl.pallas_call(functools.partial(middle_kernel, chunk, order), grid=(coun...  58 us
    pallas_call x1, Pallas kernels, back_part(): pl.pallas_call(functools.partial(back_kernel, before is None, extra is no...  36.8 us
    ppermute x4, waiting for transfers between devices, across(): lax.ppermute(value, 'fsdp', [(i, i ^ bit) for i in range(size)])  29.1 us
    all_gather x1, blocking collectives, per_device(): packed = lax.all_gather(packed, 'fsdp', axis=0)  22.1 us
    ppermute x29, starting transfers between devices, swapped(): return lax.ppermute(values, 'dp', [(i, i ^ offset) for i in range(size)])  21.5 us
    pallas_call x1, Pallas kernels, front(): pl.pallas_call(front_kernel, grid=(steps // SUBS,), in_specs=[pl.BlockSpe...  20.1 us
    ppermute x29, waiting for transfers between devices, swapped(): return lax.ppermute(values, 'dp', [(i, i ^ offset) for i in range(size)])  18.3 us
    pallas_call x2, Pallas kernels, unpacked(): pl.pallas_call(functools.partial(kernel, offsets), in_specs=[pl.BlockSpec...  7.19 us
  transfers between devices with their start and end apart: 33, of which 13 were waited for; matrix products, arithmetic and copies ran while one was open for 2% of the time, Pallas kernels for 26%

profile of v2, /device:TPU:0, one launch (start us, length us, event | category | flops | bytes accessed | tf_op | source)
XLA Modules:
  0.0 227.2 jit_solution(17522268489608629274)
XLA Ops:
  0.7 2.1 pack.1
  2.7 22.1 %all-gather = bf16[1088,384]{1,0:T(8,128)(2,1)S(1)} all-gather(bf16[272,384]{1,0:T(8,128)(2,1)} %get-tuple-element.68), channel_id=2, replica_groups=mesh['dp'=8,'fsdp'=4] {'fsdp'}, dimensions={0}, use_global_device_ids=true | all-gather | bytes 1044480 | tf_op jit(solution)/shard_map/all_gather | solution.py:807
  24.8 1.6 collective-permute-start.1
  26.4 1.5 collective-permute-start.2
  27.9 0.5 collective-permute-start.3
  28.4 0.7 add_select_fusion
  29.1 0.1 copy.43
  29.2 0.7 reshape.103.targets.refs_7_
  29.9 0.9 copy-done.5
  30.8 20.1 %front.1 = (f32[4224,384]{1,0:T(8,128)}, bf16[4224,1152]{1,0:T(8,128)(2,1)}, bf16[4224,384]{1,0:T(8,128)(2,1)}, bf16[4224,384]{1,0:T(8,128)(2,1)}, bf16[64,80,76...) custom-call(s32[1]{0:T(128)S(6)} %select_n.60.core.refs_12_, ...), custom_call_target="tpu_custom_call" | custom-call | flops 25200001024 | bytes 56000000 | tf_op jit(solution)/shard_map/front/pallas_call | solution.py:362
  51.1 0.5 collective-permute-start.5
  51.6 0.6 broadcast_in_dim.19.up_b
  52.2 0.5 collective-permute-done.4.refs_3_
  52.7 0.5 collective-permute-done.5.refs_4_
  53.2 0.5 collective-permute-done.6.refs_5_
  53.7 0.2 copy-done.10
  53.9 0.5 copy-done.11
  54.4 58.0 %middle.1 = (bf16[4224,384]{1,0:T(8,128)(2,1)}, f32[4224,384]{1,0:T(8,128)}, bf16[4224,384]{1,0:T(8,128)(2,1)}, bf16[1728,384]{1,0:T(8,128)(2,1)}, bf16[1728,384...) custom-call(s32[1]{0:T(128)} %bitcast.spot, f32[4224,384]{1,0:T(8,128)} %get-tuple-element.69.entry.refs_0_, ...), custom_call_target="tpu_custom_call" | custom-call | flops 49500000256 | bytes 110000000 | tf_op jit(solution)/shard_map/middle/pallas_call | solution.py:484
  112.4 0.2 collective-permute-start.7
  112.6 3.1 %collective-permute-done.7 = bf16[1728,384]{1,0:T(8,128)(2,1)S(1)} collective-permute-done((bf16[1728,384]{1,0:T(8,128)(2,1)}, bf16[1728,384]{1,0:T(8,128)(2,1)S(1)}, u32[]{:S(2)}, u32[]{:S(2)}) %collective-permute-start.7) | collective-permute-done | bytes 1327136 | tf_op jit(solution)/shard_map/ppermute | solution.py:743
  115.7 1.5 fusion.3
  117.2 2.5 %collective-permute-start.10 = (bf16[432,384]{1,0:T(8,128)(2,1)S(1)}, bf16[432,384]{1,0:T(8,128)(2,1)S(1)}, u32[]{:S(2)}, u32[]{:S(2)}) collective-permute-start(bf16[432,384]{1,0:T(8,128)(2,1)S(1)} %get-tuple-element.117), channel_id=1, source_target_pairs={{0,24},{4,28},{8,16},{12,20},{16,8},{20,12},{24,0},{28,4},{1,25},{... | collective-permute-start | bytes 995336 | tf_op jit(solution)/shard_map/ppermute | solution.py:743
  119.7 0.6 collective-permute-start.8
  120.2 0.5 collective-permute-start.9
  120.7 36.8 %back.1 = (bf16[4224,384]{1,0:T(8,128)(2,1)}, bf16[704,384]{1,0:T(8,128)(2,1)}, bf16[704,384]{1,0:T(8,128)(2,1)}) custom-call(f32[4224,384]{1,0:T(8,128)} %get-tuple-element.69.entry.refs_0_, bf16[4224,1152]{1,0:T(8,128)(2,1)} %get-tuple-element.77.refs_1_, bf16[4224,384]{1,0:T(8,128)(2,1)} %get-tuple-element.71.mixture.refs_2_, ...), custom_call_target="tpu_custom_call" | custom-call | flops 35999997952 | bytes 80000000 | tf_op jit(solution)/shard_map/back/pallas_call | solution.py:652
  157.7 1.2 fusion.2
  159.0 10.1 %collective-permute-done.11 = bf16[432,384]{1,0:T(8,128)(2,1)S(1)} collective-permute-done((bf16[432,384]{1,0:T(8,128)(2,1)S(1)}, bf16[432,384]{1,0:T(8,128)(2,1)S(1)}, u32[]{:S(2)}, u32[]{:S(2)}) %collective-permute-start.11) | collective-permute-done | bytes 331808 | tf_op jit(solution)/shard_map/ppermute | solution.py:771
  169.1 0.1 add_convert_fusion.1
  169.2 0.9 collective-permute-start.15
  170.1 0.1 fusion.9
  170.2 2.5 %collective-permute-start.16 = (bf16[176,384]{1,0:T(8,128)(2,1)S(1)}, bf16[176,384]{1,0:T(8,128)(2,1)S(1)}, u32[]{:S(2)}, u32[]{:S(2)}) collective-permute-start(bf16[176,384]{1,0:T(8,128)(2,1)S(1)} %get-tuple-element.120), channel_id=1, source_target_pairs={{0,24},{4,28},{8,16},{12,20},{16,8},{20,12},{24,0},{28,4},{1,25},{... | collective-permute-start | bytes 405512 | tf_op jit(solution)/shard_map/ppermute | solution.py:743
  172.7 0.5 collective-permute-start.13
  173.3 0.5 collective-permute-start.14
  173.8 3.8 %collective-permute-done.16 = bf16[176,384]{1,0:T(8,128)(2,1)S(1)} collective-permute-done((bf16[176,384]{1,0:T(8,128)(2,1)S(1)}, bf16[176,384]{1,0:T(8,128)(2,1)S(1)}, u32[]{:S(2)}, u32[]{:S(2)}) %collective-permute-start.16) | collective-permute-done | bytes 135200 | tf_op jit(solution)/shard_map/ppermute | solution.py:743
  177.6 9.0 %collective-permute-done.15 = bf16[432,384]{1,0:T(8,128)(2,1)S(1)} collective-permute-done((bf16[432,384]{1,0:T(8,128)(2,1)S(1)}, bf16[432,384]{1,0:T(8,128)(2,1)S(1)}, u32[]{:S(2)}, u32[]{:S(2)}) %collective-permute-start.15) | collective-permute-done | bytes 331808 | tf_op jit(solution)/shard_map/ppermute | solution.py:771
  186.6 0.1 fusion.8
  186.8 5.5 %collective-permute-done.17 = bf16[176,384]{1,0:T(8,128)(2,1)S(1)} collective-permute-done((bf16[176,384]{1,0:T(8,128)(2,1)S(1)}, bf16[176,384]{1,0:T(8,128)(2,1)S(1)}, u32[]{:S(2)}, u32[]{:S(2)}) %collective-permute-start.17) | collective-permute-done | bytes 135200 | tf_op jit(solution)/shard_map/ppermute | solution.py:771
  192.3 0.3 collective-permute-start.18
  192.6 0.1 add_convert_fusion.refs_0_
  192.7 1.6 collective-permute-start.26
  194.3 1.5 collective-permute-start.27
  195.8 0.5 collective-permute-start.28
  196.3 4.5 %collective-permute-done.18 = bf16[176,384]{1,0:T(8,128)(2,1)S(1)} collective-permute-done((bf16[176,384]{1,0:T(8,128)(2,1)S(1)}, bf16[176,384]{1,0:T(8,128)(2,1)S(1)}, u32[]{:S(2)}, u32[]{:S(2)}) %collective-permute-start.18) | collective-permute-done | bytes 135200 | tf_op jit(solution)/shard_map/ppermute | solution.py:771
  200.9 1.6 collective-permute-start.19
  202.4 1.5 collective-permute-start.20
  203.9 2.0 collective-permute-start.21
  206.0 4.9 %collective-permute-done.27.refs_2_ = bf16[432,384]{1,0:T(8,128)(2,1)S(1)} collective-permute-done((bf16[432,384]{1,0:T(8,128)(2,1)S(1)}, bf16[432,384]{1,0:T(8,128)(2,1)S(1)}, u32[]{:S(2)}, u32[]{:S(2)}) %collective-permute-start.27) | collective-permute-done | bytes 331808 | tf_op jit(solution)/shard_map/ppermute | solution.py:743
  210.8 2.2 collective-permute-done.19.refs_1_
  213.0 2.6 %collective-permute-done.20.refs_2_ = bf16[176,384]{1,0:T(8,128)(2,1)S(1)} collective-permute-done((bf16[176,384]{1,0:T(8,128)(2,1)S(1)}, bf16[176,384]{1,0:T(8,128)(2,1)S(1)}, u32[]{:S(2)}, u32[]{:S(2)}) %collective-permute-start.20) | collective-permute-done | bytes 135200 | tf_op jit(solution)/shard_map/ppermute | solution.py:743
  215.6 0.5 collective-permute-start.25
  216.1 0.1 collective-permute-start.29
  216.2 0.4 collective-permute-start.30
  216.7 0.1 collective-permute-start.31
  216.7 0.2 collective-permute-done.24.refs_6_
  217.0 0.2 collective-permute-start.32
  217.2 0.1 copy-done.23
  217.3 0.3 copy-done.24
  217.6 0.7 copy-done.25
  218.3 2.8 %close.1 = (f32[384,1152]{1,0:T(8,128)}, f32[128,384]{1,0:T(8,128)}, f32[3,128]{1,0:T(4,128)}, f32[128]{0:T(128)}, f32[1536]{0:T(1024)}, /*index=5*/f32[384]{0:T...) custom-call(s32[1]{0:T(128)} %bitcast.spot, ...), custom_call_target="tpu_custom_call" | custom-call | flops 3600000000 | bytes 8000000 | tf_op jit(solution)/shard_map/close/pallas_call | solution.py:711
  221.1 0.7 copy-done.15
  221.8 0.1 copy-done.16
  221.9 0.1 copy-done.17
  222.1 0.7 copy-done.18
  222.8 4.4 %widen.1 = (f32[384,1536]{1,0:T(8,128)}, f32[1536,384]{1,0:T(8,128)}, f32[384,384]{1,0:T(8,128)}) custom-call(s32[1]{0:T(128)} %bitcast.spot, bf16[432,384]{1,0:T(8,128)(2,1)} %copy-done.2, bf16[432,384]{1,0:T(8,128)(2,1)} %copy-done.12, bf16[432,384]{1,0:T(8,128)(2,1)} %copy-done.13, bf16[432,384]{1,0:T(8,128)(2,1)} %copy-done.14, ...), custom_call_target="tpu_custom_call" | custom-call | flops 3600000000 | bytes 8000000 | tf_op jit(solution)/shard_map/widen/pallas_call | solution.py:711
  (76 shorter events, 0.7 us)
Async XLA Ops:
  24.8 5.1 %copy-start = (bf16[1088,384]{1,0:T(8,128)(2,1)}, bf16[1088,384]{1,0:T(8,128)(2,1)S(1)}, u32[]{:S(2)}) copy-start(bf16[1088,384]{1,0:T(8,128)(2,1)S(1)} %all-gather) | copy-start | bytes 2506756
  24.8 5.1 %collective-permute-start = (bf16[4,272,384]{2,1,0:T(8,128)(2,1)S(1)}, bf16[4,272,384]{2,1,0:T(8,128)(2,1)S(1)}, u32[]{:S(2)}, u32[]{:S(2)}) collective-permute-start(bf16[4,272,384]{2,1,0:T(8,128)(2,1)S(1)} %bitcast.35), channel_id=1, source_target_pairs={{0,4},{4,0},{8,12},{12,8},{16,20},{20,16},{24,28},{28,24},{1,5},{5... | collective-permute-start | bytes 2506760 | tf_op jit(solution)/shard_map/ppermute | solution.py:743
  24.8 26.1 %collective-permute-start.1 = (bf16[4,112,384]{2,1,0:T(8,128)(2,1)S(1)}, bf16[4,112,384]{2,1,0:T(8,128)(2,1)S(1)}, u32[]{:S(2)}, u32[]{:S(2)}) collective-permute-start(bf16[4,112,384]{2,1,0:T(8,128)(2,1)S(1)} %slice.4), channel_id=1, source_target_pairs={{0,8},{4,12},{8,0},{12,4},{16,24},{20,28},{24,16},{28,20},{1,9},{5... | collective-permute-start | bytes 1032200 | tf_op jit(solution)/shard_map/ppermute | solution.py:743
  26.4 24.5 %collective-permute-start.2 = (bf16[4,112,384]{2,1,0:T(8,128)(2,1)S(1)}, bf16[4,112,384]{2,1,0:T(8,128)(2,1)S(1)}, u32[]{:S(2)}, u32[]{:S(2)}) collective-permute-start(bf16[4,112,384]{2,1,0:T(8,128)(2,1)S(1)} %slice.4), channel_id=1, source_target_pairs={{0,16},{4,20},{8,24},{12,28},{16,0},{20,4},{24,8},{28,12},{1,17},{... | collective-permute-start | bytes 1032200 | tf_op jit(solution)/shard_map/ppermute | solution.py:743
  27.9 23.0 %collective-permute-start.3 = (bf16[4,112,384]{2,1,0:T(8,128)(2,1)S(1)}, bf16[4,112,384]{2,1,0:T(8,128)(2,1)S(1)}, u32[]{:S(2)}, u32[]{:S(2)}) collective-permute-start(bf16[4,112,384]{2,1,0:T(8,128)(2,1)S(1)} %slice.4), channel_id=1, source_target_pairs={{0,24},{4,28},{8,16},{12,20},{16,8},{20,12},{24,0},{28,4},{1,25},{... | collective-permute-start | bytes 1032200 | tf_op jit(solution)/shard_map/ppermute | solution.py:743
  29.9 0.9 copy-start.5
  30.8 20.8 %copy-start.4 = (f32[1536]{0:T(1024)S(1)}, f32[1536]{0:T(1024)}, u32[]{:S(2)}) copy-start(f32[1536]{0:T(1024)} %param.38) | copy-start | bytes 18436
  50.9 2.8 %copy-start.6 = (bf16[4,112,384]{2,1,0:T(8,128)(2,1)}, bf16[4,112,384]{2,1,0:T(8,128)(2,1)S(1)}, u32[]{:S(2)}) copy-start(bf16[4,112,384]{2,1,0:T(8,128)(2,1)S(1)} %collective-permute-done.1.refs_0_) | copy-start | bytes 1032196
  51.0 2.7 %copy-start.7 = (bf16[4,112,384]{2,1,0:T(8,128)(2,1)}, bf16[4,112,384]{2,1,0:T(8,128)(2,1)S(1)}, u32[]{:S(2)}) copy-start(bf16[4,112,384]{2,1,0:T(8,128)(2,1)S(1)} %collective-permute-done.2.refs_1_) | copy-start | bytes 1032196
  51.0 2.7 %copy-start.8 = (bf16[4,112,384]{2,1,0:T(8,128)(2,1)}, bf16[4,112,384]{2,1,0:T(8,128)(2,1)S(1)}, u32[]{:S(2)}) copy-start(bf16[4,112,384]{2,1,0:T(8,128)(2,1)S(1)} %collective-permute-done.3.refs_2_) | copy-start | bytes 1032196
  51.0 1.7 collective-permute-start.4
  51.1 2.1 collective-permute-start.5
  51.6 2.1 collective-permute-start.6
  52.7 1.0 copy-start.9
  53.2 0.7 copy-start.10
  53.7 0.7 copy-start.11
  112.4 3.3 %collective-permute-start.7 = (bf16[1728,384]{1,0:T(8,128)(2,1)}, bf16[1728,384]{1,0:T(8,128)(2,1)S(1)}, u32[]{:S(2)}, u32[]{:S(2)}) collective-permute-start(bf16[1728,384]{1,0:T(8,128)(2,1)} %get-tuple-element.80), channel_id=1, source_target_pairs={{0,4},{4,0},{8,12},{12,8},{16,20},{20,16},{24,28},{28,24},{1,5},{5... | collective-permute-start | bytes 3981320 | tf_op jit(solution)/shard_map/ppermute | solution.py:743
  117.2 40.4 %collective-permute-start.10 = (bf16[432,384]{1,0:T(8,128)(2,1)S(1)}, bf16[432,384]{1,0:T(8,128)(2,1)S(1)}, u32[]{:S(2)}, u32[]{:S(2)}) collective-permute-start(bf16[432,384]{1,0:T(8,128)(2,1)S(1)} %get-tuple-element.117), channel_id=1, source_target_pairs={{0,24},{4,28},{8,16},{12,20},{16,8},{20,12},{24,0},{28,4},{1,25},{... | collective-permute-start | bytes 995336 | tf_op jit(solution)/shard_map/ppermute | solution.py:743
  119.7 38.0 %collective-permute-start.8 = (bf16[432,384]{1,0:T(8,128)(2,1)S(1)}, bf16[432,384]{1,0:T(8,128)(2,1)S(1)}, u32[]{:S(2)}, u32[]{:S(2)}) collective-permute-start(bf16[432,384]{1,0:T(8,128)(2,1)S(1)} %get-tuple-element.116), channel_id=1, source_target_pairs={{0,8},{4,12},{8,0},{12,4},{16,24},{20,28},{24,16},{28,20},{1,9},{5... | collective-permute-start | bytes 995336 | tf_op jit(solution)/shard_map/ppermute | solution.py:743
  120.2 37.4 %collective-permute-start.9 = (bf16[432,384]{1,0:T(8,128)(2,1)S(1)}, bf16[432,384]{1,0:T(8,128)(2,1)S(1)}, u32[]{:S(2)}, u32[]{:S(2)}) collective-permute-start(bf16[432,384]{1,0:T(8,128)(2,1)S(1)} %get-tuple-element.118), channel_id=1, source_target_pairs={{0,16},{4,20},{8,24},{12,28},{16,0},{20,4},{24,8},{28,12},{1,17},{... | collective-permute-start | bytes 995336 | tf_op jit(solution)/shard_map/ppermute | solution.py:743
  157.5 12.6 %copy-start.1 = (bf16[704,384]{1,0:T(8,128)(2,1)S(1)}, bf16[704,384]{1,0:T(8,128)(2,1)}, u32[]{:S(2)}) copy-start(bf16[704,384]{1,0:T(8,128)(2,1)} %get-tuple-element.90) | copy-start | bytes 1622020
  157.6 11.6 %collective-permute-start.12 = (bf16[704,384]{1,0:T(8,128)(2,1)}, bf16[704,384]{1,0:T(8,128)(2,1)S(1)}, u32[]{:S(2)}, u32[]{:S(2)}) collective-permute-start(bf16[704,384]{1,0:T(8,128)(2,1)} %get-tuple-element.95), channel_id=1, source_target_pairs={{0,4},{4,0},{8,12},{12,8},{16,20},{20,16},{24,28},{28,24},{1,5},{5... | collective-permute-start | bytes 1622024 | tf_op jit(solution)/shard_map/ppermute | solution.py:743
  158.9 10.2 %collective-permute-start.11 = (bf16[432,384]{1,0:T(8,128)(2,1)S(1)}, bf16[432,384]{1,0:T(8,128)(2,1)S(1)}, u32[]{:S(2)}, u32[]{:S(2)}) collective-permute-start(bf16[432,384]{1,0:T(8,128)(2,1)S(1)} %fusion.2), channel_id=1, source_target_pairs={{0,1},{1,0},{2,3},{3,2},{4,5},{5,4},{6,7},{7,6},{8,9},{9,8},{10,11... | collective-permute-start | bytes 995336 | tf_op jit(solution)/shard_map/ppermute | solution.py:771
  169.2 17.4 %collective-permute-start.15 = (bf16[432,384]{1,0:T(8,128)(2,1)S(1)}, bf16[432,384]{1,0:T(8,128)(2,1)S(1)}, u32[]{:S(2)}, u32[]{:S(2)}) collective-permute-start(bf16[432,384]{1,0:T(8,128)(2,1)S(1)} %add_convert_fusion.1), channel_id=1, source_target_pairs={{0,2},{1,3},{2,0},{3,1},{4,6},{5,7},{6,4},{7,5},{8,10},{9,11},{10,... | collective-permute-start | bytes 995336 | tf_op jit(solution)/shard_map/ppermute | solution.py:771
  170.2 7.4 %collective-permute-start.16 = (bf16[176,384]{1,0:T(8,128)(2,1)S(1)}, bf16[176,384]{1,0:T(8,128)(2,1)S(1)}, u32[]{:S(2)}, u32[]{:S(2)}) collective-permute-start(bf16[176,384]{1,0:T(8,128)(2,1)S(1)} %get-tuple-element.120), channel_id=1, source_target_pairs={{0,24},{4,28},{8,16},{12,20},{16,8},{20,12},{24,0},{28,4},{1,25},{... | collective-permute-start | bytes 405512 | tf_op jit(solution)/shard_map/ppermute | solution.py:743
  172.7 13.9 %collective-permute-start.13 = (bf16[176,384]{1,0:T(8,128)(2,1)S(1)}, bf16[176,384]{1,0:T(8,128)(2,1)S(1)}, u32[]{:S(2)}, u32[]{:S(2)}) collective-permute-start(bf16[176,384]{1,0:T(8,128)(2,1)S(1)} %get-tuple-element.119), channel_id=1, source_target_pairs={{0,8},{4,12},{8,0},{12,4},{16,24},{20,28},{24,16},{28,20},{1,9},{5... | collective-permute-start | bytes 405512 | tf_op jit(solution)/shard_map/ppermute | solution.py:743
  173.3 13.3 %collective-permute-start.14 = (bf16[176,384]{1,0:T(8,128)(2,1)S(1)}, bf16[176,384]{1,0:T(8,128)(2,1)S(1)}, u32[]{:S(2)}, u32[]{:S(2)}) collective-permute-start(bf16[176,384]{1,0:T(8,128)(2,1)S(1)} %get-tuple-element.121), channel_id=1, source_target_pairs={{0,16},{4,20},{8,24},{12,28},{16,0},{20,4},{24,8},{28,12},{1,17},{... | collective-permute-start | bytes 405512 | tf_op jit(solution)/shard_map/ppermute | solution.py:743
  186.7 5.6 %collective-permute-start.17 = (bf16[176,384]{1,0:T(8,128)(2,1)S(1)}, bf16[176,384]{1,0:T(8,128)(2,1)S(1)}, u32[]{:S(2)}, u32[]{:S(2)}) collective-permute-start(bf16[176,384]{1,0:T(8,128)(2,1)S(1)} %fusion.8), channel_id=1, source_target_pairs={{0,1},{1,0},{2,3},{3,2},{4,5},{5,4},{6,7},{7,6},{8,9},{9,8},{10,11... | collective-permute-start | bytes 405512 | tf_op jit(solution)/shard_map/ppermute | solution.py:771
  192.3 8.5 %collective-permute-start.18 = (bf16[176,384]{1,0:T(8,128)(2,1)S(1)}, bf16[176,384]{1,0:T(8,128)(2,1)S(1)}, u32[]{:S(2)}, u32[]{:S(2)}) collective-permute-start(bf16[176,384]{1,0:T(8,128)(2,1)S(1)} %add_convert_fusion.6), channel_id=1, source_target_pairs={{0,2},{1,3},{2,0},{3,1},{4,6},{5,7},{6,4},{7,5},{8,10},{9,11},{10,... | collective-permute-start | bytes 405512 | tf_op jit(solution)/shard_map/ppermute | solution.py:771
  192.7 28.3 %copy-start.2 = (bf16[432,384]{1,0:T(8,128)(2,1)}, bf16[432,384]{1,0:T(8,128)(2,1)S(1)}, u32[]{:S(2)}) copy-start(bf16[432,384]{1,0:T(8,128)(2,1)S(1)} %add_convert_fusion.refs_0_) | copy-start | bytes 995332
  192.7 11.2 %collective-permute-start.26 = (bf16[432,384]{1,0:T(8,128)(2,1)S(1)}, bf16[432,384]{1,0:T(8,128)(2,1)S(1)}, u32[]{:S(2)}, u32[]{:S(2)}) collective-permute-start(bf16[432,384]{1,0:T(8,128)(2,1)S(1)} %add_convert_fusion.refs_0_), channel_id=1, source_target_pairs={{0,8},{4,12},{8,0},{12,4},{16,24},{20,28},{24,16},{28,20},{1,9},{5... | collective-permute-start | bytes 995336 | tf_op jit(solution)/shard_map/ppermute | solution.py:743
  194.3 16.6 %collective-permute-start.27 = (bf16[432,384]{1,0:T(8,128)(2,1)S(1)}, bf16[432,384]{1,0:T(8,128)(2,1)S(1)}, u32[]{:S(2)}, u32[]{:S(2)}) collective-permute-start(bf16[432,384]{1,0:T(8,128)(2,1)S(1)} %add_convert_fusion.refs_0_), channel_id=1, source_target_pairs={{0,16},{4,20},{8,24},{12,28},{16,0},{20,4},{24,8},{28,12},{1,17},{... | collective-permute-start | bytes 995336 | tf_op jit(solution)/shard_map/ppermute | solution.py:743
  195.8 20.3 %collective-permute-start.28 = (bf16[432,384]{1,0:T(8,128)(2,1)S(1)}, bf16[432,384]{1,0:T(8,128)(2,1)S(1)}, u32[]{:S(2)}, u32[]{:S(2)}) collective-permute-start(bf16[432,384]{1,0:T(8,128)(2,1)S(1)} %add_convert_fusion.refs_0_), channel_id=1, source_target_pairs={{0,24},{4,28},{8,16},{12,20},{16,8},{20,12},{24,0},{28,4},{1,25},{... | collective-permute-start | bytes 995336 | tf_op jit(solution)/shard_map/ppermute | solution.py:743
  200.9 16.3 %copy-start.3 = (bf16[176,384]{1,0:T(8,128)(2,1)}, bf16[176,384]{1,0:T(8,128)(2,1)S(1)}, u32[]{:S(2)}) copy-start(bf16[176,384]{1,0:T(8,128)(2,1)S(1)} %add_convert_fusion.5.refs_0_) | copy-start | bytes 405508
  200.9 12.1 %collective-permute-start.19 = (bf16[176,384]{1,0:T(8,128)(2,1)S(1)}, bf16[176,384]{1,0:T(8,128)(2,1)S(1)}, u32[]{:S(2)}, u32[]{:S(2)}) collective-permute-start(bf16[176,384]{1,0:T(8,128)(2,1)S(1)} %add_convert_fusion.5.refs_0_), channel_id=1, source_target_pairs={{0,8},{4,12},{8,0},{12,4},{16,24},{20,28},{24,16},{28,20},{1,9},{5... | collective-permute-start | bytes 405512 | tf_op jit(solution)/shard_map/ppermute | solution.py:743
  202.4 13.2 %collective-permute-start.20 = (bf16[176,384]{1,0:T(8,128)(2,1)S(1)}, bf16[176,384]{1,0:T(8,128)(2,1)S(1)}, u32[]{:S(2)}, u32[]{:S(2)}) collective-permute-start(bf16[176,384]{1,0:T(8,128)(2,1)S(1)} %add_convert_fusion.5.refs_0_), channel_id=1, source_target_pairs={{0,16},{4,20},{8,24},{12,28},{16,0},{20,4},{24,8},{28,12},{1,17},{... | collective-permute-start | bytes 405512 | tf_op jit(solution)/shard_map/ppermute | solution.py:743
  203.9 17.1 %copy-start.12 = (bf16[432,384]{1,0:T(8,128)(2,1)}, bf16[432,384]{1,0:T(8,128)(2,1)S(1)}, u32[]{:S(2)}) copy-start(bf16[432,384]{1,0:T(8,128)(2,1)S(1)} %collective-permute-done.26.refs_1_) | copy-start | bytes 995332
  203.9 11.7 %collective-permute-start.21 = (bf16[176,384]{1,0:T(8,128)(2,1)S(1)}, bf16[176,384]{1,0:T(8,128)(2,1)S(1)}, u32[]{:S(2)}, u32[]{:S(2)}) collective-permute-start(bf16[176,384]{1,0:T(8,128)(2,1)S(1)} %add_convert_fusion.5.refs_0_), channel_id=1, source_target_pairs={{0,24},{4,28},{8,16},{12,20},{16,8},{20,12},{24,0},{28,4},{1,25},{... | collective-permute-start | bytes 405512 | tf_op jit(solution)/shard_map/ppermute | solution.py:743
  210.8 10.2 %copy-start.13 = (bf16[432,384]{1,0:T(8,128)(2,1)}, bf16[432,384]{1,0:T(8,128)(2,1)S(1)}, u32[]{:S(2)}) copy-start(bf16[432,384]{1,0:T(8,128)(2,1)S(1)} %collective-permute-done.27.refs_2_) | copy-start | bytes 995332
  210.8 5.4 %collective-permute-start.22 = (bf16[176,384]{1,0:T(8,128)(2,1)S(1)}, bf16[176,384]{1,0:T(8,128)(2,1)S(1)}, u32[]{:S(2)}, u32[]{:S(2)}) collective-permute-start(bf16[176,384]{1,0:T(8,128)(2,1)S(1)} %add_convert_fusion.5.refs_0_), channel_id=1, source_target_pairs={{0,4},{4,0},{8,12},{12,8},{16,20},{20,16},{24,28},{28,24},{1,5},{5... | collective-permute-start | bytes 405512 | tf_op jit(solution)/shard_map/ppermute | solution.py:743
  213.0 4.2 %copy-start.19 = (bf16[176,384]{1,0:T(8,128)(2,1)}, bf16[176,384]{1,0:T(8,128)(2,1)S(1)}, u32[]{:S(2)}) copy-start(bf16[176,384]{1,0:T(8,128)(2,1)S(1)} %collective-permute-done.19.refs_1_) | copy-start | bytes 405508
  213.0 3.7 %collective-permute-start.23 = (bf16[176,384]{1,0:T(8,128)(2,1)S(1)}, bf16[176,384]{1,0:T(8,128)(2,1)S(1)}, u32[]{:S(2)}, u32[]{:S(2)}) collective-permute-start(bf16[176,384]{1,0:T(8,128)(2,1)S(1)} %collective-permute-done.19.refs_1_), channel_id=1, source_target_pairs={{0,4},{4,0},{8,12},{12,8},{16,20},{20,16},{24,28},{28,24},{1,5},{5... | collective-permute-start | bytes 405512 | tf_op jit(solution)/shard_map/ppermute | solution.py:743
  215.6 1.6 copy-start.20
  215.6 1.4 collective-permute-start.24
  215.6 1.5 copy-start.21
  215.6 1.5 collective-permute-start.25
  216.1 4.9 %copy-start.14 = (bf16[432,384]{1,0:T(8,128)(2,1)}, bf16[432,384]{1,0:T(8,128)(2,1)S(1)}, u32[]{:S(2)}) copy-start(bf16[432,384]{1,0:T(8,128)(2,1)S(1)} %collective-permute-done.28.refs_3_) | copy-start | bytes 995332
  216.1 4.9 %collective-permute-start.29 = (bf16[432,384]{1,0:T(8,128)(2,1)S(1)}, bf16[432,384]{1,0:T(8,128)(2,1)S(1)}, u32[]{:S(2)}, u32[]{:S(2)}) collective-permute-start(bf16[432,384]{1,0:T(8,128)(2,1)S(1)} %add_convert_fusion.refs_0_), channel_id=1, source_target_pairs={{0,4},{4,0},{8,12},{12,8},{16,20},{20,16},{24,28},{28,24},{1,5},{5... | collective-permute-start | bytes 995336 | tf_op jit(solution)/shard_map/ppermute | solution.py:743
  216.2 1.0 copy-start.22
  216.2 4.9 %collective-permute-start.30 = (bf16[432,384]{1,0:T(8,128)(2,1)S(1)}, bf16[432,384]{1,0:T(8,128)(2,1)S(1)}, u32[]{:S(2)}, u32[]{:S(2)}) collective-permute-start(bf16[432,384]{1,0:T(8,128)(2,1)S(1)} %collective-permute-done.26.refs_1_), channel_id=1, source_target_pairs={{0,4},{4,0},{8,12},{12,8},{16,20},{20,16},{24,28},{28,24},{1,5},{5... | collective-permute-start | bytes 995336 | tf_op jit(solution)/shard_map/ppermute | solution.py:743
  216.7 0.6 copy-start.23
  216.7 4.5 %collective-permute-start.31 = (bf16[432,384]{1,0:T(8,128)(2,1)S(1)}, bf16[432,384]{1,0:T(8,128)(2,1)S(1)}, u32[]{:S(2)}, u32[]{:S(2)}) collective-permute-start(bf16[432,384]{1,0:T(8,128)(2,1)S(1)} %collective-permute-done.27.refs_2_), channel_id=1, source_target_pairs={{0,4},{4,0},{8,12},{12,8},{16,20},{20,16},{24,28},{28,24},{1,5},{5... | collective-permute-start | bytes 995336 | tf_op jit(solution)/shard_map/ppermute | solution.py:743
  217.0 0.7 copy-start.24
  217.0 4.2 %collective-permute-start.32 = (bf16[432,384]{1,0:T(8,128)(2,1)S(1)}, bf16[432,384]{1,0:T(8,128)(2,1)S(1)}, u32[]{:S(2)}, u32[]{:S(2)}) collective-permute-start(bf16[432,384]{1,0:T(8,128)(2,1)S(1)} %collective-permute-done.28.refs_3_), channel_id=1, source_target_pairs={{0,4},{4,0},{8,12},{12,8},{16,20},{20,16},{24,28},{28,24},{1,5},{5... | collective-permute-start | bytes 995336 | tf_op jit(solution)/shard_map/ppermute | solution.py:743
  217.6 0.7 copy-start.25
  221.1 0.7 copy-start.15
  221.1 0.8 copy-start.16
  221.1 0.9 copy-start.17
  222.1 0.7 copy-start.18

commit v3 on v2

--- a/solution.py
+++ b/solution.py
@@ -19,6 +19,7 @@
 KEYS = 128
 PAIRS = HEADS // 2
 GROUP = 8
+BACK_GROUP = 24
 SUBS = 2
 VMEM = 60 * 2**20
 LOG2E = 1.4426950408889634
@@ -533,8 +534,8 @@
     minus = lane_ones(-1.0)
     jobs = [(pair, cloud) for pair in range(PAIRS) for cloud in range(TILE)]
     tails = {}
-    for at in range(0, len(jobs), GROUP):
-        group = jobs[at : at + GROUP]
+    for at in range(0, len(jobs), BACK_GROUP):
+        group = jobs[at : at + BACK_GROUP]
         gaps = []
         for pair, cloud in group:
             base = cloud * STEP
@@ -557,10 +558,10 @@
             sdm = stacked_heads(mix_grad[base : base + WIN, pair * 128 : pair * 128 + 128])
             e = jnp.concatenate([e[:, :KEYS], e[:, KEYS:]], axis=0)
             tall = jnp.concatenate([ds[:, :KEYS], ds[:, KEYS:]], axis=0)
-            results.append((dot(ds, key), dot(tall, query, TN), dot(e, sdm, TN)))
+            results.append((dot(ds, key), dot(tall[:, :WIN], query, TN), dot(e[:, :WIN], sdm, TN)))
         for (pair, cloud), (dq, dk, dv) in zip(group, results):
             base = cloud * STEP
-            parts = (dq * 0.125, dk[:WIN] * (1.0 / LOG2E), dv[:WIN])
+            parts = (dq * 0.125, dk * (1.0 / LOG2E), dv)
             for which, part in enumerate(parts):
                 cols = slice(which * D + pair * 128, which * D + pair * 128 + 128)
                 head = part[:16]
@@ -681,46 +682,57 @@
 
 
 def close_kernel(offsets, spot, *refs):
-    pieces, refs = refs[: len(offsets)], refs[len(offsets) :]
-    joint_g, proj_g, place_g, small, sums = refs[0], refs[1], refs[2], refs[3:-1], refs[-1]
-    gather_pieces(spot[0], offsets, pieces, sums)
-    for part in range(3):
-        joint_g[:, part * D : part * D + D] = sums[part * D : part * D + D, :].astype(f32)
-    proj_g[...] = sums[3 * D : 3 * D + POSH, :].astype(f32)
-    rows = sums[3 * D + POSH : 3 * D + POSH + 16, :].astype(f32)
-    for part in range(3):
-        place_g[part : part + 1, :] = rows[8:9, part * POSH : part * POSH + POSH]
-    small[0][...] = rows[9:10, :POSH].reshape(POSH)
-    small[1][...] = jnp.concatenate([rows[10 + part : 11 + part] for part in range(4)], axis=1).reshape(FF)
-    for at in range(8):
-        small[2 + at][...] = rows[at : at + 1].reshape(D)
-
-
-def widen_kernel(offsets, spot, *refs):
-    pieces, refs = refs[: len(offsets)], refs[len(offsets) :]
-    up_g, down_g, out_g, sums = refs
-    gather_pieces(spot[0], offsets, pieces, sums)
-    for part in range(4):
-        up_g[:, part * D : part * D + D] = sums[part * D : part * D + D, :].astype(f32)
-    down_g[...] = sums[4 * D : 8 * D, :].astype(f32)
-    out_g[...] = sums[8 * D : 9 * D, :].astype(f32)
-
-
-def unpacked(kernel, name, shapes, spot, offsets, pieces):
-    vmem = pl.BlockSpec(memory_space=pltpu.VMEM)
+    count = len(offsets)
+    first_pieces, last_pieces, refs = refs[:count], refs[count : 2 * count], refs[2 * count :]
+    up_g, down_g, out_g, joint_g, proj_g, place_g, *small = refs[:-2]
+    sums, last = refs[-2:]
+    step = pl.program_id(0)
+
+    @pl.when(step == 0)
+    def _():
+        gather_pieces(spot[0], offsets, first_pieces, sums)
+        gather_pieces(spot[0], offsets, last_pieces, last)
+        out_g[...] = sums[8 * D : 9 * D, :].astype(f32)
+        proj_g[...] = last[3 * D : 3 * D + POSH, :].astype(f32)
+        rows = last[3 * D + POSH : 3 * D + POSH + 16, :].astype(f32)
+        for part in range(3):
+            place_g[part : part + 1, :] = rows[8:9, part * POSH : part * POSH + POSH]
+        small[0][...] = rows[9:10, :POSH].reshape(POSH)
+        small[1][...] = jnp.concatenate([rows[10 + part : 11 + part] for part in range(4)], axis=1).reshape(FF)
+        for at in range(8):
+            small[2 + at][...] = rows[at : at + 1].reshape(D)
+
+    up_g[...] = sums[pl.ds(pl.multiple_of(step * D, 16), D), :].astype(f32)
+    down_g[...] = sums[pl.ds(pl.multiple_of((step + 4) * D, 16), D), :].astype(f32)
+    joint_g[...] = last[pl.ds(pl.multiple_of(jnp.minimum(step, 2) * D, 16), D), :].astype(f32)
+
+
+def close(spot, first, last):
+    pieces = [*first.values(), *last.values()]
+    count = len(first)
+
+    def one(shape):
+        return pl.BlockSpec(shape, lambda i: (0,) * len(shape))
+
+    flat = [(POSH,), (FF,)] + [(D,)] * 8
     return pl.pallas_call(
-        functools.partial(kernel, offsets),
-        in_specs=[pl.BlockSpec(memory_space=pltpu.SMEM)] + [vmem] * len(pieces),
-        out_specs=[vmem] * len(shapes),
-        out_shape=[shape_of(shape, f32) for shape in shapes],
-        scratch_shapes=[pltpu.VMEM((pieces[0].shape[0] * len(pieces), D), bf16)],
+        functools.partial(close_kernel, list(first)),
+        grid=(4,),
+        in_specs=[pl.BlockSpec(memory_space=pltpu.SMEM)] + [one(piece.shape) for piece in pieces],
+        out_specs=[
+            pl.BlockSpec((D, D), lambda i: (0, i)), pl.BlockSpec((D, D), lambda i: (i, 0)), one((D, D)),
+            pl.BlockSpec((D, D), lambda i: (0, jnp.minimum(i, 2))), one((POSH, D)), one((3, POSH)),
+        ]
+        + [one(shape) for shape in flat],
+        out_shape=[
+            shape_of(shape, f32) for shape in [(D, FF), (FF, D), (D, D), (D, 3 * D), (POSH, D), (3, POSH)] + flat
+        ],
+        scratch_shapes=[
+            pltpu.VMEM((pieces[0].shape[0] * count, D), bf16), pltpu.VMEM((pieces[-1].shape[0] * count, D), bf16),
+        ],
         compiler_params=settings(),
-        cost_estimate=cost(4),
-        name=name,
+        name="close",
     )(spot, *pieces)
-
-
-CALLS = 1
 
 
 def bits_of(size):
@@ -766,13 +778,16 @@
     return found
 
 
-def across(terms, bit, size):
-    value = total(terms)
-    return [value, lax.ppermute(value, "fsdp", [(i, i ^ bit) for i in range(size)])]
+def crossed(values, offset, size):
+    return lax.ppermute(values, "fsdp", [(i, i ^ offset) for i in range(size)])
 
 
 def tied(first, second):
     return lax.optimization_barrier((first, second))
+
+
+def after(value, other):
+    return lax.optimization_barrier((value, other))[0]
 
 
 def per_device(
@@ -808,61 +823,59 @@
     packed_other = swapped(packed, 1, dp)
     half = (3 * joint_weight.shape[0] + place_proj.shape[0]) // 2
     late = packed[:, half:]
-    near = [swapped(late, 2 * offset, dp) for offset in range(1, dp // 2)]
+    pieces = [swapped(late, 2 * offset, dp) for offset in range(1, dp // 2)]
     targets = marked_targets(mask_count, mask_index)
     up_b = up_bias[None, :]
     entry, joint, mixture, shares, weights, joint_w, proj, cen, place_w = front(
         core, tokens, centers, targets, vec, place_weight, place_bias[None, :], packed, packed_other
     )
-    near, mixture = tied(near, mixture)
-    near_other = [swapped(piece, 1, dp) for piece in near]
+    pieces, mixture = tied(pieces, mixture)
+    pieces_other = [swapped(piece, 1, dp) for piece in pieces]
     order = list(range(dp))
     output, mid_grad, mix_grad, kept, sent, up_bg, vec_g = middle_part(
-        spot, entry, mixture, shares, cotangent, vec, up_b, packed, packed_other, near, near_other, order
+        spot, entry, mixture, shares, cotangent, vec, up_b, packed, packed_other, pieces, pieces_other, order
     )
     chips = chip_bits(dp)
-    stages = [functools.partial(scattered, bits=bits, size=dp) for bits in chips]
-    stages += [functools.partial(across, bit=bit, size=fsdp) for bit in bits_of(fsdp)]
+    near, far = [offset % fsdp for offset in (1, 2)]
+    sums = [kept, swapped(sent, 1, dp)]
+    mix_grad, sums[-1] = tied(mix_grad, sums[-1])
+    sums = scattered(sums, chips[0], dp)
+    given = [entry, joint, mixture, weights, mix_grad, mid_grad, cen, targets, vec, place_w, proj, joint_w]
     steps = tokens.shape[0] // ROWS
-    parts = [steps * (part + 1) // CALLS - steps * part // CALLS for part in range(CALLS)]
-    before, first = None, 0
-    sums = [kept, swapped(sent, 1, dp)]
-    for part, count in enumerate(parts):
-        mix_grad, sums[-1] = tied(mix_grad, sums[-1])
-        sums = stages[part](sums)
-        given = (entry, joint, mixture, weights, mix_grad, mid_grad, cen, targets, vec, place_w, proj, joint_w)
-        extra = [core, up_bg, vec_g] if part == CALLS - 1 else None
-        before = back_part(given, first, count, order, before, extra)
-        first += count
-    tokens_grad, kept, sent = before
-    rest = stages[CALLS:]
-    sent, sums[-1] = tied(sent, sums[-1])
-    sums = rest[0](sums)
+    early_steps = steps // 2
+    before = list(back_part(given, 0, early_steps, order))
+    for bits in chips[1:]:
+        sums = scattered(sums, bits, dp)
+    sums[-1], before[0] = tied(sums[-1], before[0])
+    middle_row = sums[0].shape[0] // 2
+    upper = total([term[:middle_row] for term in sums])
+    lower = total([term[middle_row:] for term in sums])
+    upper_got, lower_got = crossed(upper, near, fsdp), crossed(lower, far, fsdp)
+    given[4] = after(given[4], lower)
+    tokens_grad, kept, sent = back_part(given, early_steps, steps - early_steps, order, before, [core, up_bg, vec_g])
+    sent, upper_got, lower_got = lax.optimization_barrier((sent, upper_got, lower_got))
+    upper, lower = total([upper, upper_got]), total([lower, lower_got])
+    upper_got, lower_got = crossed(upper, far, fsdp), crossed(lower, near, fsdp)
     last = [kept, swapped(sent, 1, dp)]
-    sums[-1], last[-1] = tied(sums[-1], last[-1])
-    for at, stage in enumerate(rest[1:]):
-        sums = stage(sums)
-        last = stages[at](last)
-        sums[-1], last[-1] = tied(sums[-1], last[-1])
-    sums = {0: total(sums)}
+    last = scattered(last, chips[0], dp)
+    upper_got = after(upper_got, last[-1])
+    sums = {0: jnp.concatenate([total([upper, upper_got]), total([lower, lower_got])], axis=0)}
+    for bits in chips[1:]:
+        last = scattered(last, bits, dp)
+    value = total(last)
+    near_got = after(crossed(value, near, fsdp), sums[0])
     for bits in reversed(chips):
         sums = joined(sums, bits, dp)
-    for stage in stages[len(rest) - 1 :]:
-        last = stage(last)
-    last = {0: total(last)}
+    value = total([value, near_got])
+    far_got = crossed(value, far, fsdp)
+    newest = list(sums)[-1]
+    far_got, sums[newest] = tied(far_got, sums[newest])
+    last = {0: total([value, far_got])}
     for bits in reversed(chips):
         last = joined(last, bits, dp)
     sums, last = joined(sums, [1], dp), joined(last, [1], dp)
-    up_grad, down_grad, out_grad = unpacked(
-        widen_kernel, "widen", [(D, FF), (FF, D), (D, D)], spot, list(sums), list(sums.values())
-    )
-    joint_grad, proj_grad, place_weight_grad, place_bias_grad, up_bias_grad, *small = unpacked(
-        close_kernel,
-        "close",
-        [(D, 3 * D), (POSH, D), (3, POSH), (POSH,), (FF,)] + [(D,)] * 8,
-        spot,
-        list(last),
-        list(last.values()),
+    up_grad, down_grad, out_grad, joint_grad, proj_grad, place_weight_grad, place_bias_grad, up_bias_grad, *small = close(
+        spot, sums, last
     )
     return (
         output,

time: 228 us -> 212 us (0.930)
  waiting for transfers between devices: 47.4 us -> 27.1 us
  starting transfers between devices: 22.9 us -> 26.9 us
    ppermute x4 -> x6, waiting for transfers between devices: 29.1 us -> 11.2 us  [crossed(): return lax.ppermute(values, 'fsdp', [(i, i ^ offset) for i in range(size)])]
    ppermute x4 -> x6, starting transfers between devices: 1.38 us -> 6.42 us  [crossed(): return lax.ppermute(values, 'fsdp', [(i, i ^ offset) for i in range(size)])]
    ppermute x29, waiting for transfers between devices: 18.3 us -> 15.9 us  [swapped(): return lax.ppermute(values, 'dp', [(i, i ^ offset) for i in range(size)])]
    convert_element_type x8 -> x10, other arithmetic: 3.14 us -> 5.1 us  [total(): return sum((term.astype(f32) for term in terms)).astype(bf16)]
    pallas_call x1 -> x2, Pallas kernels: 36.8 us -> 38.4 us  [back_part(): pl.pallas_call(functools.partial(back_kernel, before is None, extra is no...]
    pallas_call x2 -> x1, Pallas kernels: 7.19 us -> 5.81 us  [close(): pl.pallas_call(functools.partial(close_kernel, list(first)), grid=(4,), i...]
  transfers between devices with their start and end apart: 33 -> 35, of which waited for: 13 -> 17; matrix products, arithmetic and copies ran while one was open for 2% -> 2% of each run, Pallas kernels for 26% -> 28%
where the time goes in v3:
time: 212 us
  Pallas kernels  124 us (58%)
  waiting for transfers between devices  27.1 us (13%)
  starting transfers between devices  26.9 us (13%)
  blocking collectives  22.1 us (10%)
  other arithmetic  5.86 us (3%)
  local copies, waits for them, and re-layouts  4.6 us (2%)
    pallas_call x1, Pallas kernels, middle_part(): pl.pallas_call(functools.partial(middle_kernel, chunk, order), grid=(coun...  58 us
    pallas_call x2, Pallas kernels, back_part(): pl.pallas_call(functools.partial(back_kernel, before is None, extra is no...  38.4 us
    all_gather x1, blocking collectives, per_device(): packed = lax.all_gather(packed, 'fsdp', axis=0)  22.1 us
    ppermute x29, starting transfers between devices, swapped(): return lax.ppermute(values, 'dp', [(i, i ^ offset) for i in range(size)])  20.5 us
    pallas_call x1, Pallas kernels, front(): pl.pallas_call(front_kernel, grid=(steps // SUBS,), in_specs=[pl.BlockSpe...  20.1 us
    ppermute x29, waiting for transfers between devices, swapped(): return lax.ppermute(values, 'dp', [(i, i ^ offset) for i in range(size)])  15.9 us
    ppermute x6, waiting for transfers between devices, crossed(): return lax.ppermute(values, 'fsdp', [(i, i ^ offset) for i in range(size)])  11.2 us
    ppermute x6, starting transfers between devices, crossed(): return lax.ppermute(values, 'fsdp', [(i, i ^ offset) for i in range(size)])  6.42 us
  transfers between devices with their start and end apart: 35, of which 17 were waited for; matrix products, arithmetic and copies ran while one was open for 2% of the time, Pallas kernels for 28%

profile of v3, /device:TPU:0, one launch (start us, length us, event | category | flops | bytes accessed | tf_op | source)
XLA Modules:
  0.0 212.1 jit_solution(17715229061677867908)
XLA Ops:
  0.7 2.1 pack.1
  2.7 22.1 %all-gather = bf16[1088,384]{1,0:T(8,128)(2,1)S(1)} all-gather(bf16[272,384]{1,0:T(8,128)(2,1)} %get-tuple-element.77), channel_id=2, replica_groups=mesh['dp'=8,'fsdp'=4] {'fsdp'}, dimensions={0}, use_global_device_ids=true | all-gather | bytes 1044480 | tf_op jit(solution)/shard_map/all_gather | solution.py:822
  24.8 2.5 %collective-permute-start.3 = (bf16[4,112,384]{2,1,0:T(8,128)(2,1)S(1)}, bf16[4,112,384]{2,1,0:T(8,128)(2,1)S(1)}, u32[]{:S(2)}, u32[]{:S(2)}) collective-permute-start(bf16[4,112,384]{2,1,0:T(8,128)(2,1)S(1)} %slice.48), channel_id=1, source_target_pairs={{0,24},{4,28},{8,16},{12,20},{16,8},{20,12},{24,0},{28,4},{1,25},{... | collective-permute-start | bytes 1032200 | tf_op jit(solution)/shard_map/ppermute | solution.py:755
  27.4 0.5 collective-permute-start.2
  27.9 0.5 collective-permute-start.1
  28.4 0.7 add_select_fusion
  29.2 0.7 reshape.110.targets.refs_7_
  29.9 0.9 copy-done.18
  30.8 20.1 %front.1 = (f32[4224,384]{1,0:T(8,128)}, bf16[4224,1152]{1,0:T(8,128)(2,1)}, bf16[4224,384]{1,0:T(8,128)(2,1)}, bf16[4224,384]{1,0:T(8,128)(2,1)}, bf16[64,80,76...) custom-call(s32[1]{0:T(128)S(6)} %select_n.60.core.refs_17_, ...), custom_call_target="tpu_custom_call" | custom-call | flops 25200001024 | bytes 56000000 | tf_op jit(solution)/shard_map/front/pallas_call | solution.py:363
  51.1 0.5 collective-permute-start.5
  51.6 0.6 broadcast_in_dim.19.up_b
  52.2 0.5 collective-permute-done.4.refs_3_
  52.7 0.5 collective-permute-done.5.refs_4_
  53.2 0.5 collective-permute-done.6.refs_5_
  53.7 0.2 copy-done.23
  53.9 0.5 copy-done.24
  54.4 58.0 %middle.1 = (bf16[4224,384]{1,0:T(8,128)(2,1)}, f32[4224,384]{1,0:T(8,128)}, bf16[4224,384]{1,0:T(8,128)(2,1)}, bf16[1728,384]{1,0:T(8,128)(2,1)}, bf16[1728,384...) custom-call(s32[1]{0:T(128)} %bitcast.spot, f32[4224,384]{1,0:T(8,128)} %get-tuple-element.78.entry.refs_0_, ...), custom_call_target="tpu_custom_call" | custom-call | flops 49500000256 | bytes 110000000 | tf_op jit(solution)/shard_map/middle/pallas_call | solution.py:485
  112.4 0.2 collective-permute-start.7
  112.6 3.1 %collective-permute-done.7 = bf16[1728,384]{1,0:T(8,128)(2,1)S(1)} collective-permute-done((bf16[1728,384]{1,0:T(8,128)(2,1)}, bf16[1728,384]{1,0:T(8,128)(2,1)S(1)}, u32[]{:S(2)}, u32[]{:S(2)}) %collective-permute-start.7) | collective-permute-done | bytes 1327136 | tf_op jit(solution)/shard_map/ppermute | solution.py:755
  115.7 1.4 fusion.2
  117.2 2.5 %collective-permute-start.10 = (bf16[432,384]{1,0:T(8,128)(2,1)S(1)}, bf16[432,384]{1,0:T(8,128)(2,1)S(1)}, u32[]{:S(2)}, u32[]{:S(2)}) collective-permute-start(bf16[432,384]{1,0:T(8,128)(2,1)S(1)} %get-tuple-element.136), channel_id=1, source_target_pairs={{0,24},{4,28},{8,16},{12,20},{16,8},{20,12},{24,0},{28,4},{1,25},{... | collective-permute-start | bytes 995336 | tf_op jit(solution)/shard_map/ppermute | solution.py:755
  119.7 0.5 collective-permute-start.9
  120.2 0.6 collective-permute-start.8
  120.7 18.8 %back.2 = (bf16[4224,384]{1,0:T(8,128)(2,1)}, f32[384,1152]{1,0:T(8,128)}, f32[128,384]{1,0:T(8,128)}, f32[16,256]{1,0:T(8,128)}, f32[8,384]{1,0:T(8,128)}) custom-call(f32[4224,384]{1,0:T(8,128)} %get-tuple-element.78.entry.refs_0_, bf16[4224,1152]{1,0:T(8,128)(2,1)} %get-tuple-element.86.refs_1_, bf16[4224,384]{1,0:T(8,128)(2,1)} %get-tuple-element.80.mixture.refs_2_, ...), custom_call_target="tpu_custom_call" | custom-call | flops 17999998976 | bytes 40000000 | tf_op jit(solution)/shard_map/back/pallas_call | solution.py:653
  139.6 1.2 fusion.5
  140.8 0.9 collective-permute-start.12
  141.7 1.3 collective-permute-start.11
  143.0 19.6 %back.3 = (bf16[4224,384]{1,0:T(8,128)(2,1)}, bf16[704,384]{1,0:T(8,128)(2,1)}, bf16[704,384]{1,0:T(8,128)(2,1)}) custom-call(f32[4224,384]{1,0:T(8,128)} %get-tuple-element.78.entry.refs_0_, bf16[4224,1152]{1,0:T(8,128)(2,1)} %get-tuple-element.86.refs_1_, bf16[4224,384]{1,0:T(8,128)(2,1)} %get-tuple-element.80.mixture.refs_2_, ...), custom_call_target="tpu_custom_call", output_to_operand_aliasing={{0}: (12, {})} | custom-call | flops 17999998976 | bytes 40000000 | tf_op jit(solution)/shard_map/back/pallas_call | solution.py:653
  162.7 0.8 collective-permute-start.16
  163.6 2.2 %collective-permute-start.13 = (bf16[216,384]{1,0:T(8,128)(2,1)S(1)}, bf16[216,384]{1,0:T(8,128)(2,1)S(1)}, u32[]{:S(2)}, u32[]{:S(2)}) collective-permute-start(bf16[216,384]{1,0:T(8,128)(2,1)S(1)} %add_convert_fusion.6), channel_id=1, source_target_pairs={{0,2},{1,3},{2,0},{3,1},{4,6},{5,7},{6,4},{7,5},{8,10},{9,11},{10,... | collective-permute-start | bytes 497672 | tf_op jit(solution)/shard_map/ppermute | solution.py:782
  165.8 1.2 fusion.13
  166.9 1.5 collective-permute-start.19
  168.4 1.5 collective-permute-start.20
  169.9 0.5 collective-permute-start.15
  170.5 1.6 collective-permute-done.16
  172.2 2.4 %collective-permute-done.13 = bf16[216,384]{1,0:T(8,128)(2,1)S(1)} collective-permute-done((bf16[216,384]{1,0:T(8,128)(2,1)S(1)}, bf16[216,384]{1,0:T(8,128)(2,1)S(1)}, u32[]{:S(2)}, u32[]{:S(2)}) %collective-permute-start.13) | collective-permute-done | bytes 165920 | tf_op jit(solution)/shard_map/ppermute | solution.py:782
  174.5 1.8 collective-permute-done.15
  176.3 0.1 collective-permute-done.20
  176.5 1.0 fusion.11
  177.5 0.4 collective-permute-start.21
  177.9 1.6 collective-permute-start.23
  179.5 3.0 %collective-permute-done.21 = bf16[176,384]{1,0:T(8,128)(2,1)S(1)} collective-permute-done((bf16[176,384]{1,0:T(8,128)(2,1)S(1)}, bf16[176,384]{1,0:T(8,128)(2,1)S(1)}, u32[]{:S(2)}, u32[]{:S(2)}) %collective-permute-start.21) | collective-permute-done | bytes 135200 | tf_op jit(solution)/shard_map/ppermute | solution.py:782
  182.6 0.9 collective-permute-start.22
  183.5 1.5 collective-permute-start.18
  185.0 0.6 collective-permute-start.17
  185.6 4.2 %collective-permute-done.22 = bf16[176,384]{1,0:T(8,128)(2,1)S(1)} collective-permute-done((bf16[176,384]{1,0:T(8,128)(2,1)S(1)}, bf16[176,384]{1,0:T(8,128)(2,1)S(1)}, u32[]{:S(2)}, u32[]{:S(2)}) %collective-permute-start.22) | collective-permute-done | bytes 135200 | tf_op jit(solution)/shard_map/ppermute | solution.py:782
  189.9 1.6 collective-permute-start.30
  191.5 1.3 collective-permute-start.29
  192.8 2.1 %collective-permute-done.18.refs_2_ = bf16[432,384]{1,0:T(8,128)(2,1)S(1)} collective-permute-done((bf16[432,384]{1,0:T(8,128)(2,1)S(1)}, bf16[432,384]{1,0:T(8,128)(2,1)S(1)}, u32[]{:S(2)}, u32[]{:S(2)}) %collective-permute-start.18) | collective-permute-done | bytes 331808 | tf_op jit(solution)/shard_map/ppermute | solution.py:755
  194.9 0.7 collective-permute-done.17.refs_1_
  195.7 0.5 collective-permute-start.25
  196.2 1.7 collective-permute-done.30.refs_11_
  197.9 1.2 collective-permute-start.28
  199.1 1.2 collective-permute-done.29.refs_10_
  200.3 2.6 %collective-permute-done.28.refs_9_ = bf16[176,384]{1,0:T(8,128)(2,1)S(1)} collective-permute-done((bf16[176,384]{1,0:T(8,128)(2,1)S(1)}, bf16[176,384]{1,0:T(8,128)(2,1)S(1)}, u32[]{:S(2)}, u32[]{:S(2)}) %collective-permute-start.28) | collective-permute-done | bytes 135200 | tf_op jit(solution)/shard_map/ppermute | solution.py:755
  202.9 0.5 collective-permute-start.32
  203.4 0.8 collective-permute-done.33.refs_14_
  204.3 0.2 collective-permute-done.32.refs_13_
  204.6 0.3 copy-done.15
  204.9 0.2 copy-done.16
  205.1 0.1 copy-done.7
  205.3 0.1 copy-done.8
  205.4 0.7 copy-done.9
  206.1 5.8 %close.1 = (f32[384,1536]{1,0:T(8,128)}, f32[1536,384]{1,0:T(8,128)}, f32[384,384]{1,0:T(8,128)}, f32[384,1152]{1,0:T(8,128)}, f32[128,384]{1,0:T(8,128)}, /*ind...) custom-call(s32[1]{0:T(128)} %bitcast.spot, ...), custom_call_target="tpu_custom_call" | custom-call | tf_op jit(solution)/shard_map/close/pallas_call | solution.py:718
  (81 shorter events, 0.9 us)
Async XLA Ops:
  24.8 5.1 %copy-start = (bf16[1088,384]{1,0:T(8,128)(2,1)}, bf16[1088,384]{1,0:T(8,128)(2,1)S(1)}, u32[]{:S(2)}) copy-start(bf16[1088,384]{1,0:T(8,128)(2,1)S(1)} %all-gather) | copy-start | bytes 2506756
  24.8 5.1 %collective-permute-start = (bf16[4,272,384]{2,1,0:T(8,128)(2,1)S(1)}, bf16[4,272,384]{2,1,0:T(8,128)(2,1)S(1)}, u32[]{:S(2)}, u32[]{:S(2)}) collective-permute-start(bf16[4,272,384]{2,1,0:T(8,128)(2,1)S(1)} %bitcast.43), channel_id=1, source_target_pairs={{0,4},{4,0},{8,12},{12,8},{16,20},{20,16},{24,28},{28,24},{1,5},{5... | collective-permute-start | bytes 2506760 | tf_op jit(solution)/shard_map/ppermute | solution.py:755
  24.8 26.1 %collective-permute-start.3 = (bf16[4,112,384]{2,1,0:T(8,128)(2,1)S(1)}, bf16[4,112,384]{2,1,0:T(8,128)(2,1)S(1)}, u32[]{:S(2)}, u32[]{:S(2)}) collective-permute-start(bf16[4,112,384]{2,1,0:T(8,128)(2,1)S(1)} %slice.48), channel_id=1, source_target_pairs={{0,24},{4,28},{8,16},{12,20},{16,8},{20,12},{24,0},{28,4},{1,25},{... | collective-permute-start | bytes 1032200 | tf_op jit(solution)/shard_map/ppermute | solution.py:755
  27.4 23.6 %collective-permute-start.2 = (bf16[4,112,384]{2,1,0:T(8,128)(2,1)S(1)}, bf16[4,112,384]{2,1,0:T(8,128)(2,1)S(1)}, u32[]{:S(2)}, u32[]{:S(2)}) collective-permute-start(bf16[4,112,384]{2,1,0:T(8,128)(2,1)S(1)} %slice.48), channel_id=1, source_target_pairs={{0,16},{4,20},{8,24},{12,28},{16,0},{20,4},{24,8},{28,12},{1,17},{... | collective-permute-start | bytes 1032200 | tf_op jit(solution)/shard_map/ppermute | solution.py:755
  27.9 23.1 %collective-permute-start.1 = (bf16[4,112,384]{2,1,0:T(8,128)(2,1)S(1)}, bf16[4,112,384]{2,1,0:T(8,128)(2,1)S(1)}, u32[]{:S(2)}, u32[]{:S(2)}) collective-permute-start(bf16[4,112,384]{2,1,0:T(8,128)(2,1)S(1)} %slice.48), channel_id=1, source_target_pairs={{0,8},{4,12},{8,0},{12,4},{16,24},{20,28},{24,16},{28,20},{1,9},{5... | collective-permute-start | bytes 1032200 | tf_op jit(solution)/shard_map/ppermute | solution.py:755
  29.9 0.9 copy-start.18
  30.8 20.9 %copy-start.17 = (f32[1536]{0:T(1024)S(1)}, f32[1536]{0:T(1024)}, u32[]{:S(2)}) copy-start(f32[1536]{0:T(1024)} %param.38) | copy-start | bytes 18436
  50.9 2.8 %copy-start.19 = (bf16[4,112,384]{2,1,0:T(8,128)(2,1)}, bf16[4,112,384]{2,1,0:T(8,128)(2,1)S(1)}, u32[]{:S(2)}) copy-start(bf16[4,112,384]{2,1,0:T(8,128)(2,1)S(1)} %collective-permute-done.3.refs_2_) | copy-start | bytes 1032196
  51.0 2.7 %copy-start.20 = (bf16[4,112,384]{2,1,0:T(8,128)(2,1)}, bf16[4,112,384]{2,1,0:T(8,128)(2,1)S(1)}, u32[]{:S(2)}) copy-start(bf16[4,112,384]{2,1,0:T(8,128)(2,1)S(1)} %collective-permute-done.2.refs_1_) | copy-start | bytes 1032196
  51.0 2.7 %copy-start.21 = (bf16[4,112,384]{2,1,0:T(8,128)(2,1)}, bf16[4,112,384]{2,1,0:T(8,128)(2,1)S(1)}, u32[]{:S(2)}) copy-start(bf16[4,112,384]{2,1,0:T(8,128)(2,1)S(1)} %collective-permute-done.1.refs_0_) | copy-start | bytes 1032196
  51.0 1.7 collective-permute-start.4
  51.1 2.1 %collective-permute-start.5 = (bf16[4,112,384]{2,1,0:T(8,128)(2,1)S(1)}, bf16[4,112,384]{2,1,0:T(8,128)(2,1)S(1)}, u32[]{:S(2)}, u32[]{:S(2)}) collective-permute-start(bf16[4,112,384]{2,1,0:T(8,128)(2,1)S(1)} %collective-permute-done.2.refs_1_), channel_id=1, source_target_pairs={{0,4},{4,0},{8,12},{12,8},{16,20},{20,16},{24,28},{28,24},{1,5},{5... | collective-permute-start | bytes 1032200 | tf_op jit(solution)/shard_map/ppermute | solution.py:755
  51.6 2.1 %collective-permute-start.6 = (bf16[4,112,384]{2,1,0:T(8,128)(2,1)S(1)}, bf16[4,112,384]{2,1,0:T(8,128)(2,1)S(1)}, u32[]{:S(2)}, u32[]{:S(2)}) collective-permute-start(bf16[4,112,384]{2,1,0:T(8,128)(2,1)S(1)} %collective-permute-done.3.refs_2_), channel_id=1, source_target_pairs={{0,4},{4,0},{8,12},{12,8},{16,20},{20,16},{24,28},{28,24},{1,5},{5... | collective-permute-start | bytes 1032200 | tf_op jit(solution)/shard_map/ppermute | solution.py:755
  52.7 1.0 copy-start.22
  53.2 0.7 copy-start.23
  53.7 0.7 copy-start.24
  112.4 3.3 %collective-permute-start.7 = (bf16[1728,384]{1,0:T(8,128)(2,1)}, bf16[1728,384]{1,0:T(8,128)(2,1)S(1)}, u32[]{:S(2)}, u32[]{:S(2)}) collective-permute-start(bf16[1728,384]{1,0:T(8,128)(2,1)} %get-tuple-element.89), channel_id=1, source_target_pairs={{0,4},{4,0},{8,12},{12,8},{16,20},{20,16},{24,28},{28,24},{1,5},{5... | collective-permute-start | bytes 3981320 | tf_op jit(solution)/shard_map/ppermute | solution.py:755
  117.2 22.3 %collective-permute-start.10 = (bf16[432,384]{1,0:T(8,128)(2,1)S(1)}, bf16[432,384]{1,0:T(8,128)(2,1)S(1)}, u32[]{:S(2)}, u32[]{:S(2)}) collective-permute-start(bf16[432,384]{1,0:T(8,128)(2,1)S(1)} %get-tuple-element.136), channel_id=1, source_target_pairs={{0,24},{4,28},{8,16},{12,20},{16,8},{20,12},{24,0},{28,4},{1,25},{... | collective-permute-start | bytes 995336 | tf_op jit(solution)/shard_map/ppermute | solution.py:755
  119.7 19.9 %collective-permute-start.9 = (bf16[432,384]{1,0:T(8,128)(2,1)S(1)}, bf16[432,384]{1,0:T(8,128)(2,1)S(1)}, u32[]{:S(2)}, u32[]{:S(2)}) collective-permute-start(bf16[432,384]{1,0:T(8,128)(2,1)S(1)} %get-tuple-element.137), channel_id=1, source_target_pairs={{0,16},{4,20},{8,24},{12,28},{16,0},{20,4},{24,8},{28,12},{1,17},{... | collective-permute-start | bytes 995336 | tf_op jit(solution)/shard_map/ppermute | solution.py:755
  120.2 19.4 %collective-permute-start.8 = (bf16[432,384]{1,0:T(8,128)(2,1)S(1)}, bf16[432,384]{1,0:T(8,128)(2,1)S(1)}, u32[]{:S(2)}, u32[]{:S(2)}) collective-permute-start(bf16[432,384]{1,0:T(8,128)(2,1)S(1)} %get-tuple-element.138), channel_id=1, source_target_pairs={{0,8},{4,12},{8,0},{12,4},{16,24},{20,28},{24,16},{28,20},{1,9},{5... | collective-permute-start | bytes 995336 | tf_op jit(solution)/shard_map/ppermute | solution.py:755
  140.8 21.8 %collective-permute-start.12 = (bf16[216,384]{1,0:T(8,128)(2,1)S(1)}, bf16[216,384]{1,0:T(8,128)(2,1)S(1)}, u32[]{:S(2)}, u32[]{:S(2)}) collective-permute-start(bf16[216,384]{1,0:T(8,128)(2,1)S(1)} %get-tuple-element.135), channel_id=1, source_target_pairs={{0,2},{1,3},{2,0},{3,1},{4,6},{5,7},{6,4},{7,5},{8,10},{9,11},{10,... | collective-permute-start | bytes 497672 | tf_op jit(solution)/shard_map/ppermute | solution.py:782
  141.7 20.9 %collective-permute-start.11 = (bf16[216,384]{1,0:T(8,128)(2,1)S(1)}, bf16[216,384]{1,0:T(8,128)(2,1)S(1)}, u32[]{:S(2)}, u32[]{:S(2)}) collective-permute-start(bf16[216,384]{1,0:T(8,128)(2,1)S(1)} %get-tuple-element.134), channel_id=1, source_target_pairs={{0,1},{1,0},{2,3},{3,2},{4,5},{5,4},{6,7},{7,6},{8,9},{9,8},{10,11... | collective-permute-start | bytes 497672 | tf_op jit(solution)/shard_map/ppermute | solution.py:782
  162.6 3.2 %collective-permute-start.14 = (bf16[704,384]{1,0:T(8,128)(2,1)}, bf16[704,384]{1,0:T(8,128)(2,1)S(1)}, u32[]{:S(2)}, u32[]{:S(2)}) collective-permute-start(bf16[704,384]{1,0:T(8,128)(2,1)} %get-tuple-element.112), channel_id=1, source_target_pairs={{0,4},{4,0},{8,12},{12,8},{16,20},{20,16},{24,28},{28,24},{1,5},{5... | collective-permute-start | bytes 1622024 | tf_op jit(solution)/shard_map/ppermute | solution.py:755
  162.7 9.4 %collective-permute-start.16 = (bf16[216,384]{1,0:T(8,128)(2,1)S(1)}, bf16[216,384]{1,0:T(8,128)(2,1)S(1)}, u32[]{:S(2)}, u32[]{:S(2)}) collective-permute-start(bf16[216,384]{1,0:T(8,128)(2,1)S(1)} %add_convert_fusion.4), channel_id=1, source_target_pairs={{0,1},{1,0},{2,3},{3,2},{4,5},{5,4},{6,7},{7,6},{8,9},{9,8},{10,11... | collective-permute-start | bytes 497672 | tf_op jit(solution)/shard_map/ppermute | solution.py:782
  163.6 10.9 %collective-permute-start.13 = (bf16[216,384]{1,0:T(8,128)(2,1)S(1)}, bf16[216,384]{1,0:T(8,128)(2,1)S(1)}, u32[]{:S(2)}, u32[]{:S(2)}) collective-permute-start(bf16[216,384]{1,0:T(8,128)(2,1)S(1)} %add_convert_fusion.6), channel_id=1, source_target_pairs={{0,2},{1,3},{2,0},{3,1},{4,6},{5,7},{6,4},{7,5},{8,10},{9,11},{10,... | collective-permute-start | bytes 497672 | tf_op jit(solution)/shard_map/ppermute | solution.py:782
  166.9 9.4 %collective-permute-start.19 = (bf16[176,384]{1,0:T(8,128)(2,1)S(1)}, bf16[176,384]{1,0:T(8,128)(2,1)S(1)}, u32[]{:S(2)}, u32[]{:S(2)}) collective-permute-start(bf16[176,384]{1,0:T(8,128)(2,1)S(1)} %get-tuple-element.139), channel_id=1, source_target_pairs={{0,8},{4,12},{8,0},{12,4},{16,24},{20,28},{24,16},{28,20},{1,9},{5... | collective-permute-start | bytes 405512 | tf_op jit(solution)/shard_map/ppermute | solution.py:755
  168.4 8.0 %collective-permute-start.20 = (bf16[176,384]{1,0:T(8,128)(2,1)S(1)}, bf16[176,384]{1,0:T(8,128)(2,1)S(1)}, u32[]{:S(2)}, u32[]{:S(2)}) collective-permute-start(bf16[176,384]{1,0:T(8,128)(2,1)S(1)} %get-tuple-element.140), channel_id=1, source_target_pairs={{0,16},{4,20},{8,24},{12,28},{16,0},{20,4},{24,8},{28,12},{1,17},{... | collective-permute-start | bytes 405512 | tf_op jit(solution)/shard_map/ppermute | solution.py:755
  169.9 6.4 %collective-permute-start.15 = (bf16[176,384]{1,0:T(8,128)(2,1)S(1)}, bf16[176,384]{1,0:T(8,128)(2,1)S(1)}, u32[]{:S(2)}, u32[]{:S(2)}) collective-permute-start(bf16[176,384]{1,0:T(8,128)(2,1)S(1)} %get-tuple-element.141), channel_id=1, source_target_pairs={{0,24},{4,28},{8,16},{12,20},{16,8},{20,12},{24,0},{28,4},{1,25},{... | collective-permute-start | bytes 405512 | tf_op jit(solution)/shard_map/ppermute | solution.py:755
  177.5 5.1 %collective-permute-start.21 = (bf16[176,384]{1,0:T(8,128)(2,1)S(1)}, bf16[176,384]{1,0:T(8,128)(2,1)S(1)}, u32[]{:S(2)}, u32[]{:S(2)}) collective-permute-start(bf16[176,384]{1,0:T(8,128)(2,1)S(1)} %fusion.11), channel_id=1, source_target_pairs={{0,1},{1,0},{2,3},{3,2},{4,5},{5,4},{6,7},{7,6},{8,9},{9,8},{10,11... | collective-permute-start | bytes 405512 | tf_op jit(solution)/shard_map/ppermute | solution.py:782
  177.9 26.6 %copy-start.1 = (bf16[432,384]{1,0:T(8,128)(2,1)}, bf16[432,384]{1,0:T(8,128)(2,1)S(1)}, u32[]{:S(2)}) copy-start(bf16[432,384]{1,0:T(8,128)(2,1)S(1)} %pad_maximum_fusion.refs_0_) | copy-start | bytes 995332
  177.9 11.8 %collective-permute-start.23 = (bf16[432,384]{1,0:T(8,128)(2,1)S(1)}, bf16[432,384]{1,0:T(8,128)(2,1)S(1)}, u32[]{:S(2)}, u32[]{:S(2)}) collective-permute-start(bf16[432,384]{1,0:T(8,128)(2,1)S(1)} %pad_maximum_fusion.refs_0_), channel_id=1, source_target_pairs={{0,24},{4,28},{8,16},{12,20},{16,8},{20,12},{24,0},{28,4},{1,25},{... | collective-permute-start | bytes 995336 | tf_op jit(solution)/shard_map/ppermute | solution.py:755
  182.6 7.2 %collective-permute-start.22 = (bf16[176,384]{1,0:T(8,128)(2,1)S(1)}, bf16[176,384]{1,0:T(8,128)(2,1)S(1)}, u32[]{:S(2)}, u32[]{:S(2)}) collective-permute-start(bf16[176,384]{1,0:T(8,128)(2,1)S(1)} %add_convert_fusion.8), channel_id=1, source_target_pairs={{0,2},{1,3},{2,0},{3,1},{4,6},{5,7},{6,4},{7,5},{8,10},{9,11},{10,... | collective-permute-start | bytes 405512 | tf_op jit(solution)/shard_map/ppermute | solution.py:782
  183.5 8.0 %collective-permute-start.24 = (bf16[432,384]{1,0:T(8,128)(2,1)S(1)}, bf16[432,384]{1,0:T(8,128)(2,1)S(1)}, u32[]{:S(2)}, u32[]{:S(2)}) collective-permute-start(bf16[432,384]{1,0:T(8,128)(2,1)S(1)} %pad_maximum_fusion.refs_0_), channel_id=1, source_target_pairs={{0,4},{4,0},{8,12},{12,8},{16,20},{20,16},{24,28},{28,24},{1,5},{5... | collective-permute-start | bytes 995336 | tf_op jit(solution)/shard_map/ppermute | solution.py:755
  183.5 11.4 %collective-permute-start.18 = (bf16[432,384]{1,0:T(8,128)(2,1)S(1)}, bf16[432,384]{1,0:T(8,128)(2,1)S(1)}, u32[]{:S(2)}, u32[]{:S(2)}) collective-permute-start(bf16[432,384]{1,0:T(8,128)(2,1)S(1)} %pad_maximum_fusion.refs_0_), channel_id=1, source_target_pairs={{0,16},{4,20},{8,24},{12,28},{16,0},{20,4},{24,8},{28,12},{1,17},{... | collective-permute-start | bytes 995336 | tf_op jit(solution)/shard_map/ppermute | solution.py:755
  185.0 10.6 %collective-permute-start.17 = (bf16[432,384]{1,0:T(8,128)(2,1)S(1)}, bf16[432,384]{1,0:T(8,128)(2,1)S(1)}, u32[]{:S(2)}, u32[]{:S(2)}) collective-permute-start(bf16[432,384]{1,0:T(8,128)(2,1)S(1)} %pad_maximum_fusion.refs_0_), channel_id=1, source_target_pairs={{0,8},{4,12},{8,0},{12,4},{16,24},{20,28},{24,16},{28,20},{1,9},{5... | collective-permute-start | bytes 995336 | tf_op jit(solution)/shard_map/ppermute | solution.py:755
  189.7 14.8 %copy-start.3 = (bf16[432,384]{1,0:T(8,128)(2,1)}, bf16[432,384]{1,0:T(8,128)(2,1)S(1)}, u32[]{:S(2)}) copy-start(bf16[432,384]{1,0:T(8,128)(2,1)S(1)} %collective-permute-done.23.refs_3_) | copy-start | bytes 995332
  189.8 14.7 %copy-start.2 = (bf16[176,384]{1,0:T(8,128)(2,1)}, bf16[176,384]{1,0:T(8,128)(2,1)S(1)}, u32[]{:S(2)}) copy-start(bf16[176,384]{1,0:T(8,128)(2,1)S(1)} %add_convert_fusion.7.refs_8_) | copy-start | bytes 405508
  189.8 5.9 %collective-permute-start.31 = (bf16[176,384]{1,0:T(8,128)(2,1)S(1)}, bf16[176,384]{1,0:T(8,128)(2,1)S(1)}, u32[]{:S(2)}, u32[]{:S(2)}) collective-permute-start(bf16[176,384]{1,0:T(8,128)(2,1)S(1)} %add_convert_fusion.7.refs_8_), channel_id=1, source_target_pairs={{0,4},{4,0},{8,12},{12,8},{16,20},{20,16},{24,28},{28,24},{1,5},{5... | collective-permute-start | bytes 405512 | tf_op jit(solution)/shard_map/ppermute | solution.py:755
  189.9 8.0 %collective-permute-start.30 = (bf16[176,384]{1,0:T(8,128)(2,1)S(1)}, bf16[176,384]{1,0:T(8,128)(2,1)S(1)}, u32[]{:S(2)}, u32[]{:S(2)}) collective-permute-start(bf16[176,384]{1,0:T(8,128)(2,1)S(1)} %add_convert_fusion.7.refs_8_), channel_id=1, source_target_pairs={{0,24},{4,28},{8,16},{12,20},{16,8},{20,12},{24,0},{28,4},{1,25},{... | collective-permute-start | bytes 405512 | tf_op jit(solution)/shard_map/ppermute | solution.py:755
  191.5 13.1 %copy-start.4 = (bf16[432,384]{1,0:T(8,128)(2,1)}, bf16[432,384]{1,0:T(8,128)(2,1)S(1)}, u32[]{:S(2)}) copy-start(bf16[432,384]{1,0:T(8,128)(2,1)S(1)} %collective-permute-done.24.refs_4_) | copy-start | bytes 995332
  191.5 8.8 %collective-permute-start.29 = (bf16[176,384]{1,0:T(8,128)(2,1)S(1)}, bf16[176,384]{1,0:T(8,128)(2,1)S(1)}, u32[]{:S(2)}, u32[]{:S(2)}) collective-permute-start(bf16[176,384]{1,0:T(8,128)(2,1)S(1)} %add_convert_fusion.7.refs_8_), channel_id=1, source_target_pairs={{0,16},{4,20},{8,24},{12,28},{16,0},{20,4},{24,8},{28,12},{1,17},{... | collective-permute-start | bytes 405512 | tf_op jit(solution)/shard_map/ppermute | solution.py:755
  194.9 9.6 %copy-start.5 = (bf16[432,384]{1,0:T(8,128)(2,1)}, bf16[432,384]{1,0:T(8,128)(2,1)S(1)}, u32[]{:S(2)}) copy-start(bf16[432,384]{1,0:T(8,128)(2,1)S(1)} %collective-permute-done.18.refs_2_) | copy-start | bytes 995332
  194.9 9.6 %collective-permute-start.27 = (bf16[432,384]{1,0:T(8,128)(2,1)S(1)}, bf16[432,384]{1,0:T(8,128)(2,1)S(1)}, u32[]{:S(2)}, u32[]{:S(2)}) collective-permute-start(bf16[432,384]{1,0:T(8,128)(2,1)S(1)} %collective-permute-done.23.refs_3_), channel_id=1, source_target_pairs={{0,4},{4,0},{8,12},{12,8},{16,20},{20,16},{24,28},{28,24},{1,5},{5... | collective-permute-start | bytes 995336 | tf_op jit(solution)/shard_map/ppermute | solution.py:755
  195.6 8.9 %copy-start.6 = (bf16[432,384]{1,0:T(8,128)(2,1)}, bf16[432,384]{1,0:T(8,128)(2,1)S(1)}, u32[]{:S(2)}) copy-start(bf16[432,384]{1,0:T(8,128)(2,1)S(1)} %collective-permute-done.17.refs_1_) | copy-start | bytes 995332
  195.7 8.8 %collective-permute-start.26 = (bf16[432,384]{1,0:T(8,128)(2,1)S(1)}, bf16[432,384]{1,0:T(8,128)(2,1)S(1)}, u32[]{:S(2)}, u32[]{:S(2)}) collective-permute-start(bf16[432,384]{1,0:T(8,128)(2,1)S(1)} %collective-permute-done.18.refs_2_), channel_id=1, source_target_pairs={{0,4},{4,0},{8,12},{12,8},{16,20},{20,16},{24,28},{28,24},{1,5},{5... | collective-permute-start | bytes 995336 | tf_op jit(solution)/shard_map/ppermute | solution.py:755
  195.7 8.9 %copy-start.10 = (bf16[176,384]{1,0:T(8,128)(2,1)}, bf16[176,384]{1,0:T(8,128)(2,1)S(1)}, u32[]{:S(2)}) copy-start(bf16[176,384]{1,0:T(8,128)(2,1)S(1)} %collective-permute-done.31.refs_12_) | copy-start | bytes 405508
  195.7 8.8 %collective-permute-start.25 = (bf16[432,384]{1,0:T(8,128)(2,1)S(1)}, bf16[432,384]{1,0:T(8,128)(2,1)S(1)}, u32[]{:S(2)}, u32[]{:S(2)}) collective-permute-start(bf16[432,384]{1,0:T(8,128)(2,1)S(1)} %collective-permute-done.17.refs_1_), channel_id=1, source_target_pairs={{0,4},{4,0},{8,12},{12,8},{16,20},{20,16},{24,28},{28,24},{1,5},{5... | collective-permute-start | bytes 995336 | tf_op jit(solution)/shard_map/ppermute | solution.py:755
  197.9 6.7 %copy-start.11 = (bf16[176,384]{1,0:T(8,128)(2,1)}, bf16[176,384]{1,0:T(8,128)(2,1)S(1)}, u32[]{:S(2)}) copy-start(bf16[176,384]{1,0:T(8,128)(2,1)S(1)} %collective-permute-done.30.refs_11_) | copy-start | bytes 405508
  197.9 5.0 %collective-permute-start.28 = (bf16[176,384]{1,0:T(8,128)(2,1)S(1)}, bf16[176,384]{1,0:T(8,128)(2,1)S(1)}, u32[]{:S(2)}, u32[]{:S(2)}) collective-permute-start(bf16[176,384]{1,0:T(8,128)(2,1)S(1)} %add_convert_fusion.7.refs_8_), channel_id=1, source_target_pairs={{0,8},{4,12},{8,0},{12,4},{16,24},{20,28},{24,16},{28,20},{1,9},{5... | collective-permute-start | bytes 405512 | tf_op jit(solution)/shard_map/ppermute | solution.py:755
  200.3 4.3 %copy-start.12 = (bf16[176,384]{1,0:T(8,128)(2,1)}, bf16[176,384]{1,0:T(8,128)(2,1)S(1)}, u32[]{:S(2)}) copy-start(bf16[176,384]{1,0:T(8,128)(2,1)S(1)} %collective-permute-done.29.refs_10_) | copy-start | bytes 405508
  200.3 2.6 %collective-permute-start.34 = (bf16[176,384]{1,0:T(8,128)(2,1)S(1)}, bf16[176,384]{1,0:T(8,128)(2,1)S(1)}, u32[]{:S(2)}, u32[]{:S(2)}) collective-permute-start(bf16[176,384]{1,0:T(8,128)(2,1)S(1)} %collective-permute-done.30.refs_11_), channel_id=1, source_target_pairs={{0,4},{4,0},{8,12},{12,8},{16,20},{20,16},{24,28},{28,24},{1,5},{5... | collective-permute-start | bytes 405512 | tf_op jit(solution)/shard_map/ppermute | solution.py:755
  202.9 1.7 copy-start.13
  202.9 1.4 collective-permute-start.33
  202.9 1.7 copy-start.14
  202.9 1.5 collective-permute-start.32
  204.3 0.7 copy-start.15
  204.5 0.7 copy-start.16
  204.5 0.8 copy-start.7
  204.5 0.9 copy-start.8
  205.4 0.7 copy-start.9

commit v4 on v3

--- a/solution.py
+++ b/solution.py
@@ -55,10 +55,16 @@
     return centred * scale, scale
 
 
-def hidden_column(targets, rows):
-    row_ids = lax.broadcasted_iota(jnp.int32, (rows, targets.shape[1]), 0)
-    hits = jnp.where(row_ids == targets, 1.0, 0.0)
-    return jnp.max(hits, axis=1, keepdims=True)
+def hidden_column(targets):
+    windows = []
+    for cloud in range(TILE):
+        rows = lax.broadcasted_iota(jnp.int32, (WIN, targets.shape[1]), 0) + cloud * STEP
+        windows.append(jnp.where(rows == targets[cloud : cloud + 1], 1.0, 0.0))
+    blocks = [windows[0][:STEP]]
+    for cloud in range(1, TILE):
+        blocks += [windows[cloud][:16] + windows[cloud - 1][STEP:], windows[cloud][16:STEP]]
+    blocks.append(windows[-1][STEP:])
+    return jnp.max(jnp.concatenate(blocks, axis=0), axis=1, keepdims=True)
 
 
 def lane_mask(rows, odd, kind=bf16):
@@ -102,10 +108,19 @@
     return jnp.where(rows == lanes, value, 0.0).astype(bf16)
 
 
-def pack_kernel(spot, proj, joint, out, up, down, *refs):
-    vectors, (packed, vec, early, late) = refs[:8], refs[8:]
+def pack_kernel(spot, counts, index, proj, joint, out, up, down, up_bias, *refs):
+    vectors, (packed, vec, up_b, targets, early, late, turned) = refs[:8], refs[8:]
     for at, vector in enumerate(vectors):
         vec[at : at + 1, :] = vector[...].reshape(1, D)
+    up_b[...] = up_bias[...].reshape(1, FF)
+    most, clouds = index.shape
+    slots = lax.broadcasted_iota(jnp.int32, (1, 128), 1)
+    turned[...] = jnp.zeros(turned.shape, f32)
+    turned[:most, :clouds] = index[...].astype(f32)
+    chosen = turned[...].T.astype(jnp.int32)
+    for cloud in range(clouds):
+        first = 1 + SEQ * (cloud % TILE)
+        targets[cloud : cloud + 1, :] = jnp.where(slots < counts[cloud], chosen[cloud : cloud + 1, :] + first, -1)
     rows = joint.shape[0]
     for part in range(3):
         early[part * rows : part * rows + rows, :] = joint[:, part * D : part * D + D]
@@ -116,26 +131,29 @@
     late[5 * rows : 5 * rows + down.shape[0], :] = down[...]
     half = early.shape[0] // 2
     piece = packed.shape[0] - half
+    chips = late.shape[0] // piece // 2
     packed[:half, :] = early[pl.ds(pl.multiple_of((spot[0] % 2) * half, 16), half), :]
-    chips = late.shape[0] // piece // 2
     own = (spot[0] % 2) * chips + spot[0] // 2
     packed[half:, :] = late[pl.ds(pl.multiple_of(own * piece, 16), piece), :]
 
 
-def pack(spot, proj, joint, out, up, down, vectors, parts):
+def pack(spot, counts, index, proj, joint, out, up, down, up_bias, vectors, parts):
     rows, low, deep = joint.shape[0], proj.shape[0], down.shape[0]
     size = 3 * rows + low
     late = padded(5 * rows + deep, parts)
     vmem = pl.BlockSpec(memory_space=pltpu.VMEM)
     return pl.pallas_call(
         pack_kernel,
-        in_specs=[pl.BlockSpec(memory_space=pltpu.SMEM)] + [vmem] * 13,
-        out_specs=[vmem, vmem],
-        out_shape=[shape_of((size // 2 + late // parts, D), bf16), shape_of((8, D), f32)],
-        scratch_shapes=[pltpu.VMEM((size, D), bf16), pltpu.VMEM((late, D), bf16)],
+        in_specs=[pl.BlockSpec(memory_space=pltpu.SMEM)] * 2 + [vmem] * 15,
+        out_specs=[vmem] * 4,
+        out_shape=[
+            shape_of((size // 2 + late // parts, D), bf16), shape_of((8, D), f32), shape_of((1, FF), f32),
+            shape_of((counts.shape[0], 128), jnp.int32),
+        ],
+        scratch_shapes=[pltpu.VMEM((size, D), bf16), pltpu.VMEM((late, D), bf16), pltpu.VMEM((128, 128), f32)],
         compiler_params=settings(),
         name="pack",
-    )(spot, proj, joint, out, up, down, *vectors)
+    )(spot, counts, index, proj, joint, out, up, down, up_bias, *vectors)
 
 
 def unpack_early(core, mine, other, joint_w, proj):
@@ -247,9 +265,9 @@
         pre = dot(cen[step * SUBS + sub], place_w[...], TN)
         low = (pre * cdf(pre)).astype(bf16)
         placed = dot(low, proj[...]) + vec[1:2, :]
-        hidden = hidden_column(targets[sub], ROWS)
+        hidden = hidden_column(targets[sub * TILE : sub * TILE + TILE, :])
         rows = jnp.where(hidden > 0.5, vec[0:1, :], tokens[span, :].astype(f32)) + placed
-        entry[span, :] = rows
+        entry[span, :] = rows.astype(bf16)
         unit, _ = normalised(rows)
         return (unit * vec[2:3, :] + vec[3:4, :]).astype(bf16)
 
@@ -365,7 +383,7 @@
         grid=(steps // SUBS,),
         in_specs=[
             pl.BlockSpec(memory_space=pltpu.SMEM), rows_of(D, rows), whole(centers.shape),
-            pl.BlockSpec((SUBS, 1, 256), lambda i: (i, 0, 0)), whole((8, D)),
+            pl.BlockSpec((SUBS * TILE, 128), lambda i: (i, 0)), whole((8, D)),
             whole((3, POSH)), whole((1, POSH)), whole(mine.shape), whole(other.shape),
         ],
         out_specs=[
@@ -374,7 +392,7 @@
             whole((steps, 16, ROWS)), whole((16, POSH)),
         ],
         out_shape=[
-            shape_of((count, D), f32), shape_of((count, 3 * D), bf16),
+            shape_of((count, D), bf16), shape_of((count, 3 * D), bf16),
             shape_of((count, D), bf16), shape_of((count, D), bf16),
             shape_of((steps * TILE, WIN, HEADS * KEYS), bf16), shape_of((D, 3 * D), bf16), shape_of((POSH, D), bf16),
             shape_of((steps, 16, ROWS), bf16), shape_of((16, POSH), bf16),
@@ -425,7 +443,7 @@
     spans = [slice(part * chunk, part * chunk + chunk) for part in range(parts)]
     mix = mixture[...]
     cotangent = cot[...]
-    mid = entry[...] + (dot(mix, out_w[...]) + vec[4:5, :])
+    mid = entry[...].astype(f32) + (dot(mix, out_w[...]) + vec[4:5, :])
     gates = [dot(cotangent, down_w[spans[0], :], NT)]
     unit, scale = normalised(mid)
     normed = (unit * vec[5:6, :] + vec[6:7, :]).astype(bf16)
@@ -459,8 +477,8 @@
     upstream = cotangent.astype(f32)
     tilted = back * vec[5:6, :]
     grad = upstream + scale * (tilted - row_mean(tilted) - unit * row_mean(tilted * unit))
-    mid_grad[...] = grad
     low = grad.astype(bf16)
+    mid_grad[...] = low
     mix_grad[...] = (dot(low, out_w[...], NT) * shares[...].astype(f32)).astype(bf16)
     out_acc[...] += dot(mix, low, TN)
     vec_g[0:1, :] += jnp.sum(back * unit, axis=0, keepdims=True)
@@ -479,7 +497,7 @@
         share_halves(spot[0] % 2, sums, kept, sent)
 
 
-def middle_part(spot, entry, mixture, shares, cot, vec, up_b, mine, other, near, near_other, order, rows=1056, chunk=512):
+def middle_part(spot, entry, mixture, shares, cot, vec, up_b, mine, other, near, near_other, order, rows=704, chunk=768):
     count = entry.shape[0]
     size = padded(9 * D, len(order))
     return pl.pallas_call(
@@ -495,7 +513,7 @@
             whole((size // 2, D)), whole((size // 2, D)), whole((1, FF)), whole((8, D)),
         ],
         out_shape=[
-            shape_of((count, D), bf16), shape_of((count, D), f32), shape_of((count, D), bf16),
+            shape_of((count, D), bf16), shape_of((count, D), bf16), shape_of((count, D), bf16),
             shape_of((size // 2, D), bf16), shape_of((size // 2, D), bf16), shape_of((1, FF), f32), shape_of((8, D), f32),
         ],
         scratch_shapes=[
@@ -529,7 +547,7 @@
 
     qkv[:ROWS, :] = joint[...]
     pre = dot(cen[0], place_w[...], TN)
-    unit, scale = normalised(entry[...])
+    unit, scale = normalised(entry[...].astype(f32))
     normed = (unit * vec[2:3, :] + vec[3:4, :]).astype(bf16)
     minus = lane_ones(-1.0)
     jobs = [(pair, cloud) for pair in range(PAIRS) for cloud in range(TILE)]
@@ -577,13 +595,13 @@
     back = dot(dqkv[...], joint_w[...], NT)
     joint_g[...] += dot(normed, dqkv[...], TN)
     tilted = back * vec[2:3, :]
-    grad = mid_grad[...] + scale * (tilted - row_mean(tilted) - unit * row_mean(tilted * unit))
+    grad = mid_grad[...].astype(f32) + scale * (tilted - row_mean(tilted) - unit * row_mean(tilted * unit))
     low = grad.astype(bf16)
     mass = cdf(pre)
     place_low = (pre * mass).astype(bf16)
     pre_grad = dot(low, proj[...], NT) * smooth_slope(pre, mass)
     proj_g[...] += dot(place_low, low, TN)
-    hidden = hidden_column(targets[0], ROWS)
+    hidden = hidden_column(targets[...])
     marked = jnp.where(hidden > 0.5, grad, 0.0)
     tokens_g[...] = (grad - marked).astype(bf16)
     high_part = pre_grad.astype(bf16)
@@ -631,7 +649,8 @@
     in_specs = [
         shifted(D), shifted(3 * D), shifted(D),
         pl.BlockSpec((TILE, WIN, HEADS * KEYS), lambda i: (i + first, 0, 0)),
-        shifted(D), shifted(D), shifted_slab((16, ROWS)), shifted_slab((1, 256)),
+        shifted(D), shifted(D), shifted_slab((16, ROWS)),
+        pl.BlockSpec((TILE, 128), lambda i: (i + first, 0)),
         whole((8, D)), whole((16, POSH)), whole((POSH, D)), whole((D, 3 * D)),
     ]
     given = list(given)
@@ -664,35 +683,36 @@
     )(*given)
 
 
-def marked_targets(mask_count, mask_index):
-    clouds, most = mask_index.shape
-    slot = jnp.arange(most, dtype=jnp.int32)[None, :]
-    cloud = (jnp.arange(clouds, dtype=jnp.int32) % TILE)[:, None]
-    targets = jnp.where(slot < mask_count[:, None], mask_index + (1 + SEQ * cloud), -1)
-    return jnp.pad(targets, ((0, 0), (0, 32 - most)), constant_values=-1).reshape(clouds // TILE, 1, 256)
-
-
 def gather_pieces(spot, offsets, pieces, sums):
-    segment = pieces[0].shape[0]
-    chips = len(pieces) // 2
-    for offset, piece in zip(offsets, pieces):
-        holder = spot ^ offset
-        row = pl.multiple_of(((holder % 2) * chips + holder // 2) * segment, 16)
-        sums[pl.ds(row, segment), :] = piece[...]
-
-
-def close_kernel(offsets, spot, *refs):
-    count = len(offsets)
-    first_pieces, last_pieces, refs = refs[:count], refs[count : 2 * count], refs[2 * count :]
-    up_g, down_g, out_g, joint_g, proj_g, place_g, *small = refs[:-2]
-    sums, last = refs[-2:]
+    segment = pieces[0].shape[0] // len(offsets)
+    chips = len(offsets)
+    for core, piece in enumerate(pieces):
+        for at, offset in enumerate(offsets):
+            holder = spot ^ offset ^ core
+            row = pl.multiple_of(((holder % 2) * chips + holder // 2) * segment, 16)
+            sums[pl.ds(row, segment), :] = piece[at * segment : at * segment + segment, :]
+
+
+def widen_kernel(offsets, spot, *refs):
+    pieces, (up_g, down_g, out_g, sums) = refs[:2], refs[2:]
     step = pl.program_id(0)
 
     @pl.when(step == 0)
     def _():
-        gather_pieces(spot[0], offsets, first_pieces, sums)
-        gather_pieces(spot[0], offsets, last_pieces, last)
+        gather_pieces(spot[0], offsets, pieces, sums)
         out_g[...] = sums[8 * D : 9 * D, :].astype(f32)
+
+    up_g[...] = sums[pl.ds(pl.multiple_of(step * D, 16), D), :].astype(f32)
+    down_g[...] = sums[pl.ds(pl.multiple_of((step + 4) * D, 16), D), :].astype(f32)
+
+
+def close_kernel(offsets, spot, *refs):
+    pieces, (joint_g, proj_g, place_g, *small), last = refs[:2], refs[2:-1], refs[-1]
+    step = pl.program_id(0)
+
+    @pl.when(step == 0)
+    def _():
+        gather_pieces(spot[0], offsets, pieces, last)
         proj_g[...] = last[3 * D : 3 * D + POSH, :].astype(f32)
         rows = last[3 * D + POSH : 3 * D + POSH + 16, :].astype(f32)
         for part in range(3):
@@ -702,37 +722,36 @@
         for at in range(8):
             small[2 + at][...] = rows[at : at + 1].reshape(D)
 
-    up_g[...] = sums[pl.ds(pl.multiple_of(step * D, 16), D), :].astype(f32)
-    down_g[...] = sums[pl.ds(pl.multiple_of((step + 4) * D, 16), D), :].astype(f32)
-    joint_g[...] = last[pl.ds(pl.multiple_of(jnp.minimum(step, 2) * D, 16), D), :].astype(f32)
-
-
-def close(spot, first, last):
-    pieces = [*first.values(), *last.values()]
-    count = len(first)
-
-    def one(shape):
-        return pl.BlockSpec(shape, lambda i: (0,) * len(shape))
-
-    flat = [(POSH,), (FF,)] + [(D,)] * 8
+    joint_g[...] = last[pl.ds(pl.multiple_of(step * D, 16), D), :].astype(f32)
+
+
+def one(shape):
+    return pl.BlockSpec(shape, lambda i: (0,) * len(shape))
+
+
+def unpacked(kernel, name, steps, shapes, specs, spot, offsets, values):
     return pl.pallas_call(
-        functools.partial(close_kernel, list(first)),
-        grid=(4,),
-        in_specs=[pl.BlockSpec(memory_space=pltpu.SMEM)] + [one(piece.shape) for piece in pieces],
-        out_specs=[
-            pl.BlockSpec((D, D), lambda i: (0, i)), pl.BlockSpec((D, D), lambda i: (i, 0)), one((D, D)),
-            pl.BlockSpec((D, D), lambda i: (0, jnp.minimum(i, 2))), one((POSH, D)), one((3, POSH)),
-        ]
-        + [one(shape) for shape in flat],
-        out_shape=[
-            shape_of(shape, f32) for shape in [(D, FF), (FF, D), (D, D), (D, 3 * D), (POSH, D), (3, POSH)] + flat
-        ],
-        scratch_shapes=[
-            pltpu.VMEM((pieces[0].shape[0] * count, D), bf16), pltpu.VMEM((pieces[-1].shape[0] * count, D), bf16),
-        ],
+        functools.partial(kernel, offsets),
+        grid=(steps,),
+        in_specs=[pl.BlockSpec(memory_space=pltpu.SMEM)] + [one(value.shape) for value in values],
+        out_specs=specs,
+        out_shape=[shape_of(shape, f32) for shape in shapes],
+        scratch_shapes=[pltpu.VMEM((values[0].shape[0] * 2, D), bf16)],
         compiler_params=settings(),
-        name="close",
-    )(spot, *pieces)
+        cost_estimate=cost(4),
+        name=name,
+    )(spot, *values)
+
+
+def widen(spot, offsets, values):
+    specs = [pl.BlockSpec((D, D), lambda i: (0, i)), pl.BlockSpec((D, D), lambda i: (i, 0)), one((D, D))]
+    return unpacked(widen_kernel, "widen", 4, [(D, FF), (FF, D), (D, D)], specs, spot, offsets, values)
+
+
+def close(spot, offsets, values):
+    shapes = [(POSH, D), (3, POSH), (POSH,), (FF,)] + [(D,)] * 8
+    specs = [pl.BlockSpec((D, D), lambda i: (0, i))] + [one(shape) for shape in shapes]
+    return unpacked(close_kernel, "close", 3, [(D, 3 * D)] + shapes, specs, spot, offsets, values)
 
 
 def bits_of(size):
@@ -818,14 +837,14 @@
     spot = lax.axis_index("dp").astype(jnp.int32)[None]
     core = spot % 2
     vectors = (mask_embed, place_shift, norm_gain, norm_shift, out_bias, mlp_gain, mlp_shift, down_bias)
-    packed, vec = pack(spot, place_proj, joint_weight, out_weight, up_weight, down_weight, vectors, dp)
+    packed, vec, up_b, targets = pack(
+        spot, mask_count, mask_index.T, place_proj, joint_weight, out_weight, up_weight, down_weight, up_bias, vectors, dp
+    )
     packed = lax.all_gather(packed, "fsdp", axis=0)
     packed_other = swapped(packed, 1, dp)
     half = (3 * joint_weight.shape[0] + place_proj.shape[0]) // 2
     late = packed[:, half:]
     pieces = [swapped(late, 2 * offset, dp) for offset in range(1, dp // 2)]
-    targets = marked_targets(mask_count, mask_index)
-    up_b = up_bias[None, :]
     entry, joint, mixture, shares, weights, joint_w, proj, cen, place_w = front(
         core, tokens, centers, targets, vec, place_weight, place_bias[None, :], packed, packed_other
     )
@@ -868,14 +887,18 @@
         sums = joined(sums, bits, dp)
     value = total([value, near_got])
     far_got = crossed(value, far, fsdp)
-    newest = list(sums)[-1]
-    far_got, sums[newest] = tied(far_got, sums[newest])
+    soonest = list(sums)[1]
+    far_got, sums[soonest] = tied(far_got, sums[soonest])
     last = {0: total([value, far_got])}
     for bits in reversed(chips):
         last = joined(last, bits, dp)
-    sums, last = joined(sums, [1], dp), joined(last, [1], dp)
-    up_grad, down_grad, out_grad, joint_grad, proj_grad, place_weight_grad, place_bias_grad, up_bias_grad, *small = close(
-        spot, sums, last
+    held = jnp.concatenate(list(sums.values()), axis=0)
+    up_grad, down_grad, out_grad = widen(spot, list(sums), [held, swapped(held, 1, dp)])
+    newest = list(last)[-1]
+    last[newest] = after(last[newest], out_grad)
+    held = jnp.concatenate(list(last.values()), axis=0)
+    joint_grad, proj_grad, place_weight_grad, place_bias_grad, up_bias_grad, *small = close(
+        spot, list(last), [held, swapped(held, 1, dp)]
     )
     return (
         output,

time: 212 us -> 207 us (0.976)
  starting transfers between devices: 26.9 us -> 24.7 us
    pallas_call x1, Pallas kernels: 58 us -> 54.7 us  [middle_part(): pl.pallas_call(functools.partial(middle_kernel, chunk, order), grid=(coun...]
    pallas_call x1 -> x2, Pallas kernels: 5.81 us -> 7.83 us  [unpacked(): pl.pallas_call(functools.partial(kernel, offsets), grid=(steps,), in_spec...]
    ppermute x29 -> x23, starting transfers between devices: 20.5 us -> 18.8 us  [swapped(): return lax.ppermute(values, 'dp', [(i, i ^ offset) for i in range(size)])]
    ppermute x29 -> x23, waiting for transfers between devices: 15.9 us -> 17 us  [swapped(): return lax.ppermute(values, 'dp', [(i, i ^ offset) for i in range(size)])]
    convert_element_type x10 -> x8, other arithmetic: 5.1 us -> 5 us  [total(): return sum((term.astype(f32) for term in terms)).astype(bf16)]
  transfers between devices with their start and end apart: 35 -> 29, of which waited for: 17 -> 13; matrix products, arithmetic and copies ran while one was open for 2% -> 1% of each run, Pallas kernels for 28% -> 30%
where the time goes in v4:
time: 207 us
  Pallas kernels  122 us (59%)
  waiting for transfers between devices  27.4 us (13%)
  starting transfers between devices  24.7 us (12%)
  blocking collectives  22.1 us (11%)
  other arithmetic  5.21 us (3%)
  local copies, waits for them, and re-layouts  3.76 us (2%)
    pallas_call x1, Pallas kernels, middle_part(): pl.pallas_call(functools.partial(middle_kernel, chunk, order), grid=(coun...  54.7 us
    pallas_call x2, Pallas kernels, back_part(): pl.pallas_call(functools.partial(back_kernel, before is None, extra is no...  37.8 us
    all_gather x1, blocking collectives, per_device(): packed = lax.all_gather(packed, 'fsdp', axis=0)  22.1 us
    pallas_call x1, Pallas kernels, front(): pl.pallas_call(front_kernel, grid=(steps // SUBS,), in_specs=[pl.BlockSpe...  19.9 us
    ppermute x23, starting transfers between devices, swapped(): return lax.ppermute(values, 'dp', [(i, i ^ offset) for i in range(size)])  18.8 us
    ppermute x23, waiting for transfers between devices, swapped(): return lax.ppermute(values, 'dp', [(i, i ^ offset) for i in range(size)])  17 us
    ppermute x6, waiting for transfers between devices, crossed(): return lax.ppermute(values, 'fsdp', [(i, i ^ offset) for i in range(size)])  10.4 us
    pallas_call x2, Pallas kernels, unpacked(): pl.pallas_call(functools.partial(kernel, offsets), grid=(steps,), in_spec...  7.83 us
  transfers between devices with their start and end apart: 29, of which 13 were waited for; matrix products, arithmetic and copies ran while one was open for 1% of the time, Pallas kernels for 30%

profile of v4, /device:TPU:0, one launch (start us, length us, event | category | flops | bytes accessed | tf_op | source)
XLA Modules:
  0.0 206.5 jit_solution(11288268404880843583)
XLA Ops:
  0.7 2.1 %pack.1 = (bf16[272,384]{1,0:T(8,128)(2,1)}, f32[8,384]{1,0:T(8,128)}, f32[1,1536]{1,0:T(1,128)}, s32[64,128]{1,0:T(8,128)}) custom-call(s32[1]{0:T(128)} %bitcast.spot, s32[64]{0:T(128)} %counts.1, s32[28,64]{1,0:T(8,128)} %bitcast.56, bf16[32,384]{1,0:T(8,128)(2,1)} %proj.1, bf16[96,1152]{1,0:T(8,128)(2,1)} %joint.1, bf16[96,384]{1,0:T(8,128)(2,1)} %out.1, ...), custom_call_target="tpu_custom_call" | custom-call | tf_op jit(solution)/shard_map/pack/pallas_call | solution.py:145
  2.8 22.1 %all-gather = bf16[1088,384]{1,0:T(8,128)(2,1)S(1)} all-gather(bf16[272,384]{1,0:T(8,128)(2,1)} %get-tuple-element.81), channel_id=2, replica_groups=mesh['dp'=8,'fsdp'=4] {'fsdp'}, dimensions={0}, use_global_device_ids=true | all-gather | bytes 1044480 | tf_op jit(solution)/shard_map/all_gather | solution.py:843
  24.9 2.5 %collective-permute-start.3 = (bf16[4,112,384]{2,1,0:T(8,128)(2,1)S(1)}, bf16[4,112,384]{2,1,0:T(8,128)(2,1)S(1)}, u32[]{:S(2)}, u32[]{:S(2)}) collective-permute-start(bf16[4,112,384]{2,1,0:T(8,128)(2,1)S(1)} %slice.48), channel_id=1, source_target_pairs={{0,24},{4,28},{8,16},{12,20},{16,8},{20,12},{24,0},{28,4},{1,25},{... | collective-permute-start | bytes 1032200 | tf_op jit(solution)/shard_map/ppermute | solution.py:774
  27.4 0.5 collective-permute-start.2
  27.9 0.5 collective-permute-start.1
  28.5 0.9 copy-done.4
  29.4 19.9 %front.1 = (bf16[4224,384]{1,0:T(8,128)(2,1)}, bf16[4224,1152]{1,0:T(8,128)(2,1)}, bf16[4224,384]{1,0:T(8,128)(2,1)}, bf16[4224,384]{1,0:T(8,128)(2,1)}, bf16[64...) custom-call(s32[1]{0:T(128)S(6)} %select_n.46.core.refs_17_, ...), custom_call_target="tpu_custom_call" | custom-call | flops 25200001024 | bytes 56000000 | tf_op jit(solution)/shard_map/front/pallas_call | solution.py:381
  49.3 0.0 copy-start.8
  49.3 0.1 collective-permute-start.4
  49.4 0.5 collective-permute-start.5
  49.9 0.1 collective-permute-start.6
  50.0 1.1 collective-permute-done.4.refs_3_
  51.0 0.5 collective-permute-done.5.refs_4_
  51.5 0.5 collective-permute-done.6.refs_5_
  52.0 0.2 copy-done.10
  52.3 0.5 copy-done.11
  52.8 54.7 %middle.1 = (bf16[4224,384]{1,0:T(8,128)(2,1)}, bf16[4224,384]{1,0:T(8,128)(2,1)}, bf16[4224,384]{1,0:T(8,128)(2,1)}, bf16[1728,384]{1,0:T(8,128)(2,1)}, bf16[17...) custom-call(s32[1]{0:T(128)} %bitcast.spot, bf16[4224,384]{1,0:T(8,128)(2,1)} %get-tuple-element.82.entry.refs_0_, ...), custom_call_target="tpu_custom_call" | custom-call | flops 49500000256 | bytes 110000000 | tf_op jit(solution)/shard_map/middle/pallas_call | solution.py:503
  107.5 0.2 collective-permute-start.7
  107.7 3.1 %collective-permute-done.7 = bf16[1728,384]{1,0:T(8,128)(2,1)S(1)} collective-permute-done((bf16[1728,384]{1,0:T(8,128)(2,1)}, bf16[1728,384]{1,0:T(8,128)(2,1)S(1)}, u32[]{:S(2)}, u32[]{:S(2)}) %collective-permute-start.7) | collective-permute-done | bytes 1327136 | tf_op jit(solution)/shard_map/ppermute | solution.py:774
  110.8 1.4 fusion.2
  112.3 2.5 %collective-permute-start.10 = (bf16[432,384]{1,0:T(8,128)(2,1)S(1)}, bf16[432,384]{1,0:T(8,128)(2,1)S(1)}, u32[]{:S(2)}, u32[]{:S(2)}) collective-permute-start(bf16[432,384]{1,0:T(8,128)(2,1)S(1)} %get-tuple-element.146), channel_id=1, source_target_pairs={{0,24},{4,28},{8,16},{12,20},{16,8},{20,12},{24,0},{28,4},{1,25},{... | collective-permute-start | bytes 995336 | tf_op jit(solution)/shard_map/ppermute | solution.py:774
  114.8 0.5 collective-permute-start.9
  115.3 0.6 collective-permute-start.8
  115.8 18.6 %back.2 = (bf16[4224,384]{1,0:T(8,128)(2,1)}, f32[384,1152]{1,0:T(8,128)}, f32[128,384]{1,0:T(8,128)}, f32[16,256]{1,0:T(8,128)}, f32[8,384]{1,0:T(8,128)}) custom-call(bf16[4224,384]{1,0:T(8,128)(2,1)} %get-tuple-element.82.entry.refs_0_, bf16[4224,1152]{1,0:T(8,128)(2,1)} %get-tuple-element.91.refs_1_, ...), custom_call_target="tpu_custom_call" | custom-call | flops 17999998976 | bytes 40000000 | tf_op jit(solution)/shard_map/back/pallas_call | solution.py:672
  134.4 1.2 fusion.5
  135.7 0.9 collective-permute-start.12
  136.6 1.3 collective-permute-start.11
  137.9 19.2 %back.3 = (bf16[4224,384]{1,0:T(8,128)(2,1)}, bf16[704,384]{1,0:T(8,128)(2,1)}, bf16[704,384]{1,0:T(8,128)(2,1)}) custom-call(bf16[4224,384]{1,0:T(8,128)(2,1)} %get-tuple-element.82.entry.refs_0_, bf16[4224,1152]{1,0:T(8,128)(2,1)} %get-tuple-element.91.refs_1_, ...), custom_call_target="tpu_custom_call", output_to_operand_aliasing={{0}: (12, {})} | custom-call | flops 17999998976 | bytes 40000000 | tf_op jit(solution)/shard_map/back/pallas_call | solution.py:672
  157.2 0.1 collective-permute-start.13
  157.3 0.9 collective-permute-start.18
  158.2 1.2 collective-permute-done.13
  159.4 1.1 fusion.12
  160.5 1.5 collective-permute-start.14
  162.0 1.5 collective-permute-start.16
  163.5 0.5 collective-permute-start.15
  164.1 0.9 collective-permute-start.19
  165.0 3.5 %collective-permute-done.18 = bf16[216,384]{1,0:T(8,128)(2,1)S(1)} collective-permute-done((bf16[216,384]{1,0:T(8,128)(2,1)S(1)}, bf16[216,384]{1,0:T(8,128)(2,1)S(1)}, u32[]{:S(2)}, u32[]{:S(2)}) %collective-permute-start.18) | collective-permute-done | bytes 165920 | tf_op jit(solution)/shard_map/ppermute | solution.py:801
  168.5 1.6 collective-permute-done.16
  170.2 1.4 collective-permute-done.15
  171.5 1.0 fusion.11
  172.5 1.0 collective-permute-start.17
  173.5 0.1 constant_dynamic-update-slice_fusion.3
  173.6 0.6 collective-permute-start.25
  174.2 1.4 collective-permute-start.21
  175.7 1.9 collective-permute-done.17
  177.6 1.1 collective-permute-start.20
  178.7 1.4 collective-permute-start.26
  180.1 5.0 %collective-permute-done.20 = bf16[176,384]{1,0:T(8,128)(2,1)S(1)} collective-permute-done((bf16[176,384]{1,0:T(8,128)(2,1)S(1)}, bf16[176,384]{1,0:T(8,128)(2,1)S(1)}, u32[]{:S(2)}, u32[]{:S(2)}) %collective-permute-start.20) | collective-permute-done | bytes 135200 | tf_op jit(solution)/shard_map/ppermute | solution.py:801
  185.1 0.1 constant_dynamic-update-slice_fusion.2
  185.1 0.1 constant_dynamic-update-slice_fusion.1
  185.2 5.3 %collective-permute-done.26 = bf16[432,384]{1,0:T(8,128)(2,1)S(1)} collective-permute-done((bf16[432,384]{1,0:T(8,128)(2,1)S(1)}, bf16[432,384]{1,0:T(8,128)(2,1)S(1)}, u32[]{:S(2)}, u32[]{:S(2)}) %collective-permute-start.26) | collective-permute-done | bytes 331808 | tf_op jit(solution)/shard_map/ppermute | solution.py:774
  190.5 0.1 constant_dynamic-update-slice_fusion.refs_0_
  190.6 0.1 collective-permute-start.27
  190.7 2.2 %collective-permute-start.24 = (bf16[176,384]{1,0:T(8,128)(2,1)S(1)}, bf16[176,384]{1,0:T(8,128)(2,1)S(1)}, u32[]{:S(2)}, u32[]{:S(2)}) collective-permute-start(bf16[176,384]{1,0:T(8,128)(2,1)S(1)} %add_convert_fusion.7), channel_id=1, source_target_pairs={{0,24},{4,28},{8,16},{12,20},{16,8},{20,12},{24,0},{28,4},{1,25},{... | collective-permute-start | bytes 405512 | tf_op jit(solution)/shard_map/ppermute | solution.py:774
  192.9 0.8 collective-permute-start.23
  193.7 0.5 collective-permute-start.22
  194.2 1.1 copy-done.3
  195.3 4.7 %widen.1 = (f32[384,1536]{1,0:T(8,128)}, f32[1536,384]{1,0:T(8,128)}, f32[384,384]{1,0:T(8,128)}) custom-call(s32[1]{0:T(128)} %bitcast.spot, bf16[1728,384]{1,0:T(8,128)(2,1)} %copy-done.2, bf16[1728,384]{1,0:T(8,128)(2,1)} %copy-done.3), custom_call_target="tpu_custom_call" | custom-call | flops 3600000000 | bytes 8000000 | tf_op jit(solution)/shard_map/widen/pallas_call | solution.py:733
  200.1 0.5 collective-permute-done.23
  200.5 0.1 pad_maximum_fusion.refs_0_
  200.6 0.1 collective-permute-start.28
  200.7 1.9 collective-permute-done.28.refs_1_
  202.6 0.8 copy-done.5
  203.4 3.1 %close.1 = (f32[384,1152]{1,0:T(8,128)}, f32[128,384]{1,0:T(8,128)}, f32[3,128]{1,0:T(4,128)}, f32[128]{0:T(128)}, f32[1536]{0:T(1024)}, /*index=5*/f32[384]{0:T...) custom-call(s32[1]{0:T(128)} %bitcast.spot, ...), custom_call_target="tpu_custom_call" | custom-call | flops 3600000000 | bytes 8000000 | tf_op jit(solution)/shard_map/close/pallas_call | solution.py:733
  (42 shorter events, 0.4 us)
Async XLA Ops:
  24.9 3.6 %copy-start = (bf16[1088,384]{1,0:T(8,128)(2,1)}, bf16[1088,384]{1,0:T(8,128)(2,1)S(1)}, u32[]{:S(2)}) copy-start(bf16[1088,384]{1,0:T(8,128)(2,1)S(1)} %all-gather) | copy-start | bytes 2506756
  24.9 3.6 %collective-permute-start = (bf16[4,272,384]{2,1,0:T(8,128)(2,1)S(1)}, bf16[4,272,384]{2,1,0:T(8,128)(2,1)S(1)}, u32[]{:S(2)}, u32[]{:S(2)}) collective-permute-start(bf16[4,272,384]{2,1,0:T(8,128)(2,1)S(1)} %bitcast.44), channel_id=1, source_target_pairs={{0,4},{4,0},{8,12},{12,8},{16,20},{20,16},{24,28},{28,24},{1,5},{5... | collective-permute-start | bytes 2506760 | tf_op jit(solution)/shard_map/ppermute | solution.py:774
  24.9 24.3 %collective-permute-start.3 = (bf16[4,112,384]{2,1,0:T(8,128)(2,1)S(1)}, bf16[4,112,384]{2,1,0:T(8,128)(2,1)S(1)}, u32[]{:S(2)}, u32[]{:S(2)}) collective-permute-start(bf16[4,112,384]{2,1,0:T(8,128)(2,1)S(1)} %slice.48), channel_id=1, source_target_pairs={{0,24},{4,28},{8,16},{12,20},{16,8},{20,12},{24,0},{28,4},{1,25},{... | collective-permute-start | bytes 1032200 | tf_op jit(solution)/shard_map/ppermute | solution.py:774
  27.4 21.9 %collective-permute-start.2 = (bf16[4,112,384]{2,1,0:T(8,128)(2,1)S(1)}, bf16[4,112,384]{2,1,0:T(8,128)(2,1)S(1)}, u32[]{:S(2)}, u32[]{:S(2)}) collective-permute-start(bf16[4,112,384]{2,1,0:T(8,128)(2,1)S(1)} %slice.48), channel_id=1, source_target_pairs={{0,16},{4,20},{8,24},{12,28},{16,0},{20,4},{24,8},{28,12},{1,17},{... | collective-permute-start | bytes 1032200 | tf_op jit(solution)/shard_map/ppermute | solution.py:774
  27.9 21.4 %collective-permute-start.1 = (bf16[4,112,384]{2,1,0:T(8,128)(2,1)S(1)}, bf16[4,112,384]{2,1,0:T(8,128)(2,1)S(1)}, u32[]{:S(2)}, u32[]{:S(2)}) collective-permute-start(bf16[4,112,384]{2,1,0:T(8,128)(2,1)S(1)} %slice.48), channel_id=1, source_target_pairs={{0,8},{4,12},{8,0},{12,4},{16,24},{20,28},{24,16},{28,20},{1,9},{5... | collective-permute-start | bytes 1032200 | tf_op jit(solution)/shard_map/ppermute | solution.py:774
  28.5 0.9 copy-start.4
  49.3 2.8 %copy-start.6 = (bf16[4,112,384]{2,1,0:T(8,128)(2,1)}, bf16[4,112,384]{2,1,0:T(8,128)(2,1)S(1)}, u32[]{:S(2)}) copy-start(bf16[4,112,384]{2,1,0:T(8,128)(2,1)S(1)} %collective-permute-done.3.refs_2_) | copy-start | bytes 1032196
  49.3 2.7 %copy-start.7 = (bf16[4,112,384]{2,1,0:T(8,128)(2,1)}, bf16[4,112,384]{2,1,0:T(8,128)(2,1)S(1)}, u32[]{:S(2)}) copy-start(bf16[4,112,384]{2,1,0:T(8,128)(2,1)S(1)} %collective-permute-done.2.refs_1_) | copy-start | bytes 1032196
  49.3 2.7 %copy-start.8 = (bf16[4,112,384]{2,1,0:T(8,128)(2,1)}, bf16[4,112,384]{2,1,0:T(8,128)(2,1)S(1)}, u32[]{:S(2)}) copy-start(bf16[4,112,384]{2,1,0:T(8,128)(2,1)S(1)} %collective-permute-done.1.refs_0_) | copy-start | bytes 1032196
  49.3 1.7 collective-permute-start.4
  49.4 2.1 %collective-permute-start.5 = (bf16[4,112,384]{2,1,0:T(8,128)(2,1)S(1)}, bf16[4,112,384]{2,1,0:T(8,128)(2,1)S(1)}, u32[]{:S(2)}, u32[]{:S(2)}) collective-permute-start(bf16[4,112,384]{2,1,0:T(8,128)(2,1)S(1)} %collective-permute-done.2.refs_1_), channel_id=1, source_target_pairs={{0,4},{4,0},{8,12},{12,8},{16,20},{20,16},{24,28},{28,24},{1,5},{5... | collective-permute-start | bytes 1032200 | tf_op jit(solution)/shard_map/ppermute | solution.py:774
  49.9 2.1 %collective-permute-start.6 = (bf16[4,112,384]{2,1,0:T(8,128)(2,1)S(1)}, bf16[4,112,384]{2,1,0:T(8,128)(2,1)S(1)}, u32[]{:S(2)}, u32[]{:S(2)}) collective-permute-start(bf16[4,112,384]{2,1,0:T(8,128)(2,1)S(1)} %collective-permute-done.3.refs_2_), channel_id=1, source_target_pairs={{0,4},{4,0},{8,12},{12,8},{16,20},{20,16},{24,28},{28,24},{1,5},{5... | collective-permute-start | bytes 1032200 | tf_op jit(solution)/shard_map/ppermute | solution.py:774
  51.0 1.0 copy-start.9
  51.5 0.7 copy-start.10
  52.0 0.7 copy-start.11
  107.5 3.3 %collective-permute-start.7 = (bf16[1728,384]{1,0:T(8,128)(2,1)}, bf16[1728,384]{1,0:T(8,128)(2,1)S(1)}, u32[]{:S(2)}, u32[]{:S(2)}) collective-permute-start(bf16[1728,384]{1,0:T(8,128)(2,1)} %get-tuple-element.94), channel_id=1, source_target_pairs={{0,4},{4,0},{8,12},{12,8},{16,20},{20,16},{24,28},{28,24},{1,5},{5... | collective-permute-start | bytes 3981320 | tf_op jit(solution)/shard_map/ppermute | solution.py:774
  112.3 22.1 %collective-permute-start.10 = (bf16[432,384]{1,0:T(8,128)(2,1)S(1)}, bf16[432,384]{1,0:T(8,128)(2,1)S(1)}, u32[]{:S(2)}, u32[]{:S(2)}) collective-permute-start(bf16[432,384]{1,0:T(8,128)(2,1)S(1)} %get-tuple-element.146), channel_id=1, source_target_pairs={{0,24},{4,28},{8,16},{12,20},{16,8},{20,12},{24,0},{28,4},{1,25},{... | collective-permute-start | bytes 995336 | tf_op jit(solution)/shard_map/ppermute | solution.py:774
  114.8 19.7 %collective-permute-start.9 = (bf16[432,384]{1,0:T(8,128)(2,1)S(1)}, bf16[432,384]{1,0:T(8,128)(2,1)S(1)}, u32[]{:S(2)}, u32[]{:S(2)}) collective-permute-start(bf16[432,384]{1,0:T(8,128)(2,1)S(1)} %get-tuple-element.147), channel_id=1, source_target_pairs={{0,16},{4,20},{8,24},{12,28},{16,0},{20,4},{24,8},{28,12},{1,17},{... | collective-permute-start | bytes 995336 | tf_op jit(solution)/shard_map/ppermute | solution.py:774
  115.3 19.2 %collective-permute-start.8 = (bf16[432,384]{1,0:T(8,128)(2,1)S(1)}, bf16[432,384]{1,0:T(8,128)(2,1)S(1)}, u32[]{:S(2)}, u32[]{:S(2)}) collective-permute-start(bf16[432,384]{1,0:T(8,128)(2,1)S(1)} %get-tuple-element.148), channel_id=1, source_target_pairs={{0,8},{4,12},{8,0},{12,4},{16,24},{20,28},{24,16},{28,20},{1,9},{5... | collective-permute-start | bytes 995336 | tf_op jit(solution)/shard_map/ppermute | solution.py:774
  135.7 21.5 %collective-permute-start.12 = (bf16[216,384]{1,0:T(8,128)(2,1)S(1)}, bf16[216,384]{1,0:T(8,128)(2,1)S(1)}, u32[]{:S(2)}, u32[]{:S(2)}) collective-permute-start(bf16[216,384]{1,0:T(8,128)(2,1)S(1)} %get-tuple-element.145), channel_id=1, source_target_pairs={{0,2},{1,3},{2,0},{3,1},{4,6},{5,7},{6,4},{7,5},{8,10},{9,11},{10,... | collective-permute-start | bytes 497672 | tf_op jit(solution)/shard_map/ppermute | solution.py:801
  136.6 20.5 %collective-permute-start.11 = (bf16[216,384]{1,0:T(8,128)(2,1)S(1)}, bf16[216,384]{1,0:T(8,128)(2,1)S(1)}, u32[]{:S(2)}, u32[]{:S(2)}) collective-permute-start(bf16[216,384]{1,0:T(8,128)(2,1)S(1)} %get-tuple-element.144), channel_id=1, source_target_pairs={{0,1},{1,0},{2,3},{3,2},{4,5},{5,4},{6,7},{7,6},{8,9},{9,8},{10,11... | collective-permute-start | bytes 497672 | tf_op jit(solution)/shard_map/ppermute | solution.py:801
  157.2 2.2 %collective-permute-start.13 = (bf16[704,384]{1,0:T(8,128)(2,1)}, bf16[704,384]{1,0:T(8,128)(2,1)S(1)}, u32[]{:S(2)}, u32[]{:S(2)}) collective-permute-start(bf16[704,384]{1,0:T(8,128)(2,1)} %get-tuple-element.116), channel_id=1, source_target_pairs={{0,4},{4,0},{8,12},{12,8},{16,20},{20,16},{24,28},{28,24},{1,5},{5... | collective-permute-start | bytes 1622024 | tf_op jit(solution)/shard_map/ppermute | solution.py:774
  157.3 11.3 %collective-permute-start.18 = (bf16[216,384]{1,0:T(8,128)(2,1)S(1)}, bf16[216,384]{1,0:T(8,128)(2,1)S(1)}, u32[]{:S(2)}, u32[]{:S(2)}) collective-permute-start(bf16[216,384]{1,0:T(8,128)(2,1)S(1)} %add_convert_fusion.6), channel_id=1, source_target_pairs={{0,2},{1,3},{2,0},{3,1},{4,6},{5,7},{6,4},{7,5},{8,10},{9,11},{10,... | collective-permute-start | bytes 497672 | tf_op jit(solution)/shard_map/ppermute | solution.py:801
  160.5 9.6 %collective-permute-start.14 = (bf16[176,384]{1,0:T(8,128)(2,1)S(1)}, bf16[176,384]{1,0:T(8,128)(2,1)S(1)}, u32[]{:S(2)}, u32[]{:S(2)}) collective-permute-start(bf16[176,384]{1,0:T(8,128)(2,1)S(1)} %get-tuple-element.149), channel_id=1, source_target_pairs={{0,8},{4,12},{8,0},{12,4},{16,24},{20,28},{24,16},{28,20},{1,9},{5... | collective-permute-start | bytes 405512 | tf_op jit(solution)/shard_map/ppermute | solution.py:774
  162.0 8.1 %collective-permute-start.16 = (bf16[176,384]{1,0:T(8,128)(2,1)S(1)}, bf16[176,384]{1,0:T(8,128)(2,1)S(1)}, u32[]{:S(2)}, u32[]{:S(2)}) collective-permute-start(bf16[176,384]{1,0:T(8,128)(2,1)S(1)} %get-tuple-element.150), channel_id=1, source_target_pairs={{0,24},{4,28},{8,16},{12,20},{16,8},{20,12},{24,0},{28,4},{1,25},{... | collective-permute-start | bytes 405512 | tf_op jit(solution)/shard_map/ppermute | solution.py:774
  163.5 8.0 %collective-permute-start.15 = (bf16[176,384]{1,0:T(8,128)(2,1)S(1)}, bf16[176,384]{1,0:T(8,128)(2,1)S(1)}, u32[]{:S(2)}, u32[]{:S(2)}) collective-permute-start(bf16[176,384]{1,0:T(8,128)(2,1)S(1)} %get-tuple-element.151), channel_id=1, source_target_pairs={{0,16},{4,20},{8,24},{12,28},{16,0},{20,4},{24,8},{28,12},{1,17},{... | collective-permute-start | bytes 405512 | tf_op jit(solution)/shard_map/ppermute | solution.py:774
  164.1 9.4 %collective-permute-start.19 = (bf16[216,384]{1,0:T(8,128)(2,1)S(1)}, bf16[216,384]{1,0:T(8,128)(2,1)S(1)}, u32[]{:S(2)}, u32[]{:S(2)}) collective-permute-start(bf16[216,384]{1,0:T(8,128)(2,1)S(1)} %add_convert_fusion.4), channel_id=1, source_target_pairs={{0,1},{1,0},{2,3},{3,2},{4,5},{5,4},{6,7},{7,6},{8,9},{9,8},{10,11... | collective-permute-start | bytes 497672 | tf_op jit(solution)/shard_map/ppermute | solution.py:801
  172.5 5.1 %collective-permute-start.17 = (bf16[176,384]{1,0:T(8,128)(2,1)S(1)}, bf16[176,384]{1,0:T(8,128)(2,1)S(1)}, u32[]{:S(2)}, u32[]{:S(2)}) collective-permute-start(bf16[176,384]{1,0:T(8,128)(2,1)S(1)} %fusion.11), channel_id=1, source_target_pairs={{0,1},{1,0},{2,3},{3,2},{4,5},{5,4},{6,7},{7,6},{8,9},{9,8},{10,11... | collective-permute-start | bytes 405512 | tf_op jit(solution)/shard_map/ppermute | solution.py:801
  173.6 11.5 %collective-permute-start.25 = (bf16[432,384]{1,0:T(8,128)(2,1)S(1)}, bf16[432,384]{1,0:T(8,128)(2,1)S(1)}, u32[]{:S(2)}, u32[]{:S(2)}) collective-permute-start(bf16[432,384]{1,0:T(8,128)(2,1)S(1)} %pad_maximum_fusion.1), channel_id=1, source_target_pairs={{0,16},{4,20},{8,24},{12,28},{16,0},{20,4},{24,8},{28,12},{1,17},{... | collective-permute-start | bytes 995336 | tf_op jit(solution)/shard_map/ppermute | solution.py:774
  174.2 10.8 %collective-permute-start.21 = (bf16[432,384]{1,0:T(8,128)(2,1)S(1)}, bf16[432,384]{1,0:T(8,128)(2,1)S(1)}, u32[]{:S(2)}, u32[]{:S(2)}) collective-permute-start(bf16[432,384]{1,0:T(8,128)(2,1)S(1)} %pad_maximum_fusion.1), channel_id=1, source_target_pairs={{0,8},{4,12},{8,0},{12,4},{16,24},{20,28},{24,16},{28,20},{1,9},{5... | collective-permute-start | bytes 995336 | tf_op jit(solution)/shard_map/ppermute | solution.py:774
  177.6 7.4 %collective-permute-start.20 = (bf16[176,384]{1,0:T(8,128)(2,1)S(1)}, bf16[176,384]{1,0:T(8,128)(2,1)S(1)}, u32[]{:S(2)}, u32[]{:S(2)}) collective-permute-start(bf16[176,384]{1,0:T(8,128)(2,1)S(1)} %add_convert_fusion.8), channel_id=1, source_target_pairs={{0,2},{1,3},{2,0},{3,1},{4,6},{5,7},{6,4},{7,5},{8,10},{9,11},{10,... | collective-permute-start | bytes 405512 | tf_op jit(solution)/shard_map/ppermute | solution.py:801
  178.7 11.8 %collective-permute-start.26 = (bf16[432,384]{1,0:T(8,128)(2,1)S(1)}, bf16[432,384]{1,0:T(8,128)(2,1)S(1)}, u32[]{:S(2)}, u32[]{:S(2)}) collective-permute-start(bf16[432,384]{1,0:T(8,128)(2,1)S(1)} %pad_maximum_fusion.1), channel_id=1, source_target_pairs={{0,24},{4,28},{8,16},{12,20},{16,8},{20,12},{24,0},{28,4},{1,25},{... | collective-permute-start | bytes 995336 | tf_op jit(solution)/shard_map/ppermute | solution.py:774
  190.5 3.7 %copy-start.2 = (bf16[1728,384]{1,0:T(8,128)(2,1)}, bf16[1728,384]{1,0:T(8,128)(2,1)S(1)}, u32[]{:S(2)}) copy-start(bf16[1728,384]{1,0:T(8,128)(2,1)S(1)} %constant_dynamic-update-slice_fusion.refs_0_) | copy-start | bytes 3981316
  190.6 3.7 %collective-permute-start.27 = (bf16[1728,384]{1,0:T(8,128)(2,1)S(1)}, bf16[1728,384]{1,0:T(8,128)(2,1)S(1)}, u32[]{:S(2)}, u32[]{:S(2)}) collective-permute-start(bf16[1728,384]{1,0:T(8,128)(2,1)S(1)} %constant_dynamic-update-slice_fusion.refs_0_), channel_id=1, source_target_pairs={{0,4},{4,0},{8,12},{12,8},{16,20},{20,16},{24,28},{28,24},{1,5},{5... | collective-permute-start | bytes 3981320 | tf_op jit(solution)/shard_map/ppermute | solution.py:774
  190.7 9.4 %collective-permute-start.24 = (bf16[176,384]{1,0:T(8,128)(2,1)S(1)}, bf16[176,384]{1,0:T(8,128)(2,1)S(1)}, u32[]{:S(2)}, u32[]{:S(2)}) collective-permute-start(bf16[176,384]{1,0:T(8,128)(2,1)S(1)} %add_convert_fusion.7), channel_id=1, source_target_pairs={{0,24},{4,28},{8,16},{12,20},{16,8},{20,12},{24,0},{28,4},{1,25},{... | collective-permute-start | bytes 405512 | tf_op jit(solution)/shard_map/ppermute | solution.py:774
  192.9 7.7 %collective-permute-start.23 = (bf16[176,384]{1,0:T(8,128)(2,1)S(1)}, bf16[176,384]{1,0:T(8,128)(2,1)S(1)}, u32[]{:S(2)}, u32[]{:S(2)}) collective-permute-start(bf16[176,384]{1,0:T(8,128)(2,1)S(1)} %add_convert_fusion.7), channel_id=1, source_target_pairs={{0,16},{4,20},{8,24},{12,28},{16,0},{20,4},{24,8},{28,12},{1,17},{... | collective-permute-start | bytes 405512 | tf_op jit(solution)/shard_map/ppermute | solution.py:774
  193.7 6.8 %collective-permute-start.22 = (bf16[176,384]{1,0:T(8,128)(2,1)S(1)}, bf16[176,384]{1,0:T(8,128)(2,1)S(1)}, u32[]{:S(2)}, u32[]{:S(2)}) collective-permute-start(bf16[176,384]{1,0:T(8,128)(2,1)S(1)} %add_convert_fusion.7), channel_id=1, source_target_pairs={{0,8},{4,12},{8,0},{12,4},{16,24},{20,28},{24,16},{28,20},{1,9},{5... | collective-permute-start | bytes 405512 | tf_op jit(solution)/shard_map/ppermute | solution.py:774
  194.2 1.1 copy-start.3
  200.6 2.0 copy-start.1
  200.6 2.0 collective-permute-start.28
  202.6 0.8 copy-start.5

commit v5 on v4

--- a/solution.py
+++ b/solution.py
@@ -21,7 +21,6 @@
 GROUP = 8
 BACK_GROUP = 24
 SUBS = 2
-VMEM = 60 * 2**20
 LOG2E = 1.4426950408889634
 ROOT_HALF = 0.7071067811865476
 PDF = 0.3989422804014327
@@ -370,8 +369,8 @@
     return pl.CostEstimate(flops=int(microseconds * 9e8), bytes_accessed=int(microseconds * 2e6), transcendentals=0)
 
 
-def settings():
-    return pltpu.CompilerParams(vmem_limit_bytes=VMEM)
+def settings(megabytes=60):
+    return pltpu.CompilerParams(vmem_limit_bytes=megabytes * 2**20)
 
 
 def front(core, tokens, centers, targets, vec, place_weight, place_bias, mine, other):
@@ -737,7 +736,7 @@
         out_specs=specs,
         out_shape=[shape_of(shape, f32) for shape in shapes],
         scratch_shapes=[pltpu.VMEM((values[0].shape[0] * 2, D), bf16)],
-        compiler_params=settings(),
+        compiler_params=settings(24),
         cost_estimate=cost(4),
         name=name,
     )(spot, *values)

time: 207 us -> 205 us (level)
  Pallas kernels: 122 us -> 119 us
  waiting for transfers between devices: 27.4 us -> 30.3 us
    pallas_call x2, Pallas kernels: 7.83 us -> 4.9 us  [unpacked(): pl.pallas_call(functools.partial(kernel, offsets), grid=(steps,), in_spec...]
    ppermute x23, waiting for transfers between devices: 17 us -> 19.9 us  [swapped(): return lax.ppermute(values, 'dp', [(i, i ^ offset) for i in range(size)])]
  transfers between devices with their start and end apart: 29 -> 29, of which waited for: 13 -> 14; matrix products, arithmetic and copies ran while one was open for 1% -> 1% of each run, Pallas kernels for 30% -> 30%
where the time goes in v5:
time: 205 us
  Pallas kernels  119 us (58%)
  waiting for transfers between devices  30.3 us (15%)
  starting transfers between devices  24.7 us (12%)
  blocking collectives  22.1 us (11%)
  other arithmetic  5.21 us (3%)
    pallas_call x1, Pallas kernels, middle_part(): pl.pallas_call(functools.partial(middle_kernel, chunk, order), grid=(coun...  54.7 us
    pallas_call x2, Pallas kernels, back_part(): pl.pallas_call(functools.partial(back_kernel, before is None, extra is no...  37.8 us
    all_gather x1, blocking collectives, per_device(): packed = lax.all_gather(packed, 'fsdp', axis=0)  22.1 us
    ppermute x23, waiting for transfers between devices, swapped(): return lax.ppermute(values, 'dp', [(i, i ^ offset) for i in range(size)])  19.9 us
    pallas_call x1, Pallas kernels, front(): pl.pallas_call(front_kernel, grid=(steps // SUBS,), in_specs=[pl.BlockSpe...  19.8 us
    ppermute x23, starting transfers between devices, swapped(): return lax.ppermute(values, 'dp', [(i, i ^ offset) for i in range(size)])  18.8 us
    ppermute x6, waiting for transfers between devices, crossed(): return lax.ppermute(values, 'fsdp', [(i, i ^ offset) for i in range(size)])  10.4 us
    ppermute x6, starting transfers between devices, crossed(): return lax.ppermute(values, 'fsdp', [(i, i ^ offset) for i in range(size)])  5.94 us
  transfers between devices with their start and end apart: 29, of which 14 were waited for; matrix products, arithmetic and copies ran while one was open for 1% of the time, Pallas kernels for 30%

profile of v5, /device:TPU:0, one launch (start us, length us, event | category | flops | bytes accessed | tf_op | source)
XLA Modules:
  0.0 204.5 jit_solution(15348532409813201386)
XLA Ops:
  0.7 2.1 %pack.1 = (bf16[272,384]{1,0:T(8,128)(2,1)}, f32[8,384]{1,0:T(8,128)}, f32[1,1536]{1,0:T(1,128)}, s32[64,128]{1,0:T(8,128)}) custom-call(s32[1]{0:T(128)} %bitcast.spot, s32[64]{0:T(128)} %counts.1, s32[28,64]{1,0:T(8,128)} %bitcast.56, bf16[32,384]{1,0:T(8,128)(2,1)} %proj.1, bf16[96,1152]{1,0:T(8,128)(2,1)} %joint.1, bf16[96,384]{1,0:T(8,128)(2,1)} %out.1, ...), custom_call_target="tpu_custom_call" | custom-call | tf_op jit(solution)/shard_map/pack/pallas_call | solution.py:144
  2.8 22.1 %all-gather = bf16[1088,384]{1,0:T(8,128)(2,1)S(1)} all-gather(bf16[272,384]{1,0:T(8,128)(2,1)} %get-tuple-element.81), channel_id=2, replica_groups=mesh['dp'=8,'fsdp'=4] {'fsdp'}, dimensions={0}, use_global_device_ids=true | all-gather | bytes 1044480 | tf_op jit(solution)/shard_map/all_gather | solution.py:842
  24.9 2.5 %collective-permute-start.3 = (bf16[4,112,384]{2,1,0:T(8,128)(2,1)S(1)}, bf16[4,112,384]{2,1,0:T(8,128)(2,1)S(1)}, u32[]{:S(2)}, u32[]{:S(2)}) collective-permute-start(bf16[4,112,384]{2,1,0:T(8,128)(2,1)S(1)} %slice.48), channel_id=1, source_target_pairs={{0,24},{4,28},{8,16},{12,20},{16,8},{20,12},{24,0},{28,4},{1,25},{... | collective-permute-start | bytes 1032200 | tf_op jit(solution)/shard_map/ppermute | solution.py:773
  27.4 0.5 collective-permute-start.2
  27.9 0.5 collective-permute-start.1
  28.5 0.0 collective-permute-done.other
  28.5 0.9 copy-done.1
  29.4 19.8 %front.1 = (bf16[4224,384]{1,0:T(8,128)(2,1)}, bf16[4224,1152]{1,0:T(8,128)(2,1)}, bf16[4224,384]{1,0:T(8,128)(2,1)}, bf16[4224,384]{1,0:T(8,128)(2,1)}, bf16[64...) custom-call(s32[1]{0:T(128)S(6)} %select_n.46.core.refs_17_, ...), custom_call_target="tpu_custom_call" | custom-call | flops 25200001024 | bytes 56000000 | tf_op jit(solution)/shard_map/front/pallas_call | solution.py:380
  49.3 0.0 copy-start.4
  49.3 0.1 collective-permute-start.4
  49.4 0.5 collective-permute-start.5
  49.9 0.1 collective-permute-start.6
  50.0 1.1 collective-permute-done.4.refs_3_
  51.0 0.5 collective-permute-done.5.refs_4_
  51.5 0.5 collective-permute-done.6.refs_5_
  52.0 0.2 copy-done.6
  52.2 0.5 copy-done.7
  52.7 54.7 %middle.1 = (bf16[4224,384]{1,0:T(8,128)(2,1)}, bf16[4224,384]{1,0:T(8,128)(2,1)}, bf16[4224,384]{1,0:T(8,128)(2,1)}, bf16[1728,384]{1,0:T(8,128)(2,1)}, bf16[17...) custom-call(s32[1]{0:T(128)} %bitcast.spot, bf16[4224,384]{1,0:T(8,128)(2,1)} %get-tuple-element.82.entry.refs_0_, ...), custom_call_target="tpu_custom_call" | custom-call | flops 49500000256 | bytes 110000000 | tf_op jit(solution)/shard_map/middle/pallas_call | solution.py:502
  107.5 0.2 collective-permute-start.7
  107.7 3.1 %collective-permute-done.7 = bf16[1728,384]{1,0:T(8,128)(2,1)S(1)} collective-permute-done((bf16[1728,384]{1,0:T(8,128)(2,1)}, bf16[1728,384]{1,0:T(8,128)(2,1)S(1)}, u32[]{:S(2)}, u32[]{:S(2)}) %collective-permute-start.7) | collective-permute-done | bytes 1327136 | tf_op jit(solution)/shard_map/ppermute | solution.py:773
  110.8 1.4 fusion.2
  112.3 2.5 %collective-permute-start.10 = (bf16[432,384]{1,0:T(8,128)(2,1)S(1)}, bf16[432,384]{1,0:T(8,128)(2,1)S(1)}, u32[]{:S(2)}, u32[]{:S(2)}) collective-permute-start(bf16[432,384]{1,0:T(8,128)(2,1)S(1)} %get-tuple-element.146), channel_id=1, source_target_pairs={{0,24},{4,28},{8,16},{12,20},{16,8},{20,12},{24,0},{28,4},{1,25},{... | collective-permute-start | bytes 995336 | tf_op jit(solution)/shard_map/ppermute | solution.py:773
  114.8 0.5 collective-permute-start.9
  115.3 0.5 collective-permute-start.8
  115.8 18.6 %back.2 = (bf16[4224,384]{1,0:T(8,128)(2,1)}, f32[384,1152]{1,0:T(8,128)}, f32[128,384]{1,0:T(8,128)}, f32[16,256]{1,0:T(8,128)}, f32[8,384]{1,0:T(8,128)}) custom-call(bf16[4224,384]{1,0:T(8,128)(2,1)} %get-tuple-element.82.entry.refs_0_, bf16[4224,1152]{1,0:T(8,128)(2,1)} %get-tuple-element.91.refs_1_, ...), custom_call_target="tpu_custom_call" | custom-call | flops 17999998976 | bytes 40000000 | tf_op jit(solution)/shard_map/back/pallas_call | solution.py:671
  134.4 1.2 fusion.5
  135.7 0.9 collective-permute-start.12
  136.6 1.3 collective-permute-start.11
  137.9 19.2 %back.3 = (bf16[4224,384]{1,0:T(8,128)(2,1)}, bf16[704,384]{1,0:T(8,128)(2,1)}, bf16[704,384]{1,0:T(8,128)(2,1)}) custom-call(bf16[4224,384]{1,0:T(8,128)(2,1)} %get-tuple-element.82.entry.refs_0_, bf16[4224,1152]{1,0:T(8,128)(2,1)} %get-tuple-element.91.refs_1_, ...), custom_call_target="tpu_custom_call", output_to_operand_aliasing={{0}: (12, {})} | custom-call | flops 17999998976 | bytes 40000000 | tf_op jit(solution)/shard_map/back/pallas_call | solution.py:671
  157.2 0.1 collective-permute-start.13
  157.3 0.9 collective-permute-start.18
  158.1 1.2 collective-permute-done.13
  159.4 1.1 fusion.12
  160.5 1.5 collective-permute-start.14
  162.0 1.5 collective-permute-start.16
  163.5 0.5 collective-permute-start.15
  164.1 0.9 collective-permute-start.19
  165.0 3.6 %collective-permute-done.18 = bf16[216,384]{1,0:T(8,128)(2,1)S(1)} collective-permute-done((bf16[216,384]{1,0:T(8,128)(2,1)S(1)}, bf16[216,384]{1,0:T(8,128)(2,1)S(1)}, u32[]{:S(2)}, u32[]{:S(2)}) %collective-permute-start.18) | collective-permute-done | bytes 165920 | tf_op jit(solution)/shard_map/ppermute | solution.py:800
  168.5 1.6 collective-permute-done.16
  170.2 1.4 collective-permute-done.15
  171.5 1.0 fusion.11
  172.5 1.0 collective-permute-start.17
  173.5 0.1 constant_dynamic-update-slice_fusion.3
  173.6 0.6 collective-permute-start.25
  174.2 1.5 collective-permute-start.21
  175.7 1.9 collective-permute-done.17
  177.6 1.1 collective-permute-start.20
  178.7 1.4 collective-permute-start.26
  180.1 5.0 %collective-permute-done.20 = bf16[176,384]{1,0:T(8,128)(2,1)S(1)} collective-permute-done((bf16[176,384]{1,0:T(8,128)(2,1)S(1)}, bf16[176,384]{1,0:T(8,128)(2,1)S(1)}, u32[]{:S(2)}, u32[]{:S(2)}) %collective-permute-start.20) | collective-permute-done | bytes 135200 | tf_op jit(solution)/shard_map/ppermute | solution.py:800
  185.1 0.1 constant_dynamic-update-slice_fusion.2
  185.1 0.1 constant_dynamic-update-slice_fusion.1
  185.2 5.3 %collective-permute-done.26 = bf16[432,384]{1,0:T(8,128)(2,1)S(1)} collective-permute-done((bf16[432,384]{1,0:T(8,128)(2,1)S(1)}, bf16[432,384]{1,0:T(8,128)(2,1)S(1)}, u32[]{:S(2)}, u32[]{:S(2)}) %collective-permute-start.26) | collective-permute-done | bytes 331808 | tf_op jit(solution)/shard_map/ppermute | solution.py:773
  190.5 0.1 constant_dynamic-update-slice_fusion.refs_0_
  190.5 0.1 collective-permute-start.27
  190.7 2.2 %collective-permute-start.24 = (bf16[176,384]{1,0:T(8,128)(2,1)S(1)}, bf16[176,384]{1,0:T(8,128)(2,1)S(1)}, u32[]{:S(2)}, u32[]{:S(2)}) collective-permute-start(bf16[176,384]{1,0:T(8,128)(2,1)S(1)} %add_convert_fusion.7), channel_id=1, source_target_pairs={{0,24},{4,28},{8,16},{12,20},{16,8},{20,12},{24,0},{28,4},{1,25},{... | collective-permute-start | bytes 405512 | tf_op jit(solution)/shard_map/ppermute | solution.py:773
  192.9 0.8 collective-permute-start.23
  193.7 0.5 collective-permute-start.22
  194.2 3.0 %widen.1 = (f32[384,1536]{1,0:T(8,128)}, f32[1536,384]{1,0:T(8,128)}, f32[384,384]{1,0:T(8,128)}) custom-call(s32[1]{0:T(128)} %bitcast.spot, bf16[1728,384]{1,0:T(8,128)(2,1)S(1)} %constant_dynamic-update-slice_fusion.refs_0_, bf16[1728,384]{1,0:T(8,128)(2,1)S(1)} %collective-permute-done.27.refs_1_), custom_call_target="tpu_custom_call" | custom-call | flops 3600000000 | bytes 8000000 | tf_op jit(solution)/shard_map/widen/pallas_call | solution.py:732
  197.2 0.8 collective-permute-done.24
  198.0 2.5 %collective-permute-done.23 = bf16[176,384]{1,0:T(8,128)(2,1)S(1)} collective-permute-done((bf16[176,384]{1,0:T(8,128)(2,1)S(1)}, bf16[176,384]{1,0:T(8,128)(2,1)S(1)}, u32[]{:S(2)}, u32[]{:S(2)}) %collective-permute-start.23) | collective-permute-done | bytes 135200 | tf_op jit(solution)/shard_map/ppermute | solution.py:773
  200.5 0.1 pad_maximum_fusion.refs_0_
  200.6 0.1 collective-permute-start.28
  200.7 1.9 collective-permute-done.28.refs_1_
  202.6 1.9 close.1
  (34 shorter events, 0.3 us)
Async XLA Ops:
  24.9 3.6 %copy-start = (bf16[1088,384]{1,0:T(8,128)(2,1)}, bf16[1088,384]{1,0:T(8,128)(2,1)S(1)}, u32[]{:S(2)}) copy-start(bf16[1088,384]{1,0:T(8,128)(2,1)S(1)} %all-gather) | copy-start | bytes 2506756
  24.9 3.6 %collective-permute-start = (bf16[4,272,384]{2,1,0:T(8,128)(2,1)S(1)}, bf16[4,272,384]{2,1,0:T(8,128)(2,1)S(1)}, u32[]{:S(2)}, u32[]{:S(2)}) collective-permute-start(bf16[4,272,384]{2,1,0:T(8,128)(2,1)S(1)} %bitcast.44), channel_id=1, source_target_pairs={{0,4},{4,0},{8,12},{12,8},{16,20},{20,16},{24,28},{28,24},{1,5},{5... | collective-permute-start | bytes 2506760 | tf_op jit(solution)/shard_map/ppermute | solution.py:773
  24.9 24.3 %collective-permute-start.3 = (bf16[4,112,384]{2,1,0:T(8,128)(2,1)S(1)}, bf16[4,112,384]{2,1,0:T(8,128)(2,1)S(1)}, u32[]{:S(2)}, u32[]{:S(2)}) collective-permute-start(bf16[4,112,384]{2,1,0:T(8,128)(2,1)S(1)} %slice.48), channel_id=1, source_target_pairs={{0,24},{4,28},{8,16},{12,20},{16,8},{20,12},{24,0},{28,4},{1,25},{... | collective-permute-start | bytes 1032200 | tf_op jit(solution)/shard_map/ppermute | solution.py:773
  27.4 21.8 %collective-permute-start.2 = (bf16[4,112,384]{2,1,0:T(8,128)(2,1)S(1)}, bf16[4,112,384]{2,1,0:T(8,128)(2,1)S(1)}, u32[]{:S(2)}, u32[]{:S(2)}) collective-permute-start(bf16[4,112,384]{2,1,0:T(8,128)(2,1)S(1)} %slice.48), channel_id=1, source_target_pairs={{0,16},{4,20},{8,24},{12,28},{16,0},{20,4},{24,8},{28,12},{1,17},{... | collective-permute-start | bytes 1032200 | tf_op jit(solution)/shard_map/ppermute | solution.py:773
  27.9 21.3 %collective-permute-start.1 = (bf16[4,112,384]{2,1,0:T(8,128)(2,1)S(1)}, bf16[4,112,384]{2,1,0:T(8,128)(2,1)S(1)}, u32[]{:S(2)}, u32[]{:S(2)}) collective-permute-start(bf16[4,112,384]{2,1,0:T(8,128)(2,1)S(1)} %slice.48), channel_id=1, source_target_pairs={{0,8},{4,12},{8,0},{12,4},{16,24},{20,28},{24,16},{28,20},{1,9},{5... | collective-permute-start | bytes 1032200 | tf_op jit(solution)/shard_map/ppermute | solution.py:773
  28.5 0.9 copy-start.1
  49.2 2.8 %copy-start.2 = (bf16[4,112,384]{2,1,0:T(8,128)(2,1)}, bf16[4,112,384]{2,1,0:T(8,128)(2,1)S(1)}, u32[]{:S(2)}) copy-start(bf16[4,112,384]{2,1,0:T(8,128)(2,1)S(1)} %collective-permute-done.3.refs_2_) | copy-start | bytes 1032196
  49.3 2.7 %copy-start.3 = (bf16[4,112,384]{2,1,0:T(8,128)(2,1)}, bf16[4,112,384]{2,1,0:T(8,128)(2,1)S(1)}, u32[]{:S(2)}) copy-start(bf16[4,112,384]{2,1,0:T(8,128)(2,1)S(1)} %collective-permute-done.2.refs_1_) | copy-start | bytes 1032196
  49.3 2.7 %copy-start.4 = (bf16[4,112,384]{2,1,0:T(8,128)(2,1)}, bf16[4,112,384]{2,1,0:T(8,128)(2,1)S(1)}, u32[]{:S(2)}) copy-start(bf16[4,112,384]{2,1,0:T(8,128)(2,1)S(1)} %collective-permute-done.1.refs_0_) | copy-start | bytes 1032196
  49.3 1.7 collective-permute-start.4
  49.4 2.1 %collective-permute-start.5 = (bf16[4,112,384]{2,1,0:T(8,128)(2,1)S(1)}, bf16[4,112,384]{2,1,0:T(8,128)(2,1)S(1)}, u32[]{:S(2)}, u32[]{:S(2)}) collective-permute-start(bf16[4,112,384]{2,1,0:T(8,128)(2,1)S(1)} %collective-permute-done.2.refs_1_), channel_id=1, source_target_pairs={{0,4},{4,0},{8,12},{12,8},{16,20},{20,16},{24,28},{28,24},{1,5},{5... | collective-permute-start | bytes 1032200 | tf_op jit(solution)/shard_map/ppermute | solution.py:773
  49.9 2.1 %collective-permute-start.6 = (bf16[4,112,384]{2,1,0:T(8,128)(2,1)S(1)}, bf16[4,112,384]{2,1,0:T(8,128)(2,1)S(1)}, u32[]{:S(2)}, u32[]{:S(2)}) collective-permute-start(bf16[4,112,384]{2,1,0:T(8,128)(2,1)S(1)} %collective-permute-done.3.refs_2_), channel_id=1, source_target_pairs={{0,4},{4,0},{8,12},{12,8},{16,20},{20,16},{24,28},{28,24},{1,5},{5... | collective-permute-start | bytes 1032200 | tf_op jit(solution)/shard_map/ppermute | solution.py:773
  51.0 1.0 copy-start.5
  51.5 0.7 copy-start.6
  52.0 0.7 copy-start.7
  107.5 3.3 %collective-permute-start.7 = (bf16[1728,384]{1,0:T(8,128)(2,1)}, bf16[1728,384]{1,0:T(8,128)(2,1)S(1)}, u32[]{:S(2)}, u32[]{:S(2)}) collective-permute-start(bf16[1728,384]{1,0:T(8,128)(2,1)} %get-tuple-element.94), channel_id=1, source_target_pairs={{0,4},{4,0},{8,12},{12,8},{16,20},{20,16},{24,28},{28,24},{1,5},{5... | collective-permute-start | bytes 3981320 | tf_op jit(solution)/shard_map/ppermute | solution.py:773
  112.3 22.1 %collective-permute-start.10 = (bf16[432,384]{1,0:T(8,128)(2,1)S(1)}, bf16[432,384]{1,0:T(8,128)(2,1)S(1)}, u32[]{:S(2)}, u32[]{:S(2)}) collective-permute-start(bf16[432,384]{1,0:T(8,128)(2,1)S(1)} %get-tuple-element.146), channel_id=1, source_target_pairs={{0,24},{4,28},{8,16},{12,20},{16,8},{20,12},{24,0},{28,4},{1,25},{... | collective-permute-start | bytes 995336 | tf_op jit(solution)/shard_map/ppermute | solution.py:773
  114.8 19.6 %collective-permute-start.9 = (bf16[432,384]{1,0:T(8,128)(2,1)S(1)}, bf16[432,384]{1,0:T(8,128)(2,1)S(1)}, u32[]{:S(2)}, u32[]{:S(2)}) collective-permute-start(bf16[432,384]{1,0:T(8,128)(2,1)S(1)} %get-tuple-element.147), channel_id=1, source_target_pairs={{0,16},{4,20},{8,24},{12,28},{16,0},{20,4},{24,8},{28,12},{1,17},{... | collective-permute-start | bytes 995336 | tf_op jit(solution)/shard_map/ppermute | solution.py:773
  115.3 19.1 %collective-permute-start.8 = (bf16[432,384]{1,0:T(8,128)(2,1)S(1)}, bf16[432,384]{1,0:T(8,128)(2,1)S(1)}, u32[]{:S(2)}, u32[]{:S(2)}) collective-permute-start(bf16[432,384]{1,0:T(8,128)(2,1)S(1)} %get-tuple-element.148), channel_id=1, source_target_pairs={{0,8},{4,12},{8,0},{12,4},{16,24},{20,28},{24,16},{28,20},{1,9},{5... | collective-permute-start | bytes 995336 | tf_op jit(solution)/shard_map/ppermute | solution.py:773
  135.7 21.5 %collective-permute-start.12 = (bf16[216,384]{1,0:T(8,128)(2,1)S(1)}, bf16[216,384]{1,0:T(8,128)(2,1)S(1)}, u32[]{:S(2)}, u32[]{:S(2)}) collective-permute-start(bf16[216,384]{1,0:T(8,128)(2,1)S(1)} %get-tuple-element.145), channel_id=1, source_target_pairs={{0,2},{1,3},{2,0},{3,1},{4,6},{5,7},{6,4},{7,5},{8,10},{9,11},{10,... | collective-permute-start | bytes 497672 | tf_op jit(solution)/shard_map/ppermute | solution.py:800
  136.6 20.5 %collective-permute-start.11 = (bf16[216,384]{1,0:T(8,128)(2,1)S(1)}, bf16[216,384]{1,0:T(8,128)(2,1)S(1)}, u32[]{:S(2)}, u32[]{:S(2)}) collective-permute-start(bf16[216,384]{1,0:T(8,128)(2,1)S(1)} %get-tuple-element.144), channel_id=1, source_target_pairs={{0,1},{1,0},{2,3},{3,2},{4,5},{5,4},{6,7},{7,6},{8,9},{9,8},{10,11... | collective-permute-start | bytes 497672 | tf_op jit(solution)/shard_map/ppermute | solution.py:800
  157.2 2.2 %collective-permute-start.13 = (bf16[704,384]{1,0:T(8,128)(2,1)}, bf16[704,384]{1,0:T(8,128)(2,1)S(1)}, u32[]{:S(2)}, u32[]{:S(2)}) collective-permute-start(bf16[704,384]{1,0:T(8,128)(2,1)} %get-tuple-element.116), channel_id=1, source_target_pairs={{0,4},{4,0},{8,12},{12,8},{16,20},{20,16},{24,28},{28,24},{1,5},{5... | collective-permute-start | bytes 1622024 | tf_op jit(solution)/shard_map/ppermute | solution.py:773
  157.3 11.3 %collective-permute-start.18 = (bf16[216,384]{1,0:T(8,128)(2,1)S(1)}, bf16[216,384]{1,0:T(8,128)(2,1)S(1)}, u32[]{:S(2)}, u32[]{:S(2)}) collective-permute-start(bf16[216,384]{1,0:T(8,128)(2,1)S(1)} %add_convert_fusion.6), channel_id=1, source_target_pairs={{0,2},{1,3},{2,0},{3,1},{4,6},{5,7},{6,4},{7,5},{8,10},{9,11},{10,... | collective-permute-start | bytes 497672 | tf_op jit(solution)/shard_map/ppermute | solution.py:800
  160.5 9.6 %collective-permute-start.14 = (bf16[176,384]{1,0:T(8,128)(2,1)S(1)}, bf16[176,384]{1,0:T(8,128)(2,1)S(1)}, u32[]{:S(2)}, u32[]{:S(2)}) collective-permute-start(bf16[176,384]{1,0:T(8,128)(2,1)S(1)} %get-tuple-element.149), channel_id=1, source_target_pairs={{0,8},{4,12},{8,0},{12,4},{16,24},{20,28},{24,16},{28,20},{1,9},{5... | collective-permute-start | bytes 405512 | tf_op jit(solution)/shard_map/ppermute | solution.py:773
  162.0 8.1 %collective-permute-start.16 = (bf16[176,384]{1,0:T(8,128)(2,1)S(1)}, bf16[176,384]{1,0:T(8,128)(2,1)S(1)}, u32[]{:S(2)}, u32[]{:S(2)}) collective-permute-start(bf16[176,384]{1,0:T(8,128)(2,1)S(1)} %get-tuple-element.150), channel_id=1, source_target_pairs={{0,24},{4,28},{8,16},{12,20},{16,8},{20,12},{24,0},{28,4},{1,25},{... | collective-permute-start | bytes 405512 | tf_op jit(solution)/shard_map/ppermute | solution.py:773
  163.5 8.0 %collective-permute-start.15 = (bf16[176,384]{1,0:T(8,128)(2,1)S(1)}, bf16[176,384]{1,0:T(8,128)(2,1)S(1)}, u32[]{:S(2)}, u32[]{:S(2)}) collective-permute-start(bf16[176,384]{1,0:T(8,128)(2,1)S(1)} %get-tuple-element.151), channel_id=1, source_target_pairs={{0,16},{4,20},{8,24},{12,28},{16,0},{20,4},{24,8},{28,12},{1,17},{... | collective-permute-start | bytes 405512 | tf_op jit(solution)/shard_map/ppermute | solution.py:773
  164.1 9.4 %collective-permute-start.19 = (bf16[216,384]{1,0:T(8,128)(2,1)S(1)}, bf16[216,384]{1,0:T(8,128)(2,1)S(1)}, u32[]{:S(2)}, u32[]{:S(2)}) collective-permute-start(bf16[216,384]{1,0:T(8,128)(2,1)S(1)} %add_convert_fusion.4), channel_id=1, source_target_pairs={{0,1},{1,0},{2,3},{3,2},{4,5},{5,4},{6,7},{7,6},{8,9},{9,8},{10,11... | collective-permute-start | bytes 497672 | tf_op jit(solution)/shard_map/ppermute | solution.py:800
  172.5 5.1 %collective-permute-start.17 = (bf16[176,384]{1,0:T(8,128)(2,1)S(1)}, bf16[176,384]{1,0:T(8,128)(2,1)S(1)}, u32[]{:S(2)}, u32[]{:S(2)}) collective-permute-start(bf16[176,384]{1,0:T(8,128)(2,1)S(1)} %fusion.11), channel_id=1, source_target_pairs={{0,1},{1,0},{2,3},{3,2},{4,5},{5,4},{6,7},{7,6},{8,9},{9,8},{10,11... | collective-permute-start | bytes 405512 | tf_op jit(solution)/shard_map/ppermute | solution.py:800
  173.6 11.5 %collective-permute-start.25 = (bf16[432,384]{1,0:T(8,128)(2,1)S(1)}, bf16[432,384]{1,0:T(8,128)(2,1)S(1)}, u32[]{:S(2)}, u32[]{:S(2)}) collective-permute-start(bf16[432,384]{1,0:T(8,128)(2,1)S(1)} %pad_maximum_fusion.1), channel_id=1, source_target_pairs={{0,16},{4,20},{8,24},{12,28},{16,0},{20,4},{24,8},{28,12},{1,17},{... | collective-permute-start | bytes 995336 | tf_op jit(solution)/shard_map/ppermute | solution.py:773
  174.2 10.8 %collective-permute-start.21 = (bf16[432,384]{1,0:T(8,128)(2,1)S(1)}, bf16[432,384]{1,0:T(8,128)(2,1)S(1)}, u32[]{:S(2)}, u32[]{:S(2)}) collective-permute-start(bf16[432,384]{1,0:T(8,128)(2,1)S(1)} %pad_maximum_fusion.1), channel_id=1, source_target_pairs={{0,8},{4,12},{8,0},{12,4},{16,24},{20,28},{24,16},{28,20},{1,9},{5... | collective-permute-start | bytes 995336 | tf_op jit(solution)/shard_map/ppermute | solution.py:773
  177.6 7.4 %collective-permute-start.20 = (bf16[176,384]{1,0:T(8,128)(2,1)S(1)}, bf16[176,384]{1,0:T(8,128)(2,1)S(1)}, u32[]{:S(2)}, u32[]{:S(2)}) collective-permute-start(bf16[176,384]{1,0:T(8,128)(2,1)S(1)} %add_convert_fusion.8), channel_id=1, source_target_pairs={{0,2},{1,3},{2,0},{3,1},{4,6},{5,7},{6,4},{7,5},{8,10},{9,11},{10,... | collective-permute-start | bytes 405512 | tf_op jit(solution)/shard_map/ppermute | solution.py:800
  178.7 11.8 %collective-permute-start.26 = (bf16[432,384]{1,0:T(8,128)(2,1)S(1)}, bf16[432,384]{1,0:T(8,128)(2,1)S(1)}, u32[]{:S(2)}, u32[]{:S(2)}) collective-permute-start(bf16[432,384]{1,0:T(8,128)(2,1)S(1)} %pad_maximum_fusion.1), channel_id=1, source_target_pairs={{0,24},{4,28},{8,16},{12,20},{16,8},{20,12},{24,0},{28,4},{1,25},{... | collective-permute-start | bytes 995336 | tf_op jit(solution)/shard_map/ppermute | solution.py:773
  190.5 3.7 %collective-permute-start.27 = (bf16[1728,384]{1,0:T(8,128)(2,1)S(1)}, bf16[1728,384]{1,0:T(8,128)(2,1)S(1)}, u32[]{:S(2)}, u32[]{:S(2)}) collective-permute-start(bf16[1728,384]{1,0:T(8,128)(2,1)S(1)} %constant_dynamic-update-slice_fusion.refs_0_), channel_id=1, source_target_pairs={{0,4},{4,0},{8,12},{12,8},{16,20},{20,16},{24,28},{28,24},{1,5},{5... | collective-permute-start | bytes 3981320 | tf_op jit(solution)/shard_map/ppermute | solution.py:773
  190.7 7.4 %collective-permute-start.24 = (bf16[176,384]{1,0:T(8,128)(2,1)S(1)}, bf16[176,384]{1,0:T(8,128)(2,1)S(1)}, u32[]{:S(2)}, u32[]{:S(2)}) collective-permute-start(bf16[176,384]{1,0:T(8,128)(2,1)S(1)} %add_convert_fusion.7), channel_id=1, source_target_pairs={{0,24},{4,28},{8,16},{12,20},{16,8},{20,12},{24,0},{28,4},{1,25},{... | collective-permute-start | bytes 405512 | tf_op jit(solution)/shard_map/ppermute | solution.py:773
  192.9 7.6 %collective-permute-start.23 = (bf16[176,384]{1,0:T(8,128)(2,1)S(1)}, bf16[176,384]{1,0:T(8,128)(2,1)S(1)}, u32[]{:S(2)}, u32[]{:S(2)}) collective-permute-start(bf16[176,384]{1,0:T(8,128)(2,1)S(1)} %add_convert_fusion.7), channel_id=1, source_target_pairs={{0,16},{4,20},{8,24},{12,28},{16,0},{20,4},{24,8},{28,12},{1,17},{... | collective-permute-start | bytes 405512 | tf_op jit(solution)/shard_map/ppermute | solution.py:773
  193.7 6.8 %collective-permute-start.22 = (bf16[176,384]{1,0:T(8,128)(2,1)S(1)}, bf16[176,384]{1,0:T(8,128)(2,1)S(1)}, u32[]{:S(2)}, u32[]{:S(2)}) collective-permute-start(bf16[176,384]{1,0:T(8,128)(2,1)S(1)} %add_convert_fusion.7), channel_id=1, source_target_pairs={{0,8},{4,12},{8,0},{12,4},{16,24},{20,28},{24,16},{28,20},{1,9},{5... | collective-permute-start | bytes 405512 | tf_op jit(solution)/shard_map/ppermute | solution.py:773
  200.6 2.0 collective-permute-start.28

commit v6 on v5

--- a/solution.py
+++ b/solution.py
@@ -101,10 +101,10 @@
     return jnp.where(rows == lanes, value, 0.0).astype(bf16)
 
 
-def lane_ones(value):
-    rows = lax.broadcasted_iota(jnp.int32, (128, 2 * KEYS), 0) < 64
-    lanes = lax.broadcasted_iota(jnp.int32, (128, 2 * KEYS), 1) < KEYS
-    return jnp.where(rows == lanes, value, 0.0).astype(bf16)
+def block_ones():
+    rows = lax.broadcasted_iota(jnp.int32, (2 * KEYS, 2 * KEYS), 0) < KEYS
+    lanes = lax.broadcasted_iota(jnp.int32, (2 * KEYS, 2 * KEYS), 1) < KEYS
+    return jnp.where(rows == lanes, 1.0, 0.0).astype(bf16)
 
 
 def pack_kernel(spot, counts, index, proj, joint, out, up, down, up_bias, *refs):
@@ -266,7 +266,7 @@
         placed = dot(low, proj[...]) + vec[1:2, :]
         hidden = hidden_column(targets[sub * TILE : sub * TILE + TILE, :])
         rows = jnp.where(hidden > 0.5, vec[0:1, :], tokens[span, :].astype(f32)) + placed
-        entry[span, :] = rows.astype(bf16)
+        entry[span, :] = rows
         unit, _ = normalised(rows)
         return (unit * vec[2:3, :] + vec[3:4, :]).astype(bf16)
 
@@ -391,7 +391,7 @@
             whole((steps, 16, ROWS)), whole((16, POSH)),
         ],
         out_shape=[
-            shape_of((count, D), bf16), shape_of((count, 3 * D), bf16),
+            shape_of((count, D), f32), shape_of((count, 3 * D), bf16),
             shape_of((count, D), bf16), shape_of((count, D), bf16),
             shape_of((steps * TILE, WIN, HEADS * KEYS), bf16), shape_of((D, 3 * D), bf16), shape_of((POSH, D), bf16),
             shape_of((steps, 16, ROWS), bf16), shape_of((16, POSH), bf16),
@@ -442,7 +442,7 @@
     spans = [slice(part * chunk, part * chunk + chunk) for part in range(parts)]
     mix = mixture[...]
     cotangent = cot[...]
-    mid = entry[...].astype(f32) + (dot(mix, out_w[...]) + vec[4:5, :])
+    mid = entry[...] + (dot(mix, out_w[...]) + vec[4:5, :])
     gates = [dot(cotangent, down_w[spans[0], :], NT)]
     unit, scale = normalised(mid)
     normed = (unit * vec[5:6, :] + vec[6:7, :]).astype(bf16)
@@ -546,9 +546,9 @@
 
     qkv[:ROWS, :] = joint[...]
     pre = dot(cen[0], place_w[...], TN)
-    unit, scale = normalised(entry[...].astype(f32))
+    unit, scale = normalised(entry[...])
     normed = (unit * vec[2:3, :] + vec[3:4, :]).astype(bf16)
-    minus = lane_ones(-1.0)
+    ones = block_ones()
     jobs = [(pair, cloud) for pair in range(PAIRS) for cloud in range(TILE)]
     tails = {}
     for at in range(0, len(jobs), BACK_GROUP):
@@ -559,14 +559,19 @@
             window = slice(base, base + WIN)
             cols = slice(pair * 128, pair * 128 + 128)
             value = qkv[base : base + KEYS, 2 * D + pair * 128 : 2 * D + pair * 128 + 128]
-            dmw = mix_grad[window, cols]
-            left = jnp.concatenate([dmw, dmw * mixture[window, cols]], axis=1)
-            gaps.append(dot(left, jnp.concatenate([spread_heads(value.T), minus], axis=0)))
-        es, dss = [], []
+            gaps.append(dot(mix_grad[window, cols], spread_heads(value.T)))
+        es, products, sums_of = [], [], []
         for (pair, cloud), gap in zip(group, gaps):
             e = weights[cloud, :, pair * 256 : pair * 256 + 256]
+            product = e.astype(f32) * gap
+            high, rest = split16(product)
             es.append(e)
-            dss.append((e.astype(f32) * gap).astype(bf16))
+            products.append(product)
+            sums_of.append(dot(jnp.concatenate([high, rest, e], axis=0), ones))
+        dss = []
+        for e, product, found in zip(es, products, sums_of):
+            share = (found[:WIN] + found[WIN : 2 * WIN]) / jnp.maximum(found[2 * WIN :], 1e-30)
+            dss.append((product - e.astype(f32) * share).astype(bf16))
         results = []
         for (pair, cloud), e, ds in zip(group, es, dss):
             base = cloud * STEP

time: 205 us -> 211 us (1.029)
  Pallas kernels: 119 us -> 126 us
    pallas_call x2, Pallas kernels: 37.8 us -> 44 us  [back_part(): pl.pallas_call(functools.partial(back_kernel, before is None, extra is no...]
  transfers between devices with their start and end apart: 29 -> 29, of which waited for: 14 -> 14; matrix products, arithmetic and copies ran while one was open for 1% -> 1% of each run, Pallas kernels for 30% -> 32%
where the time goes in v6:
time: 211 us
  Pallas kernels  126 us (60%)
  waiting for transfers between devices  30.3 us (14%)
  starting transfers between devices  24.7 us (12%)
  blocking collectives  22.1 us (10%)
  other arithmetic  5.21 us (2%)
    pallas_call x1, Pallas kernels, middle_part(): pl.pallas_call(functools.partial(middle_kernel, chunk, order), grid=(coun...  54.8 us
    pallas_call x2, Pallas kernels, back_part(): pl.pallas_call(functools.partial(back_kernel, before is None, extra is no...  44 us
    all_gather x1, blocking collectives, per_device(): packed = lax.all_gather(packed, 'fsdp', axis=0)  22.1 us
    pallas_call x1, Pallas kernels, front(): pl.pallas_call(front_kernel, grid=(steps // SUBS,), in_specs=[pl.BlockSpe...  20.1 us
    ppermute x23, waiting for transfers between devices, swapped(): return lax.ppermute(values, 'dp', [(i, i ^ offset) for i in range(size)])  19.8 us
    ppermute x23, starting transfers between devices, swapped(): return lax.ppermute(values, 'dp', [(i, i ^ offset) for i in range(size)])  18.8 us
    ppermute x6, waiting for transfers between devices, crossed(): return lax.ppermute(values, 'fsdp', [(i, i ^ offset) for i in range(size)])  10.4 us
    ppermute x6, starting transfers between devices, crossed(): return lax.ppermute(values, 'fsdp', [(i, i ^ offset) for i in range(size)])  5.96 us
  transfers between devices with their start and end apart: 29, of which 14 were waited for; matrix products, arithmetic and copies ran while one was open for 1% of the time, Pallas kernels for 32%

profile of v6, /device:TPU:0, one launch (start us, length us, event | category | flops | bytes accessed | tf_op | source)
XLA Modules:
  0.0 211.0 jit_solution(16175659828814150458)
XLA Ops:
  0.7 2.1 %pack.1 = (bf16[272,384]{1,0:T(8,128)(2,1)}, f32[8,384]{1,0:T(8,128)}, f32[1,1536]{1,0:T(1,128)}, s32[64,128]{1,0:T(8,128)}) custom-call(s32[1]{0:T(128)} %bitcast.spot, s32[64]{0:T(128)} %counts.1, s32[28,64]{1,0:T(8,128)} %bitcast.56, bf16[32,384]{1,0:T(8,128)(2,1)} %proj.1, bf16[96,1152]{1,0:T(8,128)(2,1)} %joint.1, bf16[96,384]{1,0:T(8,128)(2,1)} %out.1, ...), custom_call_target="tpu_custom_call" | custom-call | tf_op jit(solution)/shard_map/pack/pallas_call | solution.py:144
  2.8 22.1 %all-gather = bf16[1088,384]{1,0:T(8,128)(2,1)S(1)} all-gather(bf16[272,384]{1,0:T(8,128)(2,1)} %get-tuple-element.81), channel_id=2, replica_groups=mesh['dp'=8,'fsdp'=4] {'fsdp'}, dimensions={0}, use_global_device_ids=true | all-gather | bytes 1044480 | tf_op jit(solution)/shard_map/all_gather | solution.py:847
  24.9 2.5 %collective-permute-start.3 = (bf16[4,112,384]{2,1,0:T(8,128)(2,1)S(1)}, bf16[4,112,384]{2,1,0:T(8,128)(2,1)S(1)}, u32[]{:S(2)}, u32[]{:S(2)}) collective-permute-start(bf16[4,112,384]{2,1,0:T(8,128)(2,1)S(1)} %slice.48), channel_id=1, source_target_pairs={{0,24},{4,28},{8,16},{12,20},{16,8},{20,12},{24,0},{28,4},{1,25},{... | collective-permute-start | bytes 1032200 | tf_op jit(solution)/shard_map/ppermute | solution.py:778
  27.4 0.5 collective-permute-start.2
  27.9 0.5 collective-permute-start.1
  28.5 0.0 collective-permute-done.other
  28.5 0.9 copy-done.1
  29.4 20.1 %front.1 = (f32[4224,384]{1,0:T(8,128)}, bf16[4224,1152]{1,0:T(8,128)(2,1)}, bf16[4224,384]{1,0:T(8,128)(2,1)}, bf16[4224,384]{1,0:T(8,128)(2,1)}, bf16[64,80,76...) custom-call(s32[1]{0:T(128)S(6)} %select_n.46.core.refs_17_, ...), custom_call_target="tpu_custom_call" | custom-call | flops 25200001024 | bytes 56000000 | tf_op jit(solution)/shard_map/front/pallas_call | solution.py:380
  49.5 0.0 copy-start.4
  49.5 0.1 collective-permute-start.4
  49.6 0.5 collective-permute-start.5
  50.1 0.1 collective-permute-start.6
  50.1 1.1 collective-permute-done.4.refs_3_
  51.2 0.5 collective-permute-done.5.refs_4_
  51.7 0.5 collective-permute-done.6.refs_5_
  52.2 0.2 copy-done.6
  52.5 0.5 copy-done.7
  52.9 54.8 %middle.1 = (bf16[4224,384]{1,0:T(8,128)(2,1)}, bf16[4224,384]{1,0:T(8,128)(2,1)}, bf16[4224,384]{1,0:T(8,128)(2,1)}, bf16[1728,384]{1,0:T(8,128)(2,1)}, bf16[17...) custom-call(s32[1]{0:T(128)} %bitcast.spot, f32[4224,384]{1,0:T(8,128)} %get-tuple-element.82.entry.refs_0_, ...), custom_call_target="tpu_custom_call" | custom-call | flops 49500000256 | bytes 110000000 | tf_op jit(solution)/shard_map/middle/pallas_call | solution.py:502
  107.8 0.2 collective-permute-start.7
  108.0 3.1 %collective-permute-done.7 = bf16[1728,384]{1,0:T(8,128)(2,1)S(1)} collective-permute-done((bf16[1728,384]{1,0:T(8,128)(2,1)}, bf16[1728,384]{1,0:T(8,128)(2,1)S(1)}, u32[]{:S(2)}, u32[]{:S(2)}) %collective-permute-start.7) | collective-permute-done | bytes 1327136 | tf_op jit(solution)/shard_map/ppermute | solution.py:778
  111.1 1.4 fusion.2
  112.6 2.5 %collective-permute-start.10 = (bf16[432,384]{1,0:T(8,128)(2,1)S(1)}, bf16[432,384]{1,0:T(8,128)(2,1)S(1)}, u32[]{:S(2)}, u32[]{:S(2)}) collective-permute-start(bf16[432,384]{1,0:T(8,128)(2,1)S(1)} %get-tuple-element.146), channel_id=1, source_target_pairs={{0,24},{4,28},{8,16},{12,20},{16,8},{20,12},{24,0},{28,4},{1,25},{... | collective-permute-start | bytes 995336 | tf_op jit(solution)/shard_map/ppermute | solution.py:778
  115.1 0.5 collective-permute-start.9
  115.6 0.6 collective-permute-start.8
  116.1 21.7 %back.2 = (bf16[4224,384]{1,0:T(8,128)(2,1)}, f32[384,1152]{1,0:T(8,128)}, f32[128,384]{1,0:T(8,128)}, f32[16,256]{1,0:T(8,128)}, f32[8,384]{1,0:T(8,128)}) custom-call(f32[4224,384]{1,0:T(8,128)} %get-tuple-element.82.entry.refs_0_, bf16[4224,1152]{1,0:T(8,128)(2,1)} %get-tuple-element.91.refs_1_, bf16[4224,384]{1,0:T(8,128)(2,1)} %get-tuple-element.84.mixture.refs_2_, ...), custom_call_target="tpu_custom_call" | custom-call | flops 17999998976 | bytes 40000000 | tf_op jit(solution)/shard_map/back/pallas_call | solution.py:676
  137.8 1.2 fusion.5
  139.1 0.9 collective-permute-start.12
  140.0 1.3 collective-permute-start.11
  141.3 22.3 %back.3 = (bf16[4224,384]{1,0:T(8,128)(2,1)}, bf16[704,384]{1,0:T(8,128)(2,1)}, bf16[704,384]{1,0:T(8,128)(2,1)}) custom-call(f32[4224,384]{1,0:T(8,128)} %get-tuple-element.82.entry.refs_0_, bf16[4224,1152]{1,0:T(8,128)(2,1)} %get-tuple-element.91.refs_1_, bf16[4224,384]{1,0:T(8,128)(2,1)} %get-tuple-element.84.mixture.refs_2_, ...), custom_call_target="tpu_custom_call", output_to_operand_aliasing={{0}: (12, {})} | custom-call | flops 17999998976 | bytes 40000000 | tf_op jit(solution)/shard_map/back/pallas_call | solution.py:676
  163.6 0.1 collective-permute-start.13
  163.8 0.9 collective-permute-start.18
  164.6 1.2 collective-permute-done.13
  165.9 1.1 fusion.12
  167.0 1.5 collective-permute-start.14
  168.5 1.5 collective-permute-start.16
  170.0 0.5 collective-permute-start.15
  170.6 0.9 collective-permute-start.19
  171.5 3.5 %collective-permute-done.18 = bf16[216,384]{1,0:T(8,128)(2,1)S(1)} collective-permute-done((bf16[216,384]{1,0:T(8,128)(2,1)S(1)}, bf16[216,384]{1,0:T(8,128)(2,1)S(1)}, u32[]{:S(2)}, u32[]{:S(2)}) %collective-permute-start.18) | collective-permute-done | bytes 165920 | tf_op jit(solution)/shard_map/ppermute | solution.py:805
  175.0 1.6 collective-permute-done.16
  176.6 1.4 collective-permute-done.15
  178.0 1.0 fusion.11
  179.0 1.0 collective-permute-start.17
  180.0 0.1 constant_dynamic-update-slice_fusion.3
  180.1 0.6 collective-permute-start.25
  180.7 1.5 collective-permute-start.21
  182.2 1.9 collective-permute-done.17
  184.1 1.1 collective-permute-start.20
  185.2 1.4 collective-permute-start.26
  186.6 5.0 %collective-permute-done.20 = bf16[176,384]{1,0:T(8,128)(2,1)S(1)} collective-permute-done((bf16[176,384]{1,0:T(8,128)(2,1)S(1)}, bf16[176,384]{1,0:T(8,128)(2,1)S(1)}, u32[]{:S(2)}, u32[]{:S(2)}) %collective-permute-start.20) | collective-permute-done | bytes 135200 | tf_op jit(solution)/shard_map/ppermute | solution.py:805
  191.5 0.1 constant_dynamic-update-slice_fusion.2
  191.6 0.1 constant_dynamic-update-slice_fusion.1
  191.7 5.3 %collective-permute-done.26 = bf16[432,384]{1,0:T(8,128)(2,1)S(1)} collective-permute-done((bf16[432,384]{1,0:T(8,128)(2,1)S(1)}, bf16[432,384]{1,0:T(8,128)(2,1)S(1)}, u32[]{:S(2)}, u32[]{:S(2)}) %collective-permute-start.26) | collective-permute-done | bytes 331808 | tf_op jit(solution)/shard_map/ppermute | solution.py:778
  197.0 0.1 constant_dynamic-update-slice_fusion.refs_0_
  197.0 0.1 collective-permute-start.27
  197.2 2.2 %collective-permute-start.24 = (bf16[176,384]{1,0:T(8,128)(2,1)S(1)}, bf16[176,384]{1,0:T(8,128)(2,1)S(1)}, u32[]{:S(2)}, u32[]{:S(2)}) collective-permute-start(bf16[176,384]{1,0:T(8,128)(2,1)S(1)} %add_convert_fusion.7), channel_id=1, source_target_pairs={{0,24},{4,28},{8,16},{12,20},{16,8},{20,12},{24,0},{28,4},{1,25},{... | collective-permute-start | bytes 405512 | tf_op jit(solution)/shard_map/ppermute | solution.py:778
  199.3 0.8 collective-permute-start.23
  200.2 0.5 collective-permute-start.22
  200.7 3.0 %widen.1 = (f32[384,1536]{1,0:T(8,128)}, f32[1536,384]{1,0:T(8,128)}, f32[384,384]{1,0:T(8,128)}) custom-call(s32[1]{0:T(128)} %bitcast.spot, bf16[1728,384]{1,0:T(8,128)(2,1)S(1)} %constant_dynamic-update-slice_fusion.refs_0_, bf16[1728,384]{1,0:T(8,128)(2,1)S(1)} %collective-permute-done.27.refs_1_), custom_call_target="tpu_custom_call" | custom-call | flops 3600000000 | bytes 8000000 | tf_op jit(solution)/shard_map/widen/pallas_call | solution.py:737
  203.7 0.8 collective-permute-done.24
  204.5 2.5 %collective-permute-done.23 = bf16[176,384]{1,0:T(8,128)(2,1)S(1)} collective-permute-done((bf16[176,384]{1,0:T(8,128)(2,1)S(1)}, bf16[176,384]{1,0:T(8,128)(2,1)S(1)}, u32[]{:S(2)}, u32[]{:S(2)}) %collective-permute-start.23) | collective-permute-done | bytes 135200 | tf_op jit(solution)/shard_map/ppermute | solution.py:778
  207.0 0.1 pad_maximum_fusion.refs_0_
  207.1 0.1 collective-permute-start.28
  207.2 1.9 collective-permute-done.28.refs_1_
  209.1 1.9 close.1
  (34 shorter events, 0.3 us)
Async XLA Ops:
  24.9 3.6 %copy-start = (bf16[1088,384]{1,0:T(8,128)(2,1)}, bf16[1088,384]{1,0:T(8,128)(2,1)S(1)}, u32[]{:S(2)}) copy-start(bf16[1088,384]{1,0:T(8,128)(2,1)S(1)} %all-gather) | copy-start | bytes 2506756
  24.9 3.6 %collective-permute-start = (bf16[4,272,384]{2,1,0:T(8,128)(2,1)S(1)}, bf16[4,272,384]{2,1,0:T(8,128)(2,1)S(1)}, u32[]{:S(2)}, u32[]{:S(2)}) collective-permute-start(bf16[4,272,384]{2,1,0:T(8,128)(2,1)S(1)} %bitcast.44), channel_id=1, source_target_pairs={{0,4},{4,0},{8,12},{12,8},{16,20},{20,16},{24,28},{28,24},{1,5},{5... | collective-permute-start | bytes 2506760 | tf_op jit(solution)/shard_map/ppermute | solution.py:778
  24.9 24.5 %collective-permute-start.3 = (bf16[4,112,384]{2,1,0:T(8,128)(2,1)S(1)}, bf16[4,112,384]{2,1,0:T(8,128)(2,1)S(1)}, u32[]{:S(2)}, u32[]{:S(2)}) collective-permute-start(bf16[4,112,384]{2,1,0:T(8,128)(2,1)S(1)} %slice.48), channel_id=1, source_target_pairs={{0,24},{4,28},{8,16},{12,20},{16,8},{20,12},{24,0},{28,4},{1,25},{... | collective-permute-start | bytes 1032200 | tf_op jit(solution)/shard_map/ppermute | solution.py:778
  27.4 22.0 %collective-permute-start.2 = (bf16[4,112,384]{2,1,0:T(8,128)(2,1)S(1)}, bf16[4,112,384]{2,1,0:T(8,128)(2,1)S(1)}, u32[]{:S(2)}, u32[]{:S(2)}) collective-permute-start(bf16[4,112,384]{2,1,0:T(8,128)(2,1)S(1)} %slice.48), channel_id=1, source_target_pairs={{0,16},{4,20},{8,24},{12,28},{16,0},{20,4},{24,8},{28,12},{1,17},{... | collective-permute-start | bytes 1032200 | tf_op jit(solution)/shard_map/ppermute | solution.py:778
  27.9 21.5 %collective-permute-start.1 = (bf16[4,112,384]{2,1,0:T(8,128)(2,1)S(1)}, bf16[4,112,384]{2,1,0:T(8,128)(2,1)S(1)}, u32[]{:S(2)}, u32[]{:S(2)}) collective-permute-start(bf16[4,112,384]{2,1,0:T(8,128)(2,1)S(1)} %slice.48), channel_id=1, source_target_pairs={{0,8},{4,12},{8,0},{12,4},{16,24},{20,28},{24,16},{28,20},{1,9},{5... | collective-permute-start | bytes 1032200 | tf_op jit(solution)/shard_map/ppermute | solution.py:778
  28.5 0.9 copy-start.1
  49.4 2.8 %copy-start.2 = (bf16[4,112,384]{2,1,0:T(8,128)(2,1)}, bf16[4,112,384]{2,1,0:T(8,128)(2,1)S(1)}, u32[]{:S(2)}) copy-start(bf16[4,112,384]{2,1,0:T(8,128)(2,1)S(1)} %collective-permute-done.3.refs_2_) | copy-start | bytes 1032196
  49.5 2.7 %copy-start.3 = (bf16[4,112,384]{2,1,0:T(8,128)(2,1)}, bf16[4,112,384]{2,1,0:T(8,128)(2,1)S(1)}, u32[]{:S(2)}) copy-start(bf16[4,112,384]{2,1,0:T(8,128)(2,1)S(1)} %collective-permute-done.2.refs_1_) | copy-start | bytes 1032196
  49.5 2.7 %copy-start.4 = (bf16[4,112,384]{2,1,0:T(8,128)(2,1)}, bf16[4,112,384]{2,1,0:T(8,128)(2,1)S(1)}, u32[]{:S(2)}) copy-start(bf16[4,112,384]{2,1,0:T(8,128)(2,1)S(1)} %collective-permute-done.1.refs_0_) | copy-start | bytes 1032196
  49.5 1.7 collective-permute-start.4
  49.6 2.1 %collective-permute-start.5 = (bf16[4,112,384]{2,1,0:T(8,128)(2,1)S(1)}, bf16[4,112,384]{2,1,0:T(8,128)(2,1)S(1)}, u32[]{:S(2)}, u32[]{:S(2)}) collective-permute-start(bf16[4,112,384]{2,1,0:T(8,128)(2,1)S(1)} %collective-permute-done.2.refs_1_), channel_id=1, source_target_pairs={{0,4},{4,0},{8,12},{12,8},{16,20},{20,16},{24,28},{28,24},{1,5},{5... | collective-permute-start | bytes 1032200 | tf_op jit(solution)/shard_map/ppermute | solution.py:778
  50.1 2.1 %collective-permute-start.6 = (bf16[4,112,384]{2,1,0:T(8,128)(2,1)S(1)}, bf16[4,112,384]{2,1,0:T(8,128)(2,1)S(1)}, u32[]{:S(2)}, u32[]{:S(2)}) collective-permute-start(bf16[4,112,384]{2,1,0:T(8,128)(2,1)S(1)} %collective-permute-done.3.refs_2_), channel_id=1, source_target_pairs={{0,4},{4,0},{8,12},{12,8},{16,20},{20,16},{24,28},{28,24},{1,5},{5... | collective-permute-start | bytes 1032200 | tf_op jit(solution)/shard_map/ppermute | solution.py:778
  51.2 1.0 copy-start.5
  51.7 0.8 copy-start.6
  52.2 0.8 copy-start.7
  107.8 3.3 %collective-permute-start.7 = (bf16[1728,384]{1,0:T(8,128)(2,1)}, bf16[1728,384]{1,0:T(8,128)(2,1)S(1)}, u32[]{:S(2)}, u32[]{:S(2)}) collective-permute-start(bf16[1728,384]{1,0:T(8,128)(2,1)} %get-tuple-element.94), channel_id=1, source_target_pairs={{0,4},{4,0},{8,12},{12,8},{16,20},{20,16},{24,28},{28,24},{1,5},{5... | collective-permute-start | bytes 3981320 | tf_op jit(solution)/shard_map/ppermute | solution.py:778
  112.6 25.2 %collective-permute-start.10 = (bf16[432,384]{1,0:T(8,128)(2,1)S(1)}, bf16[432,384]{1,0:T(8,128)(2,1)S(1)}, u32[]{:S(2)}, u32[]{:S(2)}) collective-permute-start(bf16[432,384]{1,0:T(8,128)(2,1)S(1)} %get-tuple-element.146), channel_id=1, source_target_pairs={{0,24},{4,28},{8,16},{12,20},{16,8},{20,12},{24,0},{28,4},{1,25},{... | collective-permute-start | bytes 995336 | tf_op jit(solution)/shard_map/ppermute | solution.py:778
  115.1 22.7 %collective-permute-start.9 = (bf16[432,384]{1,0:T(8,128)(2,1)S(1)}, bf16[432,384]{1,0:T(8,128)(2,1)S(1)}, u32[]{:S(2)}, u32[]{:S(2)}) collective-permute-start(bf16[432,384]{1,0:T(8,128)(2,1)S(1)} %get-tuple-element.147), channel_id=1, source_target_pairs={{0,16},{4,20},{8,24},{12,28},{16,0},{20,4},{24,8},{28,12},{1,17},{... | collective-permute-start | bytes 995336 | tf_op jit(solution)/shard_map/ppermute | solution.py:778
  115.6 22.3 %collective-permute-start.8 = (bf16[432,384]{1,0:T(8,128)(2,1)S(1)}, bf16[432,384]{1,0:T(8,128)(2,1)S(1)}, u32[]{:S(2)}, u32[]{:S(2)}) collective-permute-start(bf16[432,384]{1,0:T(8,128)(2,1)S(1)} %get-tuple-element.148), channel_id=1, source_target_pairs={{0,8},{4,12},{8,0},{12,4},{16,24},{20,28},{24,16},{28,20},{1,9},{5... | collective-permute-start | bytes 995336 | tf_op jit(solution)/shard_map/ppermute | solution.py:778
  139.1 24.5 %collective-permute-start.12 = (bf16[216,384]{1,0:T(8,128)(2,1)S(1)}, bf16[216,384]{1,0:T(8,128)(2,1)S(1)}, u32[]{:S(2)}, u32[]{:S(2)}) collective-permute-start(bf16[216,384]{1,0:T(8,128)(2,1)S(1)} %get-tuple-element.145), channel_id=1, source_target_pairs={{0,2},{1,3},{2,0},{3,1},{4,6},{5,7},{6,4},{7,5},{8,10},{9,11},{10,... | collective-permute-start | bytes 497672 | tf_op jit(solution)/shard_map/ppermute | solution.py:805
  140.0 23.6 %collective-permute-start.11 = (bf16[216,384]{1,0:T(8,128)(2,1)S(1)}, bf16[216,384]{1,0:T(8,128)(2,1)S(1)}, u32[]{:S(2)}, u32[]{:S(2)}) collective-permute-start(bf16[216,384]{1,0:T(8,128)(2,1)S(1)} %get-tuple-element.144), channel_id=1, source_target_pairs={{0,1},{1,0},{2,3},{3,2},{4,5},{5,4},{6,7},{7,6},{8,9},{9,8},{10,11... | collective-permute-start | bytes 497672 | tf_op jit(solution)/shard_map/ppermute | solution.py:805
  163.6 2.2 %collective-permute-start.13 = (bf16[704,384]{1,0:T(8,128)(2,1)}, bf16[704,384]{1,0:T(8,128)(2,1)S(1)}, u32[]{:S(2)}, u32[]{:S(2)}) collective-permute-start(bf16[704,384]{1,0:T(8,128)(2,1)} %get-tuple-element.116), channel_id=1, source_target_pairs={{0,4},{4,0},{8,12},{12,8},{16,20},{20,16},{24,28},{28,24},{1,5},{5... | collective-permute-start | bytes 1622024 | tf_op jit(solution)/shard_map/ppermute | solution.py:778
  163.8 11.3 %collective-permute-start.18 = (bf16[216,384]{1,0:T(8,128)(2,1)S(1)}, bf16[216,384]{1,0:T(8,128)(2,1)S(1)}, u32[]{:S(2)}, u32[]{:S(2)}) collective-permute-start(bf16[216,384]{1,0:T(8,128)(2,1)S(1)} %add_convert_fusion.6), channel_id=1, source_target_pairs={{0,2},{1,3},{2,0},{3,1},{4,6},{5,7},{6,4},{7,5},{8,10},{9,11},{10,... | collective-permute-start | bytes 497672 | tf_op jit(solution)/shard_map/ppermute | solution.py:805
  167.0 9.6 %collective-permute-start.14 = (bf16[176,384]{1,0:T(8,128)(2,1)S(1)}, bf16[176,384]{1,0:T(8,128)(2,1)S(1)}, u32[]{:S(2)}, u32[]{:S(2)}) collective-permute-start(bf16[176,384]{1,0:T(8,128)(2,1)S(1)} %get-tuple-element.149), channel_id=1, source_target_pairs={{0,8},{4,12},{8,0},{12,4},{16,24},{20,28},{24,16},{28,20},{1,9},{5... | collective-permute-start | bytes 405512 | tf_op jit(solution)/shard_map/ppermute | solution.py:778
  168.5 8.1 %collective-permute-start.16 = (bf16[176,384]{1,0:T(8,128)(2,1)S(1)}, bf16[176,384]{1,0:T(8,128)(2,1)S(1)}, u32[]{:S(2)}, u32[]{:S(2)}) collective-permute-start(bf16[176,384]{1,0:T(8,128)(2,1)S(1)} %get-tuple-element.150), channel_id=1, source_target_pairs={{0,24},{4,28},{8,16},{12,20},{16,8},{20,12},{24,0},{28,4},{1,25},{... | collective-permute-start | bytes 405512 | tf_op jit(solution)/shard_map/ppermute | solution.py:778
  170.0 8.0 %collective-permute-start.15 = (bf16[176,384]{1,0:T(8,128)(2,1)S(1)}, bf16[176,384]{1,0:T(8,128)(2,1)S(1)}, u32[]{:S(2)}, u32[]{:S(2)}) collective-permute-start(bf16[176,384]{1,0:T(8,128)(2,1)S(1)} %get-tuple-element.151), channel_id=1, source_target_pairs={{0,16},{4,20},{8,24},{12,28},{16,0},{20,4},{24,8},{28,12},{1,17},{... | collective-permute-start | bytes 405512 | tf_op jit(solution)/shard_map/ppermute | solution.py:778
  170.6 9.4 %collective-permute-start.19 = (bf16[216,384]{1,0:T(8,128)(2,1)S(1)}, bf16[216,384]{1,0:T(8,128)(2,1)S(1)}, u32[]{:S(2)}, u32[]{:S(2)}) collective-permute-start(bf16[216,384]{1,0:T(8,128)(2,1)S(1)} %add_convert_fusion.4), channel_id=1, source_target_pairs={{0,1},{1,0},{2,3},{3,2},{4,5},{5,4},{6,7},{7,6},{8,9},{9,8},{10,11... | collective-permute-start | bytes 497672 | tf_op jit(solution)/shard_map/ppermute | solution.py:805
  179.0 5.1 %collective-permute-start.17 = (bf16[176,384]{1,0:T(8,128)(2,1)S(1)}, bf16[176,384]{1,0:T(8,128)(2,1)S(1)}, u32[]{:S(2)}, u32[]{:S(2)}) collective-permute-start(bf16[176,384]{1,0:T(8,128)(2,1)S(1)} %fusion.11), channel_id=1, source_target_pairs={{0,1},{1,0},{2,3},{3,2},{4,5},{5,4},{6,7},{7,6},{8,9},{9,8},{10,11... | collective-permute-start | bytes 405512 | tf_op jit(solution)/shard_map/ppermute | solution.py:805
  180.1 11.5 %collective-permute-start.25 = (bf16[432,384]{1,0:T(8,128)(2,1)S(1)}, bf16[432,384]{1,0:T(8,128)(2,1)S(1)}, u32[]{:S(2)}, u32[]{:S(2)}) collective-permute-start(bf16[432,384]{1,0:T(8,128)(2,1)S(1)} %pad_maximum_fusion.1), channel_id=1, source_target_pairs={{0,16},{4,20},{8,24},{12,28},{16,0},{20,4},{24,8},{28,12},{1,17},{... | collective-permute-start | bytes 995336 | tf_op jit(solution)/shard_map/ppermute | solution.py:778
  180.7 10.8 %collective-permute-start.21 = (bf16[432,384]{1,0:T(8,128)(2,1)S(1)}, bf16[432,384]{1,0:T(8,128)(2,1)S(1)}, u32[]{:S(2)}, u32[]{:S(2)}) collective-permute-start(bf16[432,384]{1,0:T(8,128)(2,1)S(1)} %pad_maximum_fusion.1), channel_id=1, source_target_pairs={{0,8},{4,12},{8,0},{12,4},{16,24},{20,28},{24,16},{28,20},{1,9},{5... | collective-permute-start | bytes 995336 | tf_op jit(solution)/shard_map/ppermute | solution.py:778
  184.1 7.4 %collective-permute-start.20 = (bf16[176,384]{1,0:T(8,128)(2,1)S(1)}, bf16[176,384]{1,0:T(8,128)(2,1)S(1)}, u32[]{:S(2)}, u32[]{:S(2)}) collective-permute-start(bf16[176,384]{1,0:T(8,128)(2,1)S(1)} %add_convert_fusion.8), channel_id=1, source_target_pairs={{0,2},{1,3},{2,0},{3,1},{4,6},{5,7},{6,4},{7,5},{8,10},{9,11},{10,... | collective-permute-start | bytes 405512 | tf_op jit(solution)/shard_map/ppermute | solution.py:805
  185.2 11.8 %collective-permute-start.26 = (bf16[432,384]{1,0:T(8,128)(2,1)S(1)}, bf16[432,384]{1,0:T(8,128)(2,1)S(1)}, u32[]{:S(2)}, u32[]{:S(2)}) collective-permute-start(bf16[432,384]{1,0:T(8,128)(2,1)S(1)} %pad_maximum_fusion.1), channel_id=1, source_target_pairs={{0,24},{4,28},{8,16},{12,20},{16,8},{20,12},{24,0},{28,4},{1,25},{... | collective-permute-start | bytes 995336 | tf_op jit(solution)/shard_map/ppermute | solution.py:778
  197.0 3.7 %collective-permute-start.27 = (bf16[1728,384]{1,0:T(8,128)(2,1)S(1)}, bf16[1728,384]{1,0:T(8,128)(2,1)S(1)}, u32[]{:S(2)}, u32[]{:S(2)}) collective-permute-start(bf16[1728,384]{1,0:T(8,128)(2,1)S(1)} %constant_dynamic-update-slice_fusion.refs_0_), channel_id=1, source_target_pairs={{0,4},{4,0},{8,12},{12,8},{16,20},{20,16},{24,28},{28,24},{1,5},{5... | collective-permute-start | bytes 3981320 | tf_op jit(solution)/shard_map/ppermute | solution.py:778
  197.2 7.4 %collective-permute-start.24 = (bf16[176,384]{1,0:T(8,128)(2,1)S(1)}, bf16[176,384]{1,0:T(8,128)(2,1)S(1)}, u32[]{:S(2)}, u32[]{:S(2)}) collective-permute-start(bf16[176,384]{1,0:T(8,128)(2,1)S(1)} %add_convert_fusion.7), channel_id=1, source_target_pairs={{0,24},{4,28},{8,16},{12,20},{16,8},{20,12},{24,0},{28,4},{1,25},{... | collective-permute-start | bytes 405512 | tf_op jit(solution)/shard_map/ppermute | solution.py:778
  199.3 7.7 %collective-permute-start.23 = (bf16[176,384]{1,0:T(8,128)(2,1)S(1)}, bf16[176,384]{1,0:T(8,128)(2,1)S(1)}, u32[]{:S(2)}, u32[]{:S(2)}) collective-permute-start(bf16[176,384]{1,0:T(8,128)(2,1)S(1)} %add_convert_fusion.7), channel_id=1, source_target_pairs={{0,16},{4,20},{8,24},{12,28},{16,0},{20,4},{24,8},{28,12},{1,17},{... | collective-permute-start | bytes 405512 | tf_op jit(solution)/shard_map/ppermute | solution.py:778
  200.2 6.8 %collective-permute-start.22 = (bf16[176,384]{1,0:T(8,128)(2,1)S(1)}, bf16[176,384]{1,0:T(8,128)(2,1)S(1)}, u32[]{:S(2)}, u32[]{:S(2)}) collective-permute-start(bf16[176,384]{1,0:T(8,128)(2,1)S(1)} %add_convert_fusion.7), channel_id=1, source_target_pairs={{0,8},{4,12},{8,0},{12,4},{16,24},{20,28},{24,16},{28,20},{1,9},{5... | collective-permute-start | bytes 405512 | tf_op jit(solution)/shard_map/ppermute | solution.py:778
  207.1 2.0 collective-permute-start.28
